TPU v7x, 32 devices: a whole 2x2x4 slice. The times are simulated.
32 devices in a mesh: region: 4 (over z), dom: 4 (over y, core), segment: 2 (over x).
Axes of the slice: x: 2, y: 2, z: 4, core: 2. Of those that a mesh axis runs over, the one named last changes fastest.
Arguments:
- stored: float32 [4, 2, 5, 125, 4096], P('segment', None, None, None, ('region', 'dom')), may hold values from -6 to 6
- new_owner: int32 [4096, 1], P(('region', 'dom')), may hold values from 0 to 3; in each aligned block of 256 rows (0 to 255, 256 to 511, ...) at most 96 rows name the same one
- adjoint: float32 [5, 125, 6144], P(None, None, ('region', 'dom')), may hold values from -6 to 6
- deriv: float32 [3, 125, 125], replicated, may hold values from -0.5 to 0.5
- mixing: float32 [3, 5, 5], replicated, may hold values from -2.5 to 2.5
- face_lists: int32 [2, 2048], P(None, ('region', 'dom')), may hold values from 0 to 383
- param_map: int32 [6144], P(('region', 'dom')), may hold values from 0 to 4095
Outputs:
- adjoint_out: float32 [5, 125, 6144], P(None, None, ('region', 'dom'))
- gradient: float32 [4096], replicated
Inputs may be any that keep to these rules, and one draw needn't show every extreme that they name: `new_owner`: within the 256 elements of one old partition no new partition is named more than 96 times, a bound that some block reaches. `face_lists`: slot numbers within a current partition, repeats allowed.
All inputs are finite; a program needn't handle non-finite values.
Results may differ from a plain program's by a relative error of at most 0.0001.
Values sent between devices are 32-bit elements; how exact they have to be, the bound alone decides.
No kernel may reach another device: no remote copies, remote signals or barrier semaphores. Data moves between devices by JAX's collectives and lax.ppermute only.
A program may use at most 64 MiB of HBM per device.

v0:
```python
import functools

import jax
import jax.numpy as jnp
from jax import lax
from jax.experimental import pallas as pl
from jax.experimental.pallas import tpu as pltpu
from jax.sharding import PartitionSpec as P

FACE_NODES = 25
STEPS = 2
PARAMS = 4096
LANES = 128

rk_weights = (1.0 / 6.0, 1.0 / 3.0, 1.0 / 3.0, 1.0 / 6.0)
step_size = 0.5
face_gain = 0.5

F32 = jnp.float32
BF16 = jnp.bfloat16
VMEM = pl.BlockSpec(memory_space=pltpu.VMEM)
SMEM = pl.BlockSpec(memory_space=pltpu.SMEM)
NN = (((1,), (0,)), ((), ()))
NT = (((1,), (1,)), ((), ()))


def call(body, outs, specs, scratch=(), flops=1e8, moved=2e6):
    return pl.pallas_call(
        body,
        out_shape=outs,
        in_specs=specs,
        out_specs=jax.tree.map(lambda _: VMEM, outs),
        scratch_shapes=list(scratch),
        compiler_params=pltpu.CompilerParams(vmem_limit_bytes=40 * 2**20),
        cost_estimate=pl.CostEstimate(
            flops=int(flops), bytes_accessed=int(moved), transcendentals=0
        ),
    )


def shape(*dims, dtype=F32):
    return jax.ShapeDtypeStruct(dims, dtype)


def halves(value):
    top = value.astype(BF16)
    return top, (value - top.astype(F32)).astype(BF16)


def dot(a, b, dims=NN):
    return lax.dot_general(a, b, dims, preferred_element_type=F32)


def pick(value, chosen, dims=NN):
    top, rest = halves(value)
    return dot(top, chosen, dims) + dot(rest, chosen, dims)


def product(left, right):
    top, rest = halves(right)
    return dot(left[0], top) + (dot(left[0], rest) + dot(left[1], top))


def chosen_slots(listed, slots):
    rows = lax.broadcasted_iota(jnp.int32, (slots, listed.shape[1]), 0)
    return (rows == listed).astype(F32).astype(BF16)


def traces_kernel(a_ref, lists_ref, low_ref, high_ref, face_ref):
    fields, nodes, slots = a_ref.shape
    face_ref[...] = jnp.zeros_like(face_ref)
    for f in range(fields):
        face_ref[0, pl.ds(f * FACE_NODES, FACE_NODES), :] = a_ref[f, 0:FACE_NODES, :]
        face_ref[1, pl.ds(f * FACE_NODES, FACE_NODES), :] = a_ref[f, nodes - FACE_NODES : nodes, :]
    low_ref[...] = pick(face_ref[0], chosen_slots(lists_ref[0:1, :], slots))
    high_ref[...] = pick(face_ref[1], chosen_slots(lists_ref[1:2, :], slots))


def operator_kernel(deriv_ref, mixing_ref, top_ref, rest_ref, sum_ref, pad_ref):
    directions, nodes, _ = deriv_ref.shape
    fields = top_ref.shape[0] // LANES
    pad_ref[...] = jnp.zeros_like(pad_ref)
    turned = []
    for d in range(directions):
        pad_ref[0:nodes, 0:nodes] = deriv_ref[d]
        turned.append(pad_ref[...].T)
    sum_ref[...] = functools.reduce(lambda a, b: a + b, turned)
    for f in range(fields):
        for g in range(fields):
            block = mixing_ref[g * fields + f] * turned[0]
            for d in range(1, directions):
                block = block + mixing_ref[(d * fields + g) * fields + f] * turned[d]
            top, rest = halves(block)
            top_ref[f * LANES : (f + 1) * LANES, g * LANES : (g + 1) * LANES] = top
            rest_ref[f * LANES : (f + 1) * LANES, g * LANES : (g + 1) * LANES] = rest


def outgoing_kernel(
    cap, major, minor, place_ref, a_ref, map_ref, lists_ref, low_ref, high_ref, near_low_ref,
    near_high_ref, *refs
):
    outs, (x_ref, f_ref, all_ref, turned_ref) = refs[:major], refs[major:]
    fields, nodes, slots = a_ref.shape
    wide = fields * LANES
    gain = step_size * face_gain
    all_ref[...] = jnp.zeros_like(all_ref)
    for f in range(fields):
        all_ref[pl.ds(f * LANES, nodes), :] = a_ref[f]
    all_ref[nodes : nodes + 1, :] = map_ref[...].astype(F32)
    x_ref[...] = all_ref[0:wide, :]
    low = pick(gain * (near_low_ref[...] - low_ref[...]), chosen_slots(lists_ref[0:1, :], slots), NT)
    high = pick(gain * (near_high_ref[...] - high_ref[...]), chosen_slots(lists_ref[1:2, :], slots), NT)
    all_ref[wide : wide + LANES, :] = low
    all_ref[wide + LANES : wide + 2 * LANES, :] = high
    f_ref[0:LANES, :] = low
    f_ref[LANES : 2 * LANES, :] = high
    turned_ref[...] = all_ref[...].T
    for j in range(major):
        s = lax.rem(place_ref[0] - j + major, major) * minor + place_ref[2]
        outs[j][...] = turned_ref[pl.ds(pl.multiple_of(s * cap, 8), cap), :]


def linear_kernel(nodes, x_ref, f_ref, top_ref, rest_ref, base_ref, face_ref, now_ref):
    wide = x_ref.shape[0]
    fields = wide // LANES
    op = (top_ref[...], rest_ref[...])
    x = x_ref[...]
    now_ref[...] = x + step_size * product(op, x)
    add_faces(now_ref, f_ref, fields, nodes)
    take_faces(now_ref, face_ref, fields, nodes)
    now = now_ref[...]
    base_ref[...] = now + step_size * product(op, now)


def add_faces(to_ref, face_ref, fields, nodes):
    for f in range(fields):
        at = f * LANES
        rows = f * FACE_NODES
        to_ref[pl.ds(at, FACE_NODES), :] += face_ref[pl.ds(rows, FACE_NODES), :]
        to_ref[pl.ds(at + nodes - FACE_NODES, FACE_NODES), :] += face_ref[
            pl.ds(LANES + rows, FACE_NODES), :
        ]


def take_faces(from_ref, face_ref, fields, nodes):
    face_ref[...] = jnp.zeros_like(face_ref)
    for f in range(fields):
        at = f * LANES
        rows = f * FACE_NODES
        face_ref[pl.ds(rows, FACE_NODES), :] = from_ref[pl.ds(at, FACE_NODES), :]
        face_ref[pl.ds(LANES + rows, FACE_NODES), :] = from_ref[
            pl.ds(at + nodes - FACE_NODES, FACE_NODES), :
        ]


def read_state(ref, segment, step, fields, nodes, f):
    parts = []
    halves_ = ref.shape[0] // (ref_segments(ref, fields, nodes) * fields * nodes * STEPS)
    stride = halves_ * STEPS
    for c in range(halves_):
        start = (segment * fields + f) * nodes * stride + c * STEPS + step
        parts.append(ref[pl.ds(start, nodes, stride=stride), :])
    return jnp.concatenate(parts, axis=1)


def ref_segments(ref, fields, nodes):
    return ref.shape[0] // (fields * nodes * STEPS * 2)


def advance(state_refs, weight_ref, step, a_ref, op, across_nodes, fields, nodes, q_ref, u_ref, sums_ref):
    elems = a_ref.shape[1]
    local = ref_segments(state_refs[0], fields, nodes)
    a = a_ref[...]
    linear = product(op, a)
    mean_state = None
    sums_ref[...] = jnp.zeros_like(sums_ref)
    density = jnp.zeros((1, elems), F32)
    u_ref[...] = jnp.zeros_like(u_ref)
    q_ref[...] = jnp.zeros_like(q_ref)
    for k, ref in enumerate(state_refs):
        for i in range(local):
            weight = weight_ref[k * local + i]
            for f in range(fields):
                u = read_state(ref, i, step, fields, nodes, f)
                u_ref[0:nodes, f * elems : (f + 1) * elems] = u
                q_ref[0:nodes, f * elems : (f + 1) * elems] = jnp.tanh(u)
            y = product(across_nodes, u_ref[...])
            p = jnp.zeros((LANES, elems), F32)
            r = jnp.zeros((LANES, elems), F32)
            line = jnp.zeros((LANES, elems), F32)
            for f in range(fields):
                q = q_ref[:, f * elems : (f + 1) * elems]
                p = p + q * a[f * LANES : (f + 1) * LANES, :]
                r = r + q * y[:, f * elems : (f + 1) * elems]
                line = line + u_ref[:, f * elems : (f + 1) * elems] * linear[f * LANES : (f + 1) * LANES, :]
            density = density + weight * jnp.sum(p * r + line, axis=0, keepdims=True)
            p = weight * p
            for f in range(fields):
                sums_ref[:, f * elems : (f + 1) * elems] += q_ref[:, f * elems : (f + 1) * elems] * p
    return linear, density


def slots_of(owner_ref, place_ref, cap, major, minor):
    elems = owner_ref.shape[1]
    owner = owner_ref[...]
    doms = -(-major * minor // 8) * 8
    rows = lax.broadcasted_iota(jnp.int32, (doms, elems), 0)
    named = (rows == owner).astype(F32)
    before = lax.broadcasted_iota(jnp.int32, (elems, elems), 0)
    after = lax.broadcasted_iota(jnp.int32, (elems, elems), 1)
    earlier = dot(named.astype(BF16), (before < after).astype(F32).astype(BF16))
    rank = jnp.sum(named * earlier, axis=0, keepdims=True).astype(jnp.int32)
    high = jnp.zeros_like(owner)
    for k in range(1, major):
        high = high + (owner >= k * minor).astype(jnp.int32)
    low = owner - high * minor
    high = high - place_ref[0]
    low = low - place_ref[2]
    high = jnp.where(high < 0, high + major, high)
    low = jnp.where(low < 0, low + minor, low)
    slot = (high * minor + low) * cap + rank
    return jnp.where(place_ref[3] > 0, slot, -1)


def product_all(total, sums_ref, linear, fields, elems):
    spread = product(total, sums_ref[...])
    return [
        linear[f * LANES : (f + 1) * LANES, :] + spread[:, f * elems : (f + 1) * elems]
        for f in range(fields)
    ]


def first_kernel(cap, major, minor, nodes, place_ref, weight_ref, owner_ref, top_ref, rest_ref, sum_ref, *refs):
    states = refs[:minor]
    blocks = refs[minor : minor + major * minor]
    refs = refs[minor + major * minor :]
    face_outs = refs[:major]
    now_ref, more_ref, got_ref, a_ref, fx_ref, q_ref, u_ref, sums_ref = refs[major:]
    elems = owner_ref.shape[1]
    slots = cap * major * minor
    wide = now_ref.shape[0]
    fields = wide // LANES
    slot = slots_of(owner_ref, place_ref, cap, major, minor)
    rows = lax.broadcasted_iota(jnp.int32, (slots, elems), 0)
    chosen = (rows == slot).astype(F32).astype(BF16)
    for n, block in enumerate(blocks):
        got_ref[n * cap : (n + 1) * cap, :] = block[...]
    here = pick(got_ref[...].T, chosen)
    a_ref[...] = here[0:wide]
    fx_ref[...] = here[wide:]
    param = here[nodes : nodes + 1, :]
    op = (top_ref[...], rest_ref[...])
    total = halves(sum_ref[...])
    across_nodes = halves(sum_ref[...].T)
    linear, density = advance(
        states, weight_ref, 0, a_ref, op, across_nodes, fields, nodes, q_ref, u_ref, sums_ref
    )
    volume = product_all(total, sums_ref, linear, fields, elems)
    for f in range(fields):
        now_ref[f * LANES : (f + 1) * LANES, :] = (
            a_ref[f * LANES : (f + 1) * LANES, :] + step_size * volume[f]
        )
    add_faces(now_ref, fx_ref, fields, nodes)
    take_faces(now_ref, fx_ref, fields, nodes)
    fx_ref[LANES - 3 : LANES - 2, :] = jnp.ones((1, elems), F32)
    sent = pick_back(chosen, fx_ref[...])
    width = cap * minor
    for k in range(major):
        face_outs[k][...] = sent[k * width : (k + 1) * width, :]
    more_ref[...] = jnp.concatenate(
        [density, param, slot.astype(F32), jnp.zeros((5, elems), F32)], axis=0
    )


def pick_back(chosen, value):
    top, rest = halves(value)
    return dot(chosen, top, NT) + dot(chosen, rest, NT)


def second_kernel(cap, major, minor, nodes, weight_ref, now_ref, more_ref, top_ref, rest_ref, sum_ref, *refs):
    states = refs[:minor]
    refs = refs[minor:]
    outs = refs[:major]
    grad_ref, t_ref, q_ref, u_ref, sums_ref = refs[major:]
    wide, elems = now_ref.shape
    fields = wide // LANES
    slots = cap * major * minor
    op = (top_ref[...], rest_ref[...])
    total = halves(sum_ref[...])
    across_nodes = halves(sum_ref[...].T)
    linear, density = advance(
        states, weight_ref, 1, now_ref, op, across_nodes, fields, nodes, q_ref, u_ref, sums_ref
    )
    volume = product_all(total, sums_ref, linear, fields, elems)
    for f in range(fields):
        t_ref[f * LANES : (f + 1) * LANES, :] = (
            now_ref[f * LANES : (f + 1) * LANES, :] + step_size * volume[f]
        )
    t_ref[nodes : nodes + 1, :] = jnp.ones((1, elems), F32)
    slot = more_ref[2:3, :].astype(jnp.int32)
    rows = lax.broadcasted_iota(jnp.int32, (slots, elems), 0)
    sent = pick_back((rows == slot).astype(F32).astype(BF16), t_ref[...])
    width = cap * minor
    for k in range(major):
        outs[k][...] = sent[k * width : (k + 1) * width, :]
    density = (more_ref[0:1, :] + density) * (1.0 / (fields * nodes))
    density = jnp.where(slot >= 0, density, 0.0)
    param = more_ref[1:2, :].astype(jnp.int32)
    count = PARAMS // LANES
    high = lax.shift_right_logical(param, 7)
    low = param - high * LANES
    in_high = lax.broadcasted_iota(jnp.int32, (count, elems), 0) == high
    in_low = (lax.broadcasted_iota(jnp.int32, (LANES, elems), 0) == low).astype(F32).astype(BF16)
    grad_ref[...] = pick(jnp.where(in_high, density, 0.0), in_low, NT)


def gathered(blocks, place_ref, got_ref, cap, major, minor):
    for j in range(major):
        for k in range(minor):
            s = lax.rem(place_ref[0] - j + major, major) * minor
            s = s + lax.rem(place_ref[1] - k + minor, minor)
            got_ref[pl.ds(pl.multiple_of(s * cap, 8), cap), :] = blocks[j * minor + k][...]


def faces_kernel(cap, major, minor, place_ref, base_ref, lists_ref, *refs):
    count = major * minor
    blocks = refs[:count]
    low_ref, high_ref, got_ref = refs[count:]
    gathered(blocks, place_ref, got_ref, cap, major, minor)
    slots = got_ref.shape[0]
    turned = got_ref[...].T
    mine = turned[LANES - 3 : LANES - 2, :] > 0.5
    now = jnp.where(mine, turned, base_ref[...])
    low_ref[...] = pick(now[0:LANES], chosen_slots(lists_ref[0:1, :], slots))
    high_ref[...] = pick(now[LANES:], chosen_slots(lists_ref[1:2, :], slots))


def last_kernel(
    cap, major, minor, place_ref, base_ref, lists_ref, low_ref, high_ref, near_low_ref, near_high_ref, *refs
):
    count = major * minor
    blocks = refs[:count]
    out_ref, got_ref, sum_ref, face_ref = refs[count:]
    fields, nodes, slots = out_ref.shape
    gain = step_size * face_gain
    gathered(blocks, place_ref, got_ref, cap, major, minor)
    turned = got_ref[...].T
    mine = turned[nodes : nodes + 1, :] > 0.5
    sum_ref[...] = jnp.where(mine, turned, base_ref[...])
    face_ref[0:LANES, :] = pick(
        gain * (near_low_ref[...] - low_ref[...]), chosen_slots(lists_ref[0:1, :], slots), NT
    )
    face_ref[LANES : 2 * LANES, :] = pick(
        gain * (near_high_ref[...] - high_ref[...]), chosen_slots(lists_ref[1:2, :], slots), NT
    )
    add_faces(sum_ref, face_ref, fields, nodes)
    for f in range(fields):
        out_ref[f] = sum_ref[pl.ds(f * LANES, nodes), :]


def across(low, high):
    size = lax.axis_size("region")
    up = [(i, i + 1) for i in range(size - 1)]
    near_low = lax.ppermute(high, "region", up)
    near_high = lax.ppermute(low, "region", [(j, i) for i, j in up])
    return near_low, near_high


def spread(parts, cap, major, minor):
    def at(sy, c, x):
        return (sy * minor + c) * minor + x

    axes = ("dom", "segment")
    moved = [parts[0]]
    for k in range(1, major):
        pairs = [(at(y, x, x), at((y + k) % major, x, x)) for y in range(major) for x in range(minor)]
        moved.append(lax.ppermute(parts[k], axes, pairs))
    blocks = []
    for part in moved:
        whole = part
        for k in range(1, minor):
            pairs = [(at(y, x, x), at(y, x, (x + k) % minor)) for y in range(major) for x in range(minor)]
            whole = whole + lax.ppermute(part, axes, pairs)
        blocks.append(whole[0:cap])
        for k in range(1, minor):
            pairs = [
                (at(y, c, x), at(y, (c + k) % minor, x))
                for y in range(major)
                for c in range(minor)
                for x in range(minor)
            ]
            blocks.append(lax.ppermute(whole[k * cap : (k + 1) * cap], axes, pairs))
    return blocks


def total_over(value, axis):
    size = lax.axis_size(axis)
    if size & (size - 1):
        return lax.psum(value, axis)
    k = 1
    while k < size:
        value = value + lax.ppermute(value, axis, [(i, i ^ k) for i in range(size)])
        k = 2 * k
    return value


def per_device(stored, new_owner, adjoint, deriv, mixing, face_lists, param_map):
    minor = lax.axis_size("segment")
    dom_count = lax.axis_size("dom")
    major = dom_count // minor
    local, _, fields, nodes, elems = stored.shape
    slots = adjoint.shape[2]
    faces = face_lists.shape[1]
    cap = slots // dom_count
    wide = fields * LANES
    axes = ("dom", "segment")

    def at(sy, c, x):
        return (sy * minor + c) * minor + x

    dom = lax.axis_index("dom")
    seg = lax.axis_index("segment")
    ty, tc = dom // minor, dom % minor
    place = jnp.stack([ty, tc, seg, (tc == seg).astype(jnp.int32)]).astype(jnp.int32)
    order = (seg + jnp.arange(minor, dtype=jnp.int32)) % minor
    table = jnp.array(rk_weights, F32).reshape(minor, local)
    weights = table[order].reshape(minor * local)
    owner = new_owner.reshape(1, elems)
    mapped = param_map.reshape(1, slots)

    rows = stored.reshape(local, STEPS, fields, nodes, elems // LANES, LANES)
    rows = rows.transpose(0, 2, 3, 4, 1, 5).reshape(-1, LANES)
    states = [rows]
    for k in range(1, minor):
        pairs = [
            (at(y, x, (x + k) % minor), at(y, x, x)) for y in range(major) for x in range(minor)
        ]
        states.append(lax.ppermute(rows, axes, pairs))

    trace = shape(LANES, faces)
    low, high = call(
        traces_kernel, (trace, trace), [VMEM, VMEM], [pltpu.VMEM((2, LANES, slots), F32)]
    )(adjoint, face_lists)
    near_low, near_high = across(low, high)
    top, rest, total = call(
        operator_kernel,
        (shape(wide, wide, dtype=BF16), shape(wide, wide, dtype=BF16), shape(LANES, LANES)),
        [VMEM, SMEM],
        [pltpu.VMEM((LANES, LANES), F32)],
    )(deriv, mixing.reshape(-1))

    sent = wide + 2 * LANES
    *outgoing, x, f0 = call(
        functools.partial(outgoing_kernel, cap, major, minor),
        (shape(cap, sent),) * major + (shape(wide, slots), shape(2 * LANES, slots)),
        [SMEM] + [VMEM] * 7,
        [pltpu.VMEM((sent, slots), F32), pltpu.VMEM((slots, sent), F32)],
    )(place, adjoint, mapped, face_lists, low, high, near_low, near_high)

    blocks = []
    for j in range(major):
        group = [outgoing[j]]
        for k in range(1, minor):
            pairs = [(at(y, (x + k) % minor, x), at(y, x, x)) for y in range(major) for x in range(minor)]
            group.append(lax.ppermute(outgoing[j], axes, pairs))
        if j:
            pairs = [(at((y + j) % major, x, x), at(y, x, x)) for y in range(major) for x in range(minor)]
            group = [lax.ppermute(g, axes, pairs) for g in group]
        blocks = blocks + group

    base, base_face = call(
        functools.partial(linear_kernel, nodes),
        (shape(wide, slots), shape(2 * LANES, slots)),
        [VMEM] * 4,
        [pltpu.VMEM((wide, slots), F32)],
        flops=2e9,
    )(x, f0, top, rest)

    width = cap * minor
    work = [
        pltpu.VMEM((LANES, fields * elems), F32),
        pltpu.VMEM((LANES, fields * elems), F32),
        pltpu.VMEM((LANES, fields * elems), F32),
    ]
    *face_parts, now, more = call(
        functools.partial(first_kernel, cap, major, minor, nodes),
        (shape(width, 2 * LANES),) * major + (shape(wide, elems), shape(8, elems)),
        [SMEM, SMEM] + [VMEM] * (4 + minor + dom_count),
        [
            pltpu.VMEM((slots, sent), F32),
            pltpu.VMEM((wide, elems), F32),
            pltpu.VMEM((2 * LANES, elems), F32),
        ]
        + work,
        flops=3e9,
    )(place, weights, owner, top, rest, total, *states, *blocks)
    face_blocks = spread(face_parts, cap, major, minor)

    *parts, grad = call(
        functools.partial(second_kernel, cap, major, minor, nodes),
        (shape(width, wide),) * major + (shape(PARAMS // LANES, LANES),),
        [SMEM] + [VMEM] * (5 + minor),
        [pltpu.VMEM((wide, elems), F32)] + work,
        flops=3e9,
    )(weights, now, more, top, rest, total, *states)
    last_blocks = spread(parts, cap, major, minor)

    low1, high1 = call(
        functools.partial(faces_kernel, cap, major, minor),
        (trace, trace),
        [SMEM] + [VMEM] * (2 + dom_count),
        [pltpu.VMEM((slots, 2 * LANES), F32)],
    )(place, base_face, face_lists, *face_blocks)
    near_low1, near_high1 = across(low1, high1)

    for axis in ("region", "dom", "segment"):
        grad = total_over(grad, axis)

    out = call(
        functools.partial(last_kernel, cap, major, minor),
        shape(fields, nodes, slots),
        [SMEM] + [VMEM] * (6 + dom_count),
        [
            pltpu.VMEM((slots, wide), F32),
            pltpu.VMEM((wide, slots), F32),
            pltpu.VMEM((2 * LANES, slots), F32),
        ],
    )(place, base, face_lists, low1, high1, near_low1, near_high1, *last_blocks)
    return (out, grad.reshape(PARAMS))


def solution(mesh):
    return jax.shard_map(
        per_device,
        mesh=mesh,
        in_specs=(
            P("segment", None, None, None, ("region", "dom")),
            P(("region", "dom"), None),
            P(None, None, ("region", "dom")),
            P(),
            P(),
            P(None, ("region", "dom")),
            P(("region", "dom")),
        ),
        out_specs=(P(None, None, ("region", "dom")), P()),
        check_vma=False,
    )
```

profile of v0, /device:TPU:0, one launch (start us, length us, event | category | flops | bytes accessed | tf_op | source)
XLA Modules:
  0.0 96.1 jit_solution(18185794375878302507)
XLA Ops:
  0.6 1.3 %collective-permute-start.2 = (f32[5000,128]{1,0:T(8,128)}, f32[5000,128]{1,0:T(8,128)S(1)}, u32[]{:S(2)}, u32[]{:S(2)}) collective-permute-start(f32[5000,128]{1,0:T(8,128)} %bitcast.14), channel_id=1, source_target_pairs={{1,0},{2,3},{5,4},{6,7},{9,8},{10,11},{13,12},{14,15},{17,16},{18,... | collective-permute-start | bytes 7680008 | tf_op jit(solution)/shard_map/ppermute | solution.py:438
  2.0 1.2 %copy-done = f32[5,125,384]{2,1,0:T(8,128)S(1)} copy-done((f32[5,125,384]{2,1,0:T(8,128)S(1)}, f32[5,125,384]{2,1,0:T(8,128)}, u32[]{:S(2)}) %copy-start) | copy-done | bytes 960024
  3.1 0.7 copy-done.2
  3.8 0.3 shard_map.95
  4.1 1.3 %collective-permute-start.1 = (f32[128,128]{1,0:T(8,128)S(1)}, f32[128,128]{1,0:T(8,128)S(1)}, u32[]{:S(2)}, u32[]{:S(2)}) collective-permute-start(f32[128,128]{1,0:T(8,128)S(1)} %get-tuple-element.22.low_ref), channel_id=1, source_target_pairs={{8,0},{16,8},{24,16},{9,1},{17,9},{25,17},{10,2},{18,10},{26,18},{... | collective-permute-start | bytes 196616 | tf_op jit(solution)/shard_map/ppermute | solution.py:365
  5.4 5.6 %collective-permute-start = (f32[128,128]{1,0:T(8,128)S(1)}, f32[128,128]{1,0:T(8,128)S(1)}, u32[]{:S(2)}, u32[]{:S(2)}) collective-permute-start(f32[128,128]{1,0:T(8,128)S(1)} %get-tuple-element.23.high_ref), channel_id=1, source_target_pairs={{0,8},{8,16},{16,24},{1,9},{9,17},{17,25},{2,10},{10,18},{18,26},{... | collective-permute-start | bytes 196616 | tf_op jit(solution)/shard_map/ppermute | solution.py:364
  11.0 0.7 reshape.77.map_ref
  11.8 1.1 %collective-permute-done.near_low_ref = f32[128,128]{1,0:T(8,128)S(1)} collective-permute-done((f32[128,128]{1,0:T(8,128)S(1)}, f32[128,128]{1,0:T(8,128)S(1)}, u32[]{:S(2)}, u32[]{:S(2)}) %collective-permute-start) | collective-permute-done | bytes 65568 | tf_op jit(solution)/shard_map/ppermute | solution.py:364
  12.9 1.2 %copy-done.1 = f32[5,125,384]{2,1,0:T(8,128)S(1)} copy-done((f32[5,125,384]{2,1,0:T(8,128)S(1)}, f32[5,125,384]{2,1,0:T(8,128)}, u32[]{:S(2)}) %copy-start.1) | copy-done | bytes 960024
  14.1 0.7 copy-done.3
  14.8 1.9 %shard_map.96 = (f32[96,896]{1,0:T(8,128)}, f32[96,896]{1,0:T(8,128)}, f32[640,384]{1,0:T(8,128)S(1)}, f32[256,384]{1,0:T(8,128)S(1)}) custom-call(s32[4]{0:T(128)S(1)} %pad_add_fusion.place_ref, f32[5,125,384]{2,1,0:T(8,128)S(1)} %copy-done.1, s32[1,384]{1,0:T(1,128)S(1)} %reshape.77.map_ref, s32[2,128]{1,0:T(2,128)S(1)} %copy-done.3, ...), custom_call_target="tpu_custom_call" | custom-call | flops 100000000 | bytes 2000000 | tf_op jit(solution)/shard_map/pallas_call | solution.py:453
  16.7 0.9 copy-done.7
  17.6 1.3 %collective-permute-start.5 = (f32[96,896]{1,0:T(8,128)}, f32[96,896]{1,0:T(8,128)}, u32[]{:S(2)}, u32[]{:S(2)}) collective-permute-start(f32[96,896]{1,0:T(8,128)} %get-tuple-element.32), channel_id=1, source_target_pairs={{2,0},{1,3},{6,4},{5,7},{10,8},{9,11},{14,12},{13,15},{18,16},{17,... | collective-permute-start | bytes 1032200 | tf_op jit(solution)/shard_map/ppermute | solution.py:465
  18.9 3.9 %collective-permute-start.4 = (f32[96,896]{1,0:T(8,128)}, f32[96,896]{1,0:T(8,128)}, u32[]{:S(2)}, u32[]{:S(2)}) collective-permute-start(f32[96,896]{1,0:T(8,128)} %get-tuple-element.32), channel_id=1, source_target_pairs={{4,0},{7,3},{0,4},{3,7},{12,8},{15,11},{8,12},{11,15},{20,16},{23,... | collective-permute-start | bytes 1032200 | tf_op jit(solution)/shard_map/ppermute | solution.py:468
  22.8 1.3 %collective-permute-start.3 = (f32[96,896]{1,0:T(8,128)}, f32[96,896]{1,0:T(8,128)}, u32[]{:S(2)}, u32[]{:S(2)}) collective-permute-start(f32[96,896]{1,0:T(8,128)} %get-tuple-element.31.refs_2_), channel_id=1, source_target_pairs={{2,0},{1,3},{6,4},{5,7},{10,8},{9,11},{14,12},{13,15},{18,16},{17,... | collective-permute-start | bytes 1032200 | tf_op jit(solution)/shard_map/ppermute | solution.py:465
  24.2 1.9 %collective-permute-start.6 = (f32[96,896]{1,0:T(8,128)}, f32[96,896]{1,0:T(8,128)}, u32[]{:S(2)}, u32[]{:S(2)}) collective-permute-start(f32[96,896]{1,0:T(8,128)} %collective-permute-done.5), channel_id=1, source_target_pairs={{4,0},{7,3},{0,4},{3,7},{12,8},{15,11},{8,12},{11,15},{20,16},{23,... | collective-permute-start | bytes 1032200 | tf_op jit(solution)/shard_map/ppermute | solution.py:468
  26.1 1.2 %gather_fusion = f32[2,2]{1,0:T(2,128)S(1)} fusion(f32[2,2]{1,0:T(2,128)} %constant.45, s32[1024]{0:T(1024)S(1)} %pad_clamp_fusion), kind=kCustom, calls=%fused_computation | custom fusion | bytes 40 | tf_op jit(solution)/shard_map/gather | solution.py:427
  27.4 0.7 copy.12
  28.3 0.9 copy-done.9
  29.2 1.2 %shard_map.97 = (bf16[640,640]{1,0:T(8,128)(2,1)S(1)}, bf16[640,640]{1,0:T(8,128)(2,1)S(1)}, f32[128,128]{1,0:T(8,128)S(1)}) custom-call(f32[3,125,125]{2,1,0:T(8,128)S(1)} %copy-done.9, f32[75]{0:T(128)S(1)} %reshape.78.mixing_ref), custom_call_target="tpu_custom_call" | custom-call | flops 100000000 | bytes 2000000 | tf_op jit(solution)/shard_map/pallas_call | solution.py:445
  30.4 3.2 %collective-permute-done.6.refs_5_ = f32[96,896]{1,0:T(8,128)} collective-permute-done((f32[96,896]{1,0:T(8,128)}, f32[96,896]{1,0:T(8,128)}, u32[]{:S(2)}, u32[]{:S(2)}) %collective-permute-start.6) | collective-permute-done | bytes 344096 | tf_op jit(solution)/shard_map/ppermute | solution.py:468
  33.6 0.4 collective-permute-done.2.refs_1_
  34.0 1.7 %copy-done.5 = f32[2,2,5,125,256]{4,1,3,2,0:T(2,128)S(1)} copy-done((f32[2,2,5,125,256]{4,1,3,2,0:T(2,128)S(1)}, f32[2,2,5,125,256]{4,1,3,2,0:T(2,128)}, u32[]{:S(2)}) %copy-start.5) | copy-done | bytes 2560024
  35.8 6.4 %shard_map.99 = (f32[192,256]{1,0:T(8,128)S(1)}, f32[192,256]{1,0:T(8,128)S(1)}, f32[640,256]{1,0:T(8,128)S(1)}, f32[8,256]{1,0:T(8,128)S(1)}) custom-call(s32[4]{0:T(128)S(1)} %pad_add_fusion.place_ref, f32[4]{0:T(128)S(1)} %reshape.80.weight_ref, s32[1,256]{1,0:T(1,128)S(1)} %bitcast.17, bf16[640,640]{1,0:T(8,128)(2,1)S(1)} %get-tuple-element.26.top_ref, ...), custom_call_target="tpu_custom_call" | custom-call | flops 3000000000 | bytes 2000000 | tf_op jit(solution)/shard_map/pallas_call | solution.py:485
  42.1 4.3 %shard_map.101 = (f32[192,640]{1,0:T(8,128)S(1)}, f32[192,640]{1,0:T(8,128)S(1)}, f32[32,128]{1,0:T(8,128)S(1)}) custom-call(f32[4]{0:T(128)S(1)} %reshape.80.weight_ref, f32[640,256]{1,0:T(8,128)S(1)} %get-tuple-element.37.now_ref, f32[8,256]{1,0:T(8,128)S(1)} %get-tuple-element.38.more_ref, bf16[640,640]{1,0:T(8,128)(2,1)S(1)} %get-tuple-element.26.top_ref, ...), custom_call_target="tpu_custom_call" | custom-call | flops 3000000000 | bytes 2000000 | tf_op jit(solution)/shard_map/pallas_call | solution.py:499
  46.4 4.6 %collective-permute-start.16 = (f32[192,640]{1,0:T(8,128)S(1)}, f32[192,640]{1,0:T(8,128)S(1)}, u32[]{:S(2)}, u32[]{:S(2)}) collective-permute-start(f32[192,640]{1,0:T(8,128)S(1)} %get-tuple-element.40), channel_id=1, source_target_pairs={{0,4},{3,7},{4,0},{7,3},{8,12},{11,15},{12,8},{15,11},{16,20},{19,... | collective-permute-start | bytes 1474568 | tf_op jit(solution)/shard_map/ppermute | solution.py:377
  51.0 1.9 %collective-permute-start.9 = (f32[192,256]{1,0:T(8,128)S(1)}, f32[192,256]{1,0:T(8,128)S(1)}, u32[]{:S(2)}, u32[]{:S(2)}) collective-permute-start(f32[192,256]{1,0:T(8,128)S(1)} %get-tuple-element.34), channel_id=1, source_target_pairs={{0,4},{3,7},{4,0},{7,3},{8,12},{11,15},{12,8},{15,11},{16,20},{19,... | collective-permute-start | bytes 589832 | tf_op jit(solution)/shard_map/ppermute | solution.py:377
  52.9 1.3 %collective-permute-start.7 = (f32[192,256]{1,0:T(8,128)S(1)}, f32[192,256]{1,0:T(8,128)S(1)}, u32[]{:S(2)}, u32[]{:S(2)}) collective-permute-start(f32[192,256]{1,0:T(8,128)S(1)} %get-tuple-element.33), channel_id=1, source_target_pairs={{0,1},{3,2},{4,5},{7,6},{8,9},{11,10},{12,13},{15,14},{16,17},{19,... | collective-permute-start | bytes 589832 | tf_op jit(solution)/shard_map/ppermute | solution.py:383
  54.3 2.1 %collective-permute-start.19 = (f32[32,128]{1,0:T(8,128)S(1)}, f32[32,128]{1,0:T(8,128)S(1)}, u32[]{:S(2)}, u32[]{:S(2)}) collective-permute-start(f32[32,128]{1,0:T(8,128)S(1)} %get-tuple-element.41), channel_id=1, source_target_pairs={{0,8},{8,0},{16,24},{24,16},{1,9},{9,1},{17,25},{25,17},{2,10},{10... | collective-permute-start | bytes 49160 | tf_op jit(solution)/shard_map/ppermute | solution.py:402
  56.4 1.7 %collective-permute-done.19 = f32[32,128]{1,0:T(8,128)S(1)} collective-permute-done((f32[32,128]{1,0:T(8,128)S(1)}, f32[32,128]{1,0:T(8,128)S(1)}, u32[]{:S(2)}, u32[]{:S(2)}) %collective-permute-start.19) | collective-permute-done | bytes 16416 | tf_op jit(solution)/shard_map/ppermute | solution.py:402
  58.1 3.0 %collective-permute-start.20 = (f32[32,128]{1,0:T(8,128)S(1)}, f32[32,128]{1,0:T(8,128)S(1)}, u32[]{:S(2)}, u32[]{:S(2)}) collective-permute-start(f32[32,128]{1,0:T(8,128)S(1)} %add.77), channel_id=1, source_target_pairs={{0,16},{8,24},{16,0},{24,8},{1,17},{9,25},{17,1},{25,9},{2,18},{10... | collective-permute-start | bytes 49160 | tf_op jit(solution)/shard_map/ppermute | solution.py:402
  61.1 1.7 %collective-permute-done.20 = f32[32,128]{1,0:T(8,128)S(1)} collective-permute-done((f32[32,128]{1,0:T(8,128)S(1)}, f32[32,128]{1,0:T(8,128)S(1)}, u32[]{:S(2)}, u32[]{:S(2)}) %collective-permute-start.20) | collective-permute-done | bytes 16416 | tf_op jit(solution)/shard_map/ppermute | solution.py:402
  62.9 1.3 %collective-permute-start.14 = (f32[192,640]{1,0:T(8,128)S(1)}, f32[192,640]{1,0:T(8,128)S(1)}, u32[]{:S(2)}, u32[]{:S(2)}) collective-permute-start(f32[192,640]{1,0:T(8,128)S(1)} %get-tuple-element.39), channel_id=1, source_target_pairs={{0,1},{3,2},{4,5},{7,6},{8,9},{11,10},{12,13},{15,14},{16,17},{19,... | collective-permute-start | bytes 1474568 | tf_op jit(solution)/shard_map/ppermute | solution.py:383
  64.2 1.9 %collective-permute-start.22 = (f32[32,128]{1,0:T(8,128)S(1)}, f32[32,128]{1,0:T(8,128)S(1)}, u32[]{:S(2)}, u32[]{:S(2)}) collective-permute-start(f32[32,128]{1,0:T(8,128)S(1)} %add.79), channel_id=1, source_target_pairs={{0,4},{2,6},{4,0},{6,2},{1,5},{3,7},{5,1},{7,3},{8,12},{10,14},{12... | collective-permute-start | bytes 49160 | tf_op jit(solution)/shard_map/ppermute | solution.py:402
  66.1 1.9 %collective-permute-done.22 = f32[32,128]{1,0:T(8,128)S(1)} collective-permute-done((f32[32,128]{1,0:T(8,128)S(1)}, f32[32,128]{1,0:T(8,128)S(1)}, u32[]{:S(2)}, u32[]{:S(2)}) %collective-permute-start.22) | collective-permute-done | bytes 16416 | tf_op jit(solution)/shard_map/ppermute | solution.py:402
  68.1 3.9 %collective-permute-start.10 = (f32[192,256]{1,0:T(8,128)S(1)}, f32[192,256]{1,0:T(8,128)S(1)}, u32[]{:S(2)}, u32[]{:S(2)}) collective-permute-start(f32[192,256]{1,0:T(8,128)S(1)} %collective-permute-done.9), channel_id=1, source_target_pairs={{0,1},{3,2},{4,5},{7,6},{8,9},{11,10},{12,13},{15,14},{16,17},{19,... | collective-permute-start | bytes 589832 | tf_op jit(solution)/shard_map/ppermute | solution.py:383
  72.0 1.5 %collective-permute-start.17 = (f32[192,640]{1,0:T(8,128)S(1)}, f32[192,640]{1,0:T(8,128)S(1)}, u32[]{:S(2)}, u32[]{:S(2)}) collective-permute-start(f32[192,640]{1,0:T(8,128)S(1)} %collective-permute-done.16), channel_id=1, source_target_pairs={{0,1},{3,2},{4,5},{7,6},{8,9},{11,10},{12,13},{15,14},{16,17},{19,... | collective-permute-start | bytes 1474568 | tf_op jit(solution)/shard_map/ppermute | solution.py:383
  73.6 1.5 %collective-permute-done.10 = f32[192,256]{1,0:T(8,128)S(1)} collective-permute-done((f32[192,256]{1,0:T(8,128)S(1)}, f32[192,256]{1,0:T(8,128)S(1)}, u32[]{:S(2)}, u32[]{:S(2)}) %collective-permute-start.10) | collective-permute-done | bytes 196640 | tf_op jit(solution)/shard_map/ppermute | solution.py:383
  75.2 1.2 %collective-permute-start.11 = (f32[96,256]{1,0:T(8,128)S(1)}, f32[96,256]{1,0:T(8,128)S(1)}, u32[]{:S(2)}, u32[]{:S(2)}) collective-permute-start(f32[96,256]{1,0:T(8,128)S(1)} %get-tuple-element.46), channel_id=1, source_target_pairs={{0,2},{1,3},{2,0},{3,1},{4,6},{5,7},{6,4},{7,5},{8,10},{9,11},{10,... | collective-permute-start | bytes 294920 | tf_op jit(solution)/shard_map/ppermute | solution.py:392
  76.6 3.8 %collective-permute-done.17 = f32[192,640]{1,0:T(8,128)S(1)} collective-permute-done((f32[192,640]{1,0:T(8,128)S(1)}, f32[192,640]{1,0:T(8,128)S(1)}, u32[]{:S(2)}, u32[]{:S(2)}) %collective-permute-start.17) | collective-permute-done | bytes 491552 | tf_op jit(solution)/shard_map/ppermute | solution.py:383
  80.5 1.2 %collective-permute-start.18 = (f32[96,640]{1,0:T(8,128)S(1)}, f32[96,640]{1,0:T(8,128)S(1)}, u32[]{:S(2)}, u32[]{:S(2)}) collective-permute-start(f32[96,640]{1,0:T(8,128)S(1)} %get-tuple-element.42), channel_id=1, source_target_pairs={{0,2},{1,3},{2,0},{3,1},{4,6},{5,7},{6,4},{7,5},{8,10},{9,11},{10,... | collective-permute-start | bytes 737288 | tf_op jit(solution)/shard_map/ppermute | solution.py:392
  81.7 3.6 %shard_map.98 = (f32[640,384]{1,0:T(8,128)S(1)}, f32[256,384]{1,0:T(8,128)S(1)}) custom-call(f32[640,384]{1,0:T(8,128)S(1)} %copy-done.8, f32[256,384]{1,0:T(8,128)S(1)} %get-tuple-element.25.f_ref, bf16[640,640]{1,0:T(8,128)(2,1)S(1)} %get-tuple-element.26.top_ref, bf16[640,640]{1,0:T(8,128)(2,1)S(1)} %get-tuple-element.27.rest_ref), custom_call_target="tpu_custom_call" | custom-call | flops 2000000000 | bytes 2000000 | tf_op jit(solution)/shard_map/pallas_call | solution.py:471
  85.3 1.0 shard_map.100
  86.3 1.3 %collective-permute-start.13 = (f32[128,128]{1,0:T(8,128)S(1)}, f32[128,128]{1,0:T(8,128)S(1)}, u32[]{:S(2)}, u32[]{:S(2)}) collective-permute-start(f32[128,128]{1,0:T(8,128)S(1)} %get-tuple-element.35.low_ref), channel_id=1, source_target_pairs={{8,0},{16,8},{24,16},{9,1},{17,9},{25,17},{10,2},{18,10},{26,18},{... | collective-permute-start | bytes 196616 | tf_op jit(solution)/shard_map/ppermute | solution.py:365
  87.6 4.5 %collective-permute-start.12 = (f32[128,128]{1,0:T(8,128)S(1)}, f32[128,128]{1,0:T(8,128)S(1)}, u32[]{:S(2)}, u32[]{:S(2)}) collective-permute-start(f32[128,128]{1,0:T(8,128)S(1)} %get-tuple-element.36.high_ref), channel_id=1, source_target_pairs={{0,8},{8,16},{16,24},{1,9},{9,17},{17,25},{2,10},{10,18},{18,26},{... | collective-permute-start | bytes 196616 | tf_op jit(solution)/shard_map/ppermute | solution.py:364
  92.2 0.6 add_bitcast_fusion
  92.8 1.3 %collective-permute-done.12.near_low_ref = f32[128,128]{1,0:T(8,128)S(1)} collective-permute-done((f32[128,128]{1,0:T(8,128)S(1)}, f32[128,128]{1,0:T(8,128)S(1)}, u32[]{:S(2)}, u32[]{:S(2)}) %collective-permute-start.12) | collective-permute-done | bytes 65568 | tf_op jit(solution)/shard_map/ppermute | solution.py:364
  94.1 2.0 %shard_map.102 = f32[5,125,384]{2,1,0:T(8,128)} custom-call(s32[4]{0:T(128)S(1)} %pad_add_fusion.place_ref, f32[640,384]{1,0:T(8,128)S(1)} %get-tuple-element.28.base_ref, s32[2,128]{1,0:T(2,128)S(1)} %copy-done.4, f32[128,128]{1,0:T(8,128)S(1)} %get-tuple-element.35.low_ref, f32[128,128]{1,0:T(8,128)S(1)} %get-tuple-element.36.high_ref, ...), custom_call_target="tpu_custom_call" | custom-call | flops 100000000 | bytes 2000000 | tf_op jit(solution)/shard_map/pallas_call | solution.py:519
  (51 shorter events, 0.8 us)
Async XLA Ops:
  0.6 33.4 %copy-start.10 = (s32[256,1]{0,1:T(1,128)S(1)}, s32[256,1]{0,1:T(1,128)}, u32[]{:S(2)}) copy-start(s32[256,1]{0,1:T(1,128)} %param.9) | copy-start | bytes 3076
  0.6 33.4 %collective-permute-start.2 = (f32[5000,128]{1,0:T(8,128)}, f32[5000,128]{1,0:T(8,128)S(1)}, u32[]{:S(2)}, u32[]{:S(2)}) collective-permute-start(f32[5000,128]{1,0:T(8,128)} %bitcast.14), channel_id=1, source_target_pairs={{1,0},{2,3},{5,4},{6,7},{9,8},{10,11},{13,12},{14,15},{17,16},{18,... | collective-permute-start | bytes 7680008 | tf_op jit(solution)/shard_map/ppermute | solution.py:438
  1.9 1.2 %copy-start = (f32[5,125,384]{2,1,0:T(8,128)S(1)}, f32[5,125,384]{2,1,0:T(8,128)}, u32[]{:S(2)}) copy-start(f32[5,125,384]{2,1,0:T(8,128)} %a_ref.3) | copy-start | bytes 2880004
  3.1 0.7 copy-start.2
  4.1 7.7 %collective-permute-start.1 = (f32[128,128]{1,0:T(8,128)S(1)}, f32[128,128]{1,0:T(8,128)S(1)}, u32[]{:S(2)}, u32[]{:S(2)}) collective-permute-start(f32[128,128]{1,0:T(8,128)S(1)} %get-tuple-element.22.low_ref), channel_id=1, source_target_pairs={{8,0},{16,8},{24,16},{9,1},{17,9},{25,17},{10,2},{18,10},{26,18},{... | collective-permute-start | bytes 196616 | tf_op jit(solution)/shard_map/ppermute | solution.py:365
  5.4 7.5 %collective-permute-start = (f32[128,128]{1,0:T(8,128)S(1)}, f32[128,128]{1,0:T(8,128)S(1)}, u32[]{:S(2)}, u32[]{:S(2)}) collective-permute-start(f32[128,128]{1,0:T(8,128)S(1)} %get-tuple-element.23.high_ref), channel_id=1, source_target_pairs={{0,8},{8,16},{16,24},{1,9},{9,17},{17,25},{2,10},{10,18},{18,26},{... | collective-permute-start | bytes 196616 | tf_op jit(solution)/shard_map/ppermute | solution.py:364
  12.9 1.2 %copy-start.1 = (f32[5,125,384]{2,1,0:T(8,128)S(1)}, f32[5,125,384]{2,1,0:T(8,128)}, u32[]{:S(2)}) copy-start(f32[5,125,384]{2,1,0:T(8,128)} %a_ref.3) | copy-start | bytes 2880004
  14.1 0.7 copy-start.3
  16.7 0.9 copy-start.7
  17.6 6.5 %collective-permute-start.5 = (f32[96,896]{1,0:T(8,128)}, f32[96,896]{1,0:T(8,128)}, u32[]{:S(2)}, u32[]{:S(2)}) collective-permute-start(f32[96,896]{1,0:T(8,128)} %get-tuple-element.32), channel_id=1, source_target_pairs={{2,0},{1,3},{6,4},{5,7},{10,8},{9,11},{14,12},{13,15},{18,16},{17,... | collective-permute-start | bytes 1032200 | tf_op jit(solution)/shard_map/ppermute | solution.py:465
  18.9 11.5 %collective-permute-start.4 = (f32[96,896]{1,0:T(8,128)}, f32[96,896]{1,0:T(8,128)}, u32[]{:S(2)}, u32[]{:S(2)}) collective-permute-start(f32[96,896]{1,0:T(8,128)} %get-tuple-element.32), channel_id=1, source_target_pairs={{4,0},{7,3},{0,4},{3,7},{12,8},{15,11},{8,12},{11,15},{20,16},{23,... | collective-permute-start | bytes 1032200 | tf_op jit(solution)/shard_map/ppermute | solution.py:468
  22.8 7.6 %collective-permute-start.3 = (f32[96,896]{1,0:T(8,128)}, f32[96,896]{1,0:T(8,128)}, u32[]{:S(2)}, u32[]{:S(2)}) collective-permute-start(f32[96,896]{1,0:T(8,128)} %get-tuple-element.31.refs_2_), channel_id=1, source_target_pairs={{2,0},{1,3},{6,4},{5,7},{10,8},{9,11},{14,12},{13,15},{18,16},{17,... | collective-permute-start | bytes 1032200 | tf_op jit(solution)/shard_map/ppermute | solution.py:465
  24.2 9.5 %collective-permute-start.6 = (f32[96,896]{1,0:T(8,128)}, f32[96,896]{1,0:T(8,128)}, u32[]{:S(2)}, u32[]{:S(2)}) collective-permute-start(f32[96,896]{1,0:T(8,128)} %collective-permute-done.5), channel_id=1, source_target_pairs={{4,0},{7,3},{0,4},{3,7},{12,8},{15,11},{8,12},{11,15},{20,16},{23,... | collective-permute-start | bytes 1032200 | tf_op jit(solution)/shard_map/ppermute | solution.py:468
  28.2 0.9 copy-start.9
  34.0 1.7 %copy-start.5 = (f32[2,2,5,125,256]{4,1,3,2,0:T(2,128)S(1)}, f32[2,2,5,125,256]{4,1,3,2,0:T(2,128)}, u32[]{:S(2)}) copy-start(f32[2,2,5,125,256]{4,1,3,2,0:T(2,128)} %param.8) | copy-start | bytes 7680004
  35.8 6.4 %copy-start.6 = (f32[2,2,5,125,256]{4,1,3,2,0:T(2,128)S(1)}, f32[2,2,5,125,256]{4,1,3,2,0:T(2,128)}, u32[]{:S(2)}) copy-start(f32[2,2,5,125,256]{4,1,3,2,0:T(2,128)} %param.8) | copy-start | bytes 7680004
  46.4 25.6 %collective-permute-start.16 = (f32[192,640]{1,0:T(8,128)S(1)}, f32[192,640]{1,0:T(8,128)S(1)}, u32[]{:S(2)}, u32[]{:S(2)}) collective-permute-start(f32[192,640]{1,0:T(8,128)S(1)} %get-tuple-element.40), channel_id=1, source_target_pairs={{0,4},{3,7},{4,0},{7,3},{8,12},{11,15},{12,8},{15,11},{16,20},{19,... | collective-permute-start | bytes 1474568 | tf_op jit(solution)/shard_map/ppermute | solution.py:377
  51.0 17.0 %collective-permute-start.9 = (f32[192,256]{1,0:T(8,128)S(1)}, f32[192,256]{1,0:T(8,128)S(1)}, u32[]{:S(2)}, u32[]{:S(2)}) collective-permute-start(f32[192,256]{1,0:T(8,128)S(1)} %get-tuple-element.34), channel_id=1, source_target_pairs={{0,4},{3,7},{4,0},{7,3},{8,12},{11,15},{12,8},{15,11},{16,20},{19,... | collective-permute-start | bytes 589832 | tf_op jit(solution)/shard_map/ppermute | solution.py:377
  52.9 19.0 %collective-permute-start.7 = (f32[192,256]{1,0:T(8,128)S(1)}, f32[192,256]{1,0:T(8,128)S(1)}, u32[]{:S(2)}, u32[]{:S(2)}) collective-permute-start(f32[192,256]{1,0:T(8,128)S(1)} %get-tuple-element.33), channel_id=1, source_target_pairs={{0,1},{3,2},{4,5},{7,6},{8,9},{11,10},{12,13},{15,14},{16,17},{19,... | collective-permute-start | bytes 589832 | tf_op jit(solution)/shard_map/ppermute | solution.py:383
  54.3 3.8 %collective-permute-start.19 = (f32[32,128]{1,0:T(8,128)S(1)}, f32[32,128]{1,0:T(8,128)S(1)}, u32[]{:S(2)}, u32[]{:S(2)}) collective-permute-start(f32[32,128]{1,0:T(8,128)S(1)} %get-tuple-element.41), channel_id=1, source_target_pairs={{0,8},{8,0},{16,24},{24,16},{1,9},{9,1},{17,25},{25,17},{2,10},{10... | collective-permute-start | bytes 49160 | tf_op jit(solution)/shard_map/ppermute | solution.py:402
  58.1 4.8 %collective-permute-start.20 = (f32[32,128]{1,0:T(8,128)S(1)}, f32[32,128]{1,0:T(8,128)S(1)}, u32[]{:S(2)}, u32[]{:S(2)}) collective-permute-start(f32[32,128]{1,0:T(8,128)S(1)} %add.77), channel_id=1, source_target_pairs={{0,16},{8,24},{16,0},{24,8},{1,17},{9,25},{17,1},{25,9},{2,18},{10... | collective-permute-start | bytes 49160 | tf_op jit(solution)/shard_map/ppermute | solution.py:402
  62.9 1.3 %collective-permute-start.21 = (f32[32,128]{1,0:T(8,128)S(1)}, f32[32,128]{1,0:T(8,128)S(1)}, u32[]{:S(2)}, u32[]{:S(2)}) collective-permute-start(f32[32,128]{1,0:T(8,128)S(1)} %add.78), channel_id=1, source_target_pairs={{0,2},{2,0},{4,6},{6,4},{1,3},{3,1},{5,7},{7,5},{8,10},{10,8},{12,... | collective-permute-start | bytes 49160 | tf_op jit(solution)/shard_map/ppermute | solution.py:402
  62.9 13.5 %collective-permute-start.14 = (f32[192,640]{1,0:T(8,128)S(1)}, f32[192,640]{1,0:T(8,128)S(1)}, u32[]{:S(2)}, u32[]{:S(2)}) collective-permute-start(f32[192,640]{1,0:T(8,128)S(1)} %get-tuple-element.39), channel_id=1, source_target_pairs={{0,1},{3,2},{4,5},{7,6},{8,9},{11,10},{12,13},{15,14},{16,17},{19,... | collective-permute-start | bytes 1474568 | tf_op jit(solution)/shard_map/ppermute | solution.py:383
  64.2 3.8 %collective-permute-start.22 = (f32[32,128]{1,0:T(8,128)S(1)}, f32[32,128]{1,0:T(8,128)S(1)}, u32[]{:S(2)}, u32[]{:S(2)}) collective-permute-start(f32[32,128]{1,0:T(8,128)S(1)} %add.79), channel_id=1, source_target_pairs={{0,4},{2,6},{4,0},{6,2},{1,5},{3,7},{5,1},{7,3},{8,12},{10,14},{12... | collective-permute-start | bytes 49160 | tf_op jit(solution)/shard_map/ppermute | solution.py:402
  68.0 24.1 %collective-permute-start.23 = (f32[32,128]{1,0:T(8,128)S(1)}, f32[32,128]{1,0:T(8,128)S(1)}, u32[]{:S(2)}, u32[]{:S(2)}) collective-permute-start(f32[32,128]{1,0:T(8,128)S(1)} %add.80), channel_id=1, source_target_pairs={{0,1},{1,0},{2,3},{3,2},{4,5},{5,4},{6,7},{7,6},{8,9},{9,8},{10,11... | collective-permute-start | bytes 49160 | tf_op jit(solution)/shard_map/ppermute | solution.py:402
  68.1 7.1 %collective-permute-start.10 = (f32[192,256]{1,0:T(8,128)S(1)}, f32[192,256]{1,0:T(8,128)S(1)}, u32[]{:S(2)}, u32[]{:S(2)}) collective-permute-start(f32[192,256]{1,0:T(8,128)S(1)} %collective-permute-done.9), channel_id=1, source_target_pairs={{0,1},{3,2},{4,5},{7,6},{8,9},{11,10},{12,13},{15,14},{16,17},{19,... | collective-permute-start | bytes 589832 | tf_op jit(solution)/shard_map/ppermute | solution.py:383
  72.0 8.4 %collective-permute-start.17 = (f32[192,640]{1,0:T(8,128)S(1)}, f32[192,640]{1,0:T(8,128)S(1)}, u32[]{:S(2)}, u32[]{:S(2)}) collective-permute-start(f32[192,640]{1,0:T(8,128)S(1)} %collective-permute-done.16), channel_id=1, source_target_pairs={{0,1},{3,2},{4,5},{7,6},{8,9},{11,10},{12,13},{15,14},{16,17},{19,... | collective-permute-start | bytes 1474568 | tf_op jit(solution)/shard_map/ppermute | solution.py:383
  73.6 11.8 %collective-permute-start.8 = (f32[96,256]{1,0:T(8,128)S(1)}, f32[96,256]{1,0:T(8,128)S(1)}, u32[]{:S(2)}, u32[]{:S(2)}) collective-permute-start(f32[96,256]{1,0:T(8,128)S(1)} %get-tuple-element.48), channel_id=1, source_target_pairs={{0,2},{1,3},{2,0},{3,1},{4,6},{5,7},{6,4},{7,5},{8,10},{9,11},{10,... | collective-permute-start | bytes 294920 | tf_op jit(solution)/shard_map/ppermute | solution.py:392
  75.2 6.5 %copy-start.8 = (f32[640,384]{1,0:T(8,128)S(1)}, f32[640,384]{1,0:T(8,128)}, u32[]{:S(2)}) copy-start(f32[640,384]{1,0:T(8,128)} %copy-done.7) | copy-start | bytes 2949124
  75.2 10.1 %collective-permute-start.11 = (f32[96,256]{1,0:T(8,128)S(1)}, f32[96,256]{1,0:T(8,128)S(1)}, u32[]{:S(2)}, u32[]{:S(2)}) collective-permute-start(f32[96,256]{1,0:T(8,128)S(1)} %get-tuple-element.46), channel_id=1, source_target_pairs={{0,2},{1,3},{2,0},{3,1},{4,6},{5,7},{6,4},{7,5},{8,10},{9,11},{10,... | collective-permute-start | bytes 294920 | tf_op jit(solution)/shard_map/ppermute | solution.py:392
  76.5 17.5 %collective-permute-start.15 = (f32[96,640]{1,0:T(8,128)S(1)}, f32[96,640]{1,0:T(8,128)S(1)}, u32[]{:S(2)}, u32[]{:S(2)}) collective-permute-start(f32[96,640]{1,0:T(8,128)S(1)} %get-tuple-element.44), channel_id=1, source_target_pairs={{0,2},{1,3},{2,0},{3,1},{4,6},{5,7},{6,4},{7,5},{8,10},{9,11},{10,... | collective-permute-start | bytes 737288 | tf_op jit(solution)/shard_map/ppermute | solution.py:392
  80.5 13.6 %collective-permute-start.18 = (f32[96,640]{1,0:T(8,128)S(1)}, f32[96,640]{1,0:T(8,128)S(1)}, u32[]{:S(2)}, u32[]{:S(2)}) collective-permute-start(f32[96,640]{1,0:T(8,128)S(1)} %get-tuple-element.42), channel_id=1, source_target_pairs={{0,2},{1,3},{2,0},{3,1},{4,6},{5,7},{6,4},{7,5},{8,10},{9,11},{10,... | collective-permute-start | bytes 737288 | tf_op jit(solution)/shard_map/ppermute | solution.py:392
  81.7 3.6 %copy-start.4 = (s32[2,128]{1,0:T(2,128)S(1)}, s32[2,128]{1,0:T(2,128)}, u32[]{:S(2)}) copy-start(s32[2,128]{1,0:T(2,128)} %lists_ref.7) | copy-start | bytes 3076
  86.3 6.5 %collective-permute-start.13 = (f32[128,128]{1,0:T(8,128)S(1)}, f32[128,128]{1,0:T(8,128)S(1)}, u32[]{:S(2)}, u32[]{:S(2)}) collective-permute-start(f32[128,128]{1,0:T(8,128)S(1)} %get-tuple-element.35.low_ref), channel_id=1, source_target_pairs={{8,0},{16,8},{24,16},{9,1},{17,9},{25,17},{10,2},{18,10},{26,18},{... | collective-permute-start | bytes 196616 | tf_op jit(solution)/shard_map/ppermute | solution.py:365
  87.6 6.4 %collective-permute-start.12 = (f32[128,128]{1,0:T(8,128)S(1)}, f32[128,128]{1,0:T(8,128)S(1)}, u32[]{:S(2)}, u32[]{:S(2)}) collective-permute-start(f32[128,128]{1,0:T(8,128)S(1)} %get-tuple-element.36.high_ref), channel_id=1, source_target_pairs={{0,8},{8,16},{16,24},{1,9},{9,17},{17,25},{2,10},{10,18},{18,26},{... | collective-permute-start | bytes 196616 | tf_op jit(solution)/shard_map/ppermute | solution.py:364
where the time goes:
time: 96.8 us; the launch traced here: 96.1 us
  starting transfers between devices  46.6 us (48%)
  Pallas kernels  20.7 us (21%)
  waiting for transfers between devices  16.6 us (17%)
  local copies, waits for them, and re-layouts  10.3 us (11%)
  between operations  1.05 us (1%)
    ppermute x2, starting transfers between devices, across(): near_low = lax.ppermute(high, 'region', up)  10.1 us
    unnamed x23, local copies, waits for them, and re-layouts  8.07 us
    ppermute x4, starting transfers between devices, spread(): whole = whole + lax.ppermute(part, axes, pairs)  8.04 us
    ppermute x5, starting transfers between devices, total_over(): value = value + lax.ppermute(value, axis, [(i, i ^ k) for i in range(size)])  7.09 us
    ppermute x2, starting transfers between devices, spread(): moved.append(lax.ppermute(parts[k], axes, pairs))  6.5 us
    pallas_call x1, Pallas kernels, per_device(): call(functools.partial(first_kernel, cap, major, minor, nodes), (shape(wi...  6.36 us
    ppermute x2, starting transfers between devices, per_device(): group = [lax.ppermute(g, axes, pairs) for g in group]  5.85 us
    ppermute x5, waiting for transfers between devices, total_over(): value = value + lax.ppermute(value, axis, [(i, i ^ k) for i in range(size)])  5.32 us
  transfers between devices with their start and end apart: 24, of which 9 were waited for; matrix products, arithmetic and copies ran while one was open for 4% of the time, Pallas kernels for 8%

commit v1 on v0

v1 whole, which is shorter than its diff:
```python
import functools

import jax
import jax.numpy as jnp
from jax import lax
from jax.experimental import pallas as pl
from jax.experimental.pallas import tpu as pltpu
from jax.sharding import PartitionSpec as P

FACE_NODES = 25
STEPS = 2
PARAMS = 4096
LANES = 128
RIDE = PARAMS // (4 * LANES)

rk_weights = (1.0 / 6.0, 1.0 / 3.0, 1.0 / 3.0, 1.0 / 6.0)
step_size = 0.5
face_gain = 0.5

F32 = jnp.float32
BF16 = jnp.bfloat16
VMEM = pl.BlockSpec(memory_space=pltpu.VMEM)
SMEM = pl.BlockSpec(memory_space=pltpu.SMEM)
NN = (((1,), (0,)), ((), ()))
NT = (((1,), (1,)), ((), ()))


def call(body, outs, specs, scratch=(), flops=1e6, moved=1e4):
    return pl.pallas_call(
        body,
        out_shape=outs,
        in_specs=specs,
        out_specs=jax.tree.map(lambda _: VMEM, outs),
        scratch_shapes=list(scratch),
        compiler_params=pltpu.CompilerParams(vmem_limit_bytes=40 * 2**20),
        cost_estimate=pl.CostEstimate(
            flops=int(flops), bytes_accessed=int(moved), transcendentals=0
        ),
    )


def shape(*dims, dtype=F32):
    return jax.ShapeDtypeStruct(dims, dtype)


def halves(value):
    top = value.astype(BF16)
    return top, (value - top.astype(F32)).astype(BF16)


def dot(a, b, dims=NN):
    return lax.dot_general(a, b, dims, preferred_element_type=F32)


def pick(value, chosen, dims=NN):
    top, rest = halves(value)
    return dot(top, chosen, dims) + dot(rest, chosen, dims)


def product(left, right):
    top, rest = halves(right)
    return dot(left[0], top) + (dot(left[0], rest) + dot(left[1], top))


def chosen_slots(listed, slots):
    rows = lax.broadcasted_iota(jnp.int32, (slots, listed.shape[1]), 0)
    return (rows == listed).astype(F32).astype(BF16)


def stacked(value):
    top, rest = halves(value)
    return jnp.concatenate(
        [jnp.concatenate([top, top], axis=1), jnp.concatenate([rest, rest], axis=1)], axis=0
    )


def through(double, value):
    top, rest = halves(value)
    both = dot(double, jnp.concatenate([top, rest], axis=0))
    return both[:LANES] + both[LANES:]


def segment_weight(place_ref, minor, local, k, i):
    at = lax.rem(place_ref[2] + k, minor) * local + i
    weight = jnp.float32(rk_weights[0])
    for n in range(1, len(rk_weights)):
        weight = jnp.where(at == n, jnp.float32(rk_weights[n]), weight)
    return weight


def states_kernel(local, fields, nodes, rows_ref, *outs):
    parts = rows_ref.shape[0] // (local * fields * nodes * STEPS)
    stride = parts * STEPS
    for step in range(STEPS):
        for n in range(local * fields):
            for c in range(parts):
                start = n * nodes * stride + c * STEPS + step
                outs[step][n * LANES : n * LANES + nodes, c * LANES : (c + 1) * LANES] = rows_ref[
                    pl.ds(start, nodes, stride=stride), :
                ]
            outs[step][n * LANES + nodes : (n + 1) * LANES, :] = jnp.zeros(
                (LANES - nodes, parts * LANES), F32
            )


def start_kernel(place_ref, a_ref, lists_ref, one_ref, two_ref, face_ref):
    fields, nodes, slots = a_ref.shape
    face_ref[...] = jnp.zeros_like(face_ref)
    for f in range(fields):
        face_ref[0, pl.ds(f * FACE_NODES, FACE_NODES), :] = a_ref[f, 0:FACE_NODES, :]
        face_ref[1, pl.ds(f * FACE_NODES, FACE_NODES), :] = a_ref[f, nodes - FACE_NODES : nodes, :]
    low = pick(face_ref[0], chosen_slots(lists_ref[0:1, :], slots))
    high = pick(face_ref[1], chosen_slots(lists_ref[1:2, :], slots))
    put_traces(place_ref, low, high, one_ref, two_ref)


def put_traces(place_ref, low, high, one_ref, two_ref):
    even = place_ref[4] == 0
    one_ref[0:LANES, :] = jnp.where(even, high, low)
    two_ref[...] = jnp.where(even, low, high)


def face_rows(place_ref, lists_ref, one_ref, two_ref, near_one_ref, near_two_ref, slots, to_ref):
    gain = step_size * face_gain
    even = place_ref[4] == 0
    one = gain * (near_one_ref[0:LANES, :] - one_ref[0:LANES, :])
    two = gain * (near_two_ref[...] - two_ref[...])
    to_ref[0:LANES, :] = pick(
        jnp.where(even, two, one), chosen_slots(lists_ref[0:1, :], slots), NT
    )
    to_ref[LANES : 2 * LANES, :] = pick(
        jnp.where(even, one, two), chosen_slots(lists_ref[1:2, :], slots), NT
    )


def outgoing_kernel(
    cap, major, minor, place_ref, a_ref, map_ref, lists_ref, one_ref, two_ref, near_one_ref, near_two_ref, *refs
):
    outs, (f_ref, all_ref, turned_ref) = refs[:major], refs[major:]
    fields, nodes, slots = a_ref.shape
    wide = fields * LANES
    all_ref[0:wide, :] = jnp.zeros((wide, slots), F32)
    for f in range(fields):
        all_ref[pl.ds(f * LANES, nodes), :] = a_ref[f]
    all_ref[nodes : nodes + 1, :] = map_ref[...].astype(F32)
    face_rows(place_ref, lists_ref, one_ref, two_ref, near_one_ref, near_two_ref, slots, f_ref)
    all_ref[wide:, :] = f_ref[...]
    turned_ref[...] = all_ref[...].T
    for j in range(major):
        s = lax.rem(place_ref[0] - j + major, major) * minor + place_ref[2]
        outs[j][...] = turned_ref[pl.ds(pl.multiple_of(s * cap, 8), cap), :]


def operator_kernel(deriv_ref, mixing_ref, top_ref, rest_ref, sum_ref, pad_ref):
    directions, nodes, _ = deriv_ref.shape
    fields = top_ref.shape[0] // LANES
    pad_ref[...] = jnp.zeros_like(pad_ref)
    turned = []
    for d in range(directions):
        pad_ref[0:nodes, 0:nodes] = deriv_ref[d]
        turned.append(pad_ref[...].T)
    sum_ref[...] = functools.reduce(lambda a, b: a + b, turned)
    for f in range(fields):
        for g in range(fields):
            block = mixing_ref[g * fields + f] * turned[0]
            for d in range(1, directions):
                block = block + mixing_ref[(d * fields + g) * fields + f] * turned[d]
            top, rest = halves(block)
            top_ref[f * LANES : (f + 1) * LANES, g * LANES : (g + 1) * LANES] = top
            rest_ref[f * LANES : (f + 1) * LANES, g * LANES : (g + 1) * LANES] = rest


def linear_kernel(a_in_ref, f_ref, top_ref, rest_ref, base_ref, face_ref, now_ref, x_ref):
    fields, nodes, _ = a_in_ref.shape
    x_ref[...] = jnp.zeros_like(x_ref)
    for f in range(fields):
        x_ref[pl.ds(f * LANES, nodes), :] = a_in_ref[f]
    op = (top_ref[...], rest_ref[...])
    x = x_ref[...]
    now_ref[...] = x + step_size * product(op, x)
    add_faces(now_ref, f_ref, fields, nodes)
    take_faces(now_ref, face_ref, fields, nodes)
    now = now_ref[...]
    base_ref[...] = now + step_size * product(op, now)


def add_faces(to_ref, face_ref, fields, nodes):
    for f in range(fields):
        at = f * LANES
        rows = f * FACE_NODES
        to_ref[pl.ds(at, FACE_NODES), :] += face_ref[pl.ds(rows, FACE_NODES), :]
        to_ref[pl.ds(at + nodes - FACE_NODES, FACE_NODES), :] += face_ref[
            pl.ds(LANES + rows, FACE_NODES), :
        ]


def take_faces(from_ref, face_ref, fields, nodes):
    face_ref[...] = jnp.zeros_like(face_ref)
    for f in range(fields):
        at = f * LANES
        rows = f * FACE_NODES
        face_ref[pl.ds(rows, FACE_NODES), :] = from_ref[pl.ds(at, FACE_NODES), :]
        face_ref[pl.ds(LANES + rows, FACE_NODES), :] = from_ref[
            pl.ds(at + nodes - FACE_NODES, FACE_NODES), :
        ]


def ready_kernel(local, minor, place_ref, sum_ref, *refs):
    states, outs = refs[:STEPS], refs[STEPS:]
    fields = states[0].shape[0] // (local * LANES)
    double = stacked(sum_ref[...].T)
    for step in range(STEPS):
        for i in range(local):
            prepare(states[step], outs[2 * step], outs[2 * step + 1], double, segment_weight(place_ref, minor, local, 0, i), i, fields, i == 0)


def prepare(state_ref, r_ref, mean_ref, double, weight, i, fields, first):
    for f in range(fields):
        at = (i * fields + f) * LANES
        u = state_ref[at : at + LANES, :]
        part = jnp.tanh(u) * through(double, u)
        rows = slice(f * LANES, (f + 1) * LANES)
        if f == 0:
            r_ref[i * LANES : (i + 1) * LANES, :] = part
        else:
            r_ref[i * LANES : (i + 1) * LANES, :] += part
        if first:
            mean_ref[rows, :] = weight * u
        else:
            mean_ref[rows, :] += weight * u


def advance(minor, local, place_ref, states, r_ref, mean_ref, a_ref, op, sum_ref, t_ref, r_more_ref, mean_more_ref, q_ref, sums_ref):
    wide, elems = a_ref.shape
    fields = wide // LANES
    double = stacked(sum_ref[...].T)
    forward = stacked(sum_ref[...])
    linear = product(op, a_ref[...])
    dense = jnp.zeros((LANES, elems), F32)
    mean_more_ref[...] = mean_ref[...]
    for k in range(minor):
        for i in range(local):
            weight = segment_weight(place_ref, minor, local, k, i)
            if k:
                prepare(states[k], r_more_ref, mean_more_ref, double, weight, i, fields, False)
            r = (r_more_ref if k else r_ref)[i * LANES : (i + 1) * LANES, :]
            p = jnp.zeros((LANES, elems), F32)
            for f in range(fields):
                at = (i * fields + f) * LANES
                q = jnp.tanh(states[k][at : at + LANES, :])
                q_ref[f * LANES : (f + 1) * LANES, :] = q
                p = p + q * a_ref[f * LANES : (f + 1) * LANES, :]
            p = weight * p
            dense = dense + p * r
            for f in range(fields):
                rows = slice(f * LANES, (f + 1) * LANES)
                if k + i == 0:
                    sums_ref[rows, :] = q_ref[rows, :] * p
                else:
                    sums_ref[rows, :] += q_ref[rows, :] * p
    for f in range(fields):
        rows = slice(f * LANES, (f + 1) * LANES)
        dense = dense + linear[rows, :] * mean_more_ref[rows, :]
        volume = linear[rows, :] + through(forward, sums_ref[rows, :])
        t_ref[rows, :] = a_ref[rows, :] + step_size * volume
    return jnp.sum(dense, axis=0, keepdims=True)


def slots_of(owner_ref, place_ref, cap, major, minor):
    elems = owner_ref.shape[1]
    owner = owner_ref[...]
    doms = -(-major * minor // 8) * 8
    rows = lax.broadcasted_iota(jnp.int32, (doms, elems), 0)
    named = (rows == owner).astype(F32)
    before = lax.broadcasted_iota(jnp.int32, (elems, elems), 0)
    after = lax.broadcasted_iota(jnp.int32, (elems, elems), 1)
    earlier = dot(named.astype(BF16), (before < after).astype(F32).astype(BF16))
    rank = jnp.sum(named * earlier, axis=0, keepdims=True).astype(jnp.int32)
    high = jnp.zeros_like(owner)
    for k in range(1, major):
        high = high + (owner >= k * minor).astype(jnp.int32)
    low = owner - high * minor
    high = high - place_ref[0]
    low = low - place_ref[2]
    high = jnp.where(high < 0, high + major, high)
    low = jnp.where(low < 0, low + minor, low)
    slot = (high * minor + low) * cap + rank
    return jnp.where(place_ref[3] > 0, slot, -1)


def first_kernel(cap, major, minor, local, nodes, place_ref, owner_ref, top_ref, rest_ref, sum_ref, r_ref, mean_ref, *refs):
    states, refs = refs[:minor], refs[minor:]
    blocks, refs = refs[: major * minor], refs[major * minor :]
    now_ref, fx_ref, more_ref, got_ref, a_ref = refs[:5]
    elems = owner_ref.shape[1]
    slots = cap * major * minor
    wide = now_ref.shape[0]
    fields = wide // LANES
    slot = slots_of(owner_ref, place_ref, cap, major, minor)
    rows = lax.broadcasted_iota(jnp.int32, (slots, elems), 0)
    chosen = (rows == slot).astype(F32).astype(BF16)
    for n, block in enumerate(blocks):
        got_ref[n * cap : (n + 1) * cap, :] = block[...]
    here = pick(got_ref[...].T, chosen)
    a_ref[...] = here[0:wide]
    fx_ref[...] = here[wide:]
    param = a_ref[nodes : nodes + 1, :]
    op = (top_ref[...], rest_ref[...])
    density = advance(
        minor, local, place_ref, states, r_ref, mean_ref, a_ref, op, sum_ref, now_ref, *refs[5:]
    )
    add_faces(now_ref, fx_ref, fields, nodes)
    take_faces(now_ref, fx_ref, fields, nodes)
    fx_ref[LANES - 3 : LANES - 2, :] = jnp.ones((1, elems), F32)
    more_ref[...] = jnp.concatenate(
        [density, param, slot.astype(F32), jnp.zeros((5, elems), F32)], axis=0
    )


def pick_back(chosen, value):
    top, rest = halves(value)
    return dot(chosen, top, NT) + dot(chosen, rest, NT)


def second_kernel(cap, major, minor, local, nodes, place_ref, now_ref, faces_ref, more_ref, top_ref, rest_ref, sum_ref, r_ref, mean_ref, *refs):
    states, refs = refs[:minor], refs[minor:]
    outs, refs = refs[: major * minor], refs[major * minor :]
    t_ref = refs[0]
    wide, elems = now_ref.shape
    fields = wide // LANES
    slots = cap * major * minor
    op = (top_ref[...], rest_ref[...])
    density = advance(
        minor, local, place_ref, states, r_ref, mean_ref, now_ref, op, sum_ref, t_ref, *refs[1:]
    )
    t_ref[nodes : nodes + 1, :] = jnp.ones((1, elems), F32)
    slot = more_ref[2:3, :].astype(jnp.int32)
    rows = lax.broadcasted_iota(jnp.int32, (slots, elems), 0)
    chosen = (rows == slot).astype(F32).astype(BF16)
    sent = pick_back(chosen, t_ref[...])
    sent_faces = pick_back(chosen, faces_ref[...])
    density = (more_ref[0:1, :] + density) * (1.0 / (fields * nodes))
    density = jnp.where(slot >= 0, density, 0.0)
    param = more_ref[1:2, :].astype(jnp.int32)
    count = PARAMS // LANES
    high = lax.shift_right_logical(param, 7)
    low = param - high * LANES
    in_high = lax.broadcasted_iota(jnp.int32, (count, elems), 0) == high
    in_low = (lax.broadcasted_iota(jnp.int32, (LANES, elems), 0) == low).astype(F32).astype(BF16)
    grad = pick(jnp.where(in_high, density, 0.0), in_low, NT)
    for n, out in enumerate(outs):
        out[0:cap, 0:wide] = sent[n * cap : (n + 1) * cap, :]
        out[0:cap, wide:] = sent_faces[n * cap : (n + 1) * cap, :]
        out[cap : cap + RIDE, :] = jnp.zeros((RIDE, wide + 2 * LANES), F32)
        for m in range(4):
            out[cap : cap + RIDE, m * LANES : (m + 1) * LANES] = grad[m * RIDE : (m + 1) * RIDE, :]


def place_block(place_ref, got_ref, block, cap, major, minor, j, k):
    s = lax.rem(place_ref[0] - j + major, major) * minor
    s = s + lax.rem(place_ref[2] - k + minor, minor)
    got_ref[pl.ds(pl.multiple_of(s * cap, 8), cap), :] = block


def faces_kernel(cap, major, minor, place_ref, base_ref, lists_ref, *refs):
    one_ref, two_ref, got_ref = refs[minor:]
    for k in range(minor):
        for j in range(major):
            place_block(place_ref, got_ref, refs[k][j * cap : (j + 1) * cap, :], cap, major, minor, j, k)
    slots = got_ref.shape[0]
    turned = got_ref[...].T
    mine = turned[LANES - 3 : LANES - 2, :] > 0.5
    now = jnp.where(mine, turned, base_ref[...])
    low = pick(now[0:LANES], chosen_slots(lists_ref[0:1, :], slots))
    high = pick(now[LANES:], chosen_slots(lists_ref[1:2, :], slots))
    put_traces(place_ref, low, high, one_ref, two_ref)
    grad = refs[0][major * cap :, :]
    for k in range(1, minor):
        grad = grad + refs[k][major * cap :, :]
    for m in range(4):
        rows = slice(m // 2 * RIDE, (m // 2 + 1) * RIDE)
        at = LANES + m * RIDE
        one_ref[at : at + RIDE, :] = grad[rows, m % 2 * LANES : (m % 2 + 1) * LANES]


def assemble_kernel(nodes, cap, major, minor, place_ref, base_ref, *refs):
    count = major * minor
    out_ref, got_ref = refs[count:]
    for j in range(major):
        for k in range(minor):
            place_block(place_ref, got_ref, refs[j * minor + k][0:cap, :], cap, major, minor, j, k)
    turned = got_ref[...].T
    mine = turned[nodes : nodes + 1, :] > 0.5
    out_ref[...] = jnp.where(mine, turned, base_ref[...])


def last_kernel(place_ref, now_ref, lists_ref, one_ref, two_ref, near_one_ref, near_two_ref, out_ref, face_ref):
    fields, nodes, slots = out_ref.shape
    face_rows(place_ref, lists_ref, one_ref, two_ref, near_one_ref, near_two_ref, slots, face_ref)
    for f in range(fields):
        out_ref[f] = now_ref[pl.ds(f * LANES, nodes), :]
        rows = f * FACE_NODES
        out_ref[f, 0:FACE_NODES, :] += face_ref[pl.ds(rows, FACE_NODES), :]
        out_ref[f, nodes - FACE_NODES : nodes, :] += face_ref[pl.ds(LANES + rows, FACE_NODES), :]


def after(value, *earlier):
    return lax.optimization_barrier((value, *earlier))[0]


def across(one, two):
    size = lax.axis_size("region")
    near = []
    for value, first in ((one, 0), (two, 1)):
        pairs = [(i, i + 1) for i in range(first, size - 1, 2)]
        near.append(lax.ppermute(value, "region", pairs + [(j, i) for i, j in pairs]))
    return near


def summed_on(value, near, axis):
    size = lax.axis_size(axis)
    if size & (size - 1):
        return lax.psum(value, axis)
    value = value + near
    k = 2
    while k < size:
        value = value + lax.ppermute(value, axis, [(i, i ^ k) for i in range(size)])
        k = 2 * k
    return value


def per_device(stored, new_owner, adjoint, deriv, mixing, face_lists, param_map):
    minor = lax.axis_size("segment")
    dom_count = lax.axis_size("dom")
    major = dom_count // minor
    local, _, fields, nodes, elems = stored.shape
    slots = adjoint.shape[2]
    faces = face_lists.shape[1]
    cap = slots // dom_count
    wide = fields * LANES
    axes = ("dom", "segment")
    ys, xs = range(major), range(minor)

    def at(sy, c, x):
        return (sy * minor + c % minor) * minor + x % minor

    def move(value, pairs):
        return lax.ppermute(value, axes, pairs)

    def to_workers(parts):
        got = []
        for j in range(major):
            for k in range(minor):
                pairs = [(at((y + j) % major, x + k, x), at(y, x, x)) for y in ys for x in xs]
                got.append(move(parts[j], pairs) if j + k else parts[j])
        return got

    def from_workers(parts):
        got = []
        for j in range(major):
            total = None
            for k in range(minor):
                pairs = [(at(y, x, x), at((y + j) % major, x + k, x)) for y in ys for x in xs]
                part = parts[j * minor + k]
                part = move(part, pairs) if j + k else part
                total = part if total is None else total + part
            got.append(total)
        return got

    def to_segment(value, k):
        return lax.ppermute(value, "segment", [(x, (x + k) % minor) for x in xs])

    dom = lax.axis_index("dom")
    seg = lax.axis_index("segment")
    region = lax.axis_index("region")
    ty, tc = dom // minor, dom % minor
    place = jnp.stack([ty, tc, seg, (tc == seg).astype(jnp.int32), region % 2]).astype(jnp.int32)
    owner = new_owner.reshape(1, elems)
    mapped = param_map.reshape(1, slots)

    rows = stored.reshape(local, STEPS, fields, nodes, elems // LANES, LANES)
    rows = rows.transpose(0, 2, 3, 4, 1, 5).reshape(-1, LANES)
    own = call(
        functools.partial(states_kernel, local, fields, nodes),
        (shape(local * wide, elems),) * STEPS,
        [VMEM],
    )(rows)
    states = [
        [own[step]]
        + [
            lax.ppermute(
                own[step], axes, [(at(y, x, x + k), at(y, x, x)) for y in ys for x in xs]
            )
            for k in range(1, minor)
        ]
        for step in range(STEPS)
    ]

    trace = shape(LANES, faces)
    low, high = call(
        start_kernel,
        (trace, trace),
        [SMEM] + [VMEM] * 2,
        [pltpu.VMEM((2, LANES, slots), F32)],
    )(place, adjoint, face_lists)
    near_low, near_high = across(low, high)
    top, rest, total = call(
        operator_kernel,
        (shape(wide, wide, dtype=BF16), shape(wide, wide, dtype=BF16), shape(LANES, LANES)),
        [VMEM, SMEM],
        [pltpu.VMEM((LANES, LANES), F32)],
    )(deriv, mixing.reshape(-1))
    ready = call(
        functools.partial(ready_kernel, local, minor),
        (shape(local * LANES, elems), shape(wide, elems)) * STEPS,
        [SMEM] + [VMEM] * (1 + STEPS),
    )(place, total, *own)

    sent = wide + 2 * LANES
    *a_out, f0 = call(
        functools.partial(outgoing_kernel, cap, major, minor),
        (shape(cap, sent),) * major + (shape(2 * LANES, slots),),
        [SMEM] + [VMEM] * 7,
        [pltpu.VMEM((sent, slots), F32), pltpu.VMEM((slots, sent), F32)],
    )(place, adjoint, mapped, face_lists, low, high, near_low, near_high)
    blocks = to_workers(a_out)

    base, base_face = call(
        linear_kernel,
        (shape(wide, slots), shape(2 * LANES, slots)),
        [VMEM] * 4,
        [pltpu.VMEM((wide, slots), F32), pltpu.VMEM((wide, slots), F32)],
    )(adjoint, f0, top, rest)
    blocks[-1] = after(blocks[-1], base, base_face)

    work = [
        pltpu.VMEM((local * LANES, elems), F32),
        pltpu.VMEM((wide, elems), F32),
        pltpu.VMEM((wide, elems), F32),
        pltpu.VMEM((wide, elems), F32),
    ]
    now, faces_now, more = call(
        functools.partial(first_kernel, cap, major, minor, local, nodes),
        (shape(wide, elems), shape(2 * LANES, elems), shape(8, elems)),
        [SMEM] + [VMEM] * (6 + minor + dom_count),
        [
            pltpu.VMEM((slots, sent), F32),
            pltpu.VMEM((wide, elems), F32),
        ]
        + work,
    )(place, owner, top, rest, total, *ready[0:2], *states[0], *blocks)

    parts = call(
        functools.partial(second_kernel, cap, major, minor, local, nodes),
        (shape(cap + RIDE, sent),) * dom_count,
        [SMEM] + [VMEM] * (8 + minor),
        [pltpu.VMEM((wide, elems), F32)] + work,
    )(place, now, faces_now, more, top, rest, total, *ready[2:4], *states[1])
    got = from_workers(parts)
    last_blocks = []
    for value in got[:1]:
        mine = value[0:cap, 0:wide]
        last_blocks = last_blocks + [mine] + [to_segment(mine, k) for k in range(1, minor)]
    grad = sum(value[cap:, 0 : 4 * LANES] for value in got)
    mine = jnp.concatenate(
        [value[0:cap, wide:] for value in got] + [grad[:, 0 : 2 * LANES], grad[:, 2 * LANES :]]
    )
    face_blocks = [mine] + [to_segment(mine, k) for k in range(1, minor)]
    for value in got[1:]:
        mine = after(value[0:cap, 0:wide], last_blocks[-1])
        last_blocks = last_blocks + [mine] + [to_segment(mine, k) for k in range(1, minor)]
    low1, high1 = call(
        functools.partial(faces_kernel, cap, major, minor),
        (shape(LANES + 4 * RIDE, faces), trace),
        [SMEM] + [VMEM] * (2 + minor),
        [pltpu.VMEM((slots, 2 * LANES), F32)],
    )(place, base_face, face_lists, *face_blocks)
    near_low1, near_high1 = across(low1, high1)
    grad = summed_on(low1[LANES:], near_low1[LANES:], "region")

    assembled = call(
        functools.partial(assemble_kernel, nodes, cap, major, minor),
        shape(wide, slots),
        [SMEM] + [VMEM] * (1 + dom_count),
        [pltpu.VMEM((slots, wide), F32)],
        moved=8e7,
    )(place, base, *last_blocks)
    out = call(
        last_kernel,
        shape(fields, nodes, slots),
        [SMEM] + [VMEM] * 6,
        [pltpu.VMEM((2 * LANES, slots), F32)],
    )(place, assembled, face_lists, low1, high1, near_low1, near_high1)
    return (out, grad.reshape(PARAMS))


def solution(mesh):
    return jax.shard_map(
        per_device,
        mesh=mesh,
        in_specs=(
            P("segment", None, None, None, ("region", "dom")),
            P(("region", "dom"), None),
            P(None, None, ("region", "dom")),
            P(),
            P(),
            P(None, ("region", "dom")),
            P(("region", "dom")),
        ),
        out_specs=(P(None, None, ("region", "dom")), P()),
        check_vma=False,
    )
```

time: 96.8 us -> 79 us (0.82)
  starting transfers between devices: 46.6 us -> 29.7 us
  local copies, waits for them, and re-layouts: 10.3 us -> 2.89 us
  Pallas kernels: 20.7 us -> 24.5 us
  waiting for transfers between devices: 16.6 us -> 19.8 us
    ppermute x24 -> x16, starting transfers between devices: 46.6 us -> 29.7 us  [the longest x6 13.7 us: move(): return lax.ppermute(value, axes, pairs)]
    unnamed x23 -> x15, local copies, waits for them, and re-layouts: 8.07 us -> 2.66 us
    pallas_call x6 -> x9, Pallas kernels: 17.5 us -> 21.4 us  [the longest x1 5.31 us: per_device(): call(functools.partial(first_kernel, cap, major, minor, local, nodes), (s...]
    ppermute x24 -> x16, waiting for transfers between devices: 16.6 us -> 19.8 us  [the longest x6 6.25 us: move(): return lax.ppermute(value, axes, pairs)]
    gather x1 -> x0, local copies, waits for them, and re-layouts: 1.25 us -> none  [per_device(): weights = table[order].reshape(minor * local)]
  transfers between devices with their start and end apart: 24 -> 16, of which waited for: 9 -> 6; matrix products, arithmetic and copies ran while one was open for 4% -> 1% of each run, Pallas kernels for 8% -> 22%
where the time goes in v1:
time: 79 us; the launch traced here: 78.6 us
  starting transfers between devices  29.7 us (38%)
  Pallas kernels  24.5 us (31%)
  waiting for transfers between devices  19.8 us (25%)
  local copies, waits for them, and re-layouts  2.89 us (4%)
  between operations  1 us (1%)
    ppermute x6, starting transfers between devices, move(): return lax.ppermute(value, axes, pairs)  13.7 us
    ppermute x4, starting transfers between devices, across(): lax.ppermute(value, 'region', pairs + [(j, i) for i, j in pairs])  7.99 us
    ppermute x6, waiting for transfers between devices, move(): return lax.ppermute(value, axes, pairs)  6.25 us
    pallas_call x1, Pallas kernels, per_device(): call(functools.partial(first_kernel, cap, major, minor, local, nodes), (s...  5.31 us
    ppermute x3, waiting for transfers between devices, to_segment(): return lax.ppermute(value, 'segment', [(x, (x + k) % minor) for x in xs])  5.25 us
    pallas_call x1, Pallas kernels, per_device(): call(functools.partial(second_kernel, cap, major, minor, local, nodes), (...  4.14 us
    ppermute x4, waiting for transfers between devices, across(): lax.ppermute(value, 'region', pairs + [(j, i) for i, j in pairs])  3.88 us
    pallas_call x1, Pallas kernels, per_device(): call(linear_kernel, (shape(wide, slots), shape(2 * LANES, slots)), [VMEM]...  3.63 us
  transfers between devices with their start and end apart: 16, of which 6 were waited for; matrix products, arithmetic and copies ran while one was open for 1% of the time, Pallas kernels for 22%

profile of v1, /device:TPU:0, one launch (start us, length us, event | category | flops | bytes accessed | tf_op | source)
XLA Modules:
  0.0 78.6 jit_solution(1564341704145725965)
XLA Ops:
  0.6 1.7 %copy-done.1 = f32[2,2,5,125,256]{4,1,3,2,0:T(2,128)S(1)} copy-done((f32[2,2,5,125,256]{4,1,3,2,0:T(2,128)S(1)}, f32[2,2,5,125,256]{4,1,3,2,0:T(2,128)}, u32[]{:S(2)}) %copy-start.1) | copy-done | bytes 2560024
  2.4 1.3 %shard_map.90 = (f32[1280,256]{1,0:T(8,128)}, f32[1280,256]{1,0:T(8,128)S(1)}) custom-call(f32[5000,128]{1,0:T(8,128)S(1)} %bitcast.13), custom_call_target="tpu_custom_call" | custom-call | flops 1000000 | bytes 10000 | tf_op jit(solution)/shard_map/pallas_call | solution.py:483
  3.6 1.4 %collective-permute-start.2 = (f32[1280,256]{1,0:T(8,128)}, f32[1280,256]{1,0:T(8,128)}, u32[]{:S(2)}, u32[]{:S(2)}) collective-permute-start(f32[1280,256]{1,0:T(8,128)} %get-tuple-element.36.refs_0_), channel_id=1, source_target_pairs={{1,0},{2,3},{5,4},{6,7},{9,8},{10,11},{13,12},{14,15},{17,16},{18,... | collective-permute-start | bytes 3932168 | tf_op jit(solution)/shard_map/ppermute | solution.py:491
  5.0 1.3 %collective-permute-start.6 = (f32[1280,256]{1,0:T(8,128)S(1)}, f32[1280,256]{1,0:T(8,128)}, u32[]{:S(2)}, u32[]{:S(2)}) collective-permute-start(f32[1280,256]{1,0:T(8,128)S(1)} %get-tuple-element.37.refs_1_.refs_0_), channel_id=1, source_target_pairs={{1,0},{2,3},{5,4},{6,7},{9,8},{10,11},{13,12},{14,15},{17,16},{18,... | collective-permute-start | bytes 3932168 | tf_op jit(solution)/shard_map/ppermute | solution.py:491
  6.4 0.1 stack.27.place_ref
  6.5 0.8 %shard_map.86 = (f32[128,128]{1,0:T(8,128)S(1)}, f32[128,128]{1,0:T(8,128)S(1)}) custom-call(s32[5]{0:T(128)S(1)} %stack.27.place_ref, f32[5,125,384]{2,1,0:T(8,128)S(1)} %copy-done, s32[2,128]{1,0:T(2,128)S(1)} %copy-done.3), custom_call_target="tpu_custom_call" | custom-call | flops 1000000 | bytes 10000 | tf_op jit(solution)/shard_map/pallas_call | solution.py:500
  7.3 3.1 %collective-permute-start = (f32[128,128]{1,0:T(8,128)S(1)}, f32[128,128]{1,0:T(8,128)S(1)}, u32[]{:S(2)}, u32[]{:S(2)}) collective-permute-start(f32[128,128]{1,0:T(8,128)S(1)} %get-tuple-element.29.one_ref), channel_id=1, source_target_pairs={{0,8},{16,24},{8,0},{24,16},{1,9},{17,25},{9,1},{25,17},{2,10},{18... | collective-permute-start | bytes 196616 | tf_op jit(solution)/shard_map/ppermute | solution.py:416
  10.4 0.7 collective-permute-start.1
  11.1 1.6 %collective-permute-done.near_one_ref = f32[128,128]{1,0:T(8,128)S(1)} collective-permute-done((f32[128,128]{1,0:T(8,128)S(1)}, f32[128,128]{1,0:T(8,128)S(1)}, u32[]{:S(2)}, u32[]{:S(2)}) %collective-permute-start) | collective-permute-done | bytes 65568 | tf_op jit(solution)/shard_map/ppermute | solution.py:416
  12.6 0.0 collective-permute-done.1.near_two_ref
  12.6 1.8 %shard_map.87 = (f32[96,896]{1,0:T(8,128)S(1)}, f32[96,896]{1,0:T(8,128)}, f32[256,384]{1,0:T(8,128)S(1)}) custom-call(s32[5]{0:T(128)S(1)} %stack.27.place_ref, f32[5,125,384]{2,1,0:T(8,128)S(1)} %copy-done, s32[1,384]{1,0:T(1,128)S(1)} %reshape.22.map_ref, s32[2,128]{1,0:T(2,128)S(1)} %copy-done.3, f32[128,128]{1,0:T(8,128)S(1)} %get-tuple-element.29.one_ref, ...), custom_call_target="tpu_custom_call" | custom-call | flops 1000000 | bytes 10000 | tf_op jit(solution)/shard_map/pallas_call | solution.py:520
  14.5 1.3 %collective-permute-start.5 = (f32[96,896]{1,0:T(8,128)}, f32[96,896]{1,0:T(8,128)S(1)}, u32[]{:S(2)}, u32[]{:S(2)}) collective-permute-start(f32[96,896]{1,0:T(8,128)} %get-tuple-element.41), channel_id=1, source_target_pairs={{6,0},{5,3},{2,4},{1,7},{14,8},{13,11},{10,12},{9,15},{22,16},{21,... | collective-permute-start | bytes 1032200 | tf_op jit(solution)/shard_map/ppermute | solution.py:448
  15.7 1.3 %collective-permute-start.3 = (f32[96,896]{1,0:T(8,128)S(1)}, f32[96,896]{1,0:T(8,128)}, u32[]{:S(2)}, u32[]{:S(2)}) collective-permute-start(f32[96,896]{1,0:T(8,128)S(1)} %get-tuple-element.40.refs_2_), channel_id=1, source_target_pairs={{2,0},{1,3},{6,4},{5,7},{10,8},{9,11},{14,12},{13,15},{18,16},{17,... | collective-permute-start | bytes 1032200 | tf_op jit(solution)/shard_map/ppermute | solution.py:448
  17.0 3.9 %collective-permute-start.4 = (f32[96,896]{1,0:T(8,128)}, f32[96,896]{1,0:T(8,128)}, u32[]{:S(2)}, u32[]{:S(2)}) collective-permute-start(f32[96,896]{1,0:T(8,128)} %get-tuple-element.41), channel_id=1, source_target_pairs={{4,0},{7,3},{0,4},{3,7},{12,8},{15,11},{8,12},{11,15},{20,16},{23,... | collective-permute-start | bytes 1032200 | tf_op jit(solution)/shard_map/ppermute | solution.py:448
  21.0 0.1 reshape.23.mixing_ref
  21.0 0.0 copy-start.2
  21.0 0.9 %copy-done.2 = f32[3,125,125]{2,1,0:T(8,128)S(1)} copy-done((f32[3,125,125]{2,1,0:T(8,128)S(1)}, f32[3,125,125]{2,1,0:T(8,128)}, u32[]{:S(2)}) %copy-start.2) | copy-done | bytes 187524
  22.0 1.2 %shard_map.88 = (bf16[640,640]{1,0:T(8,128)(2,1)S(1)}, bf16[640,640]{1,0:T(8,128)(2,1)S(1)}, f32[128,128]{1,0:T(8,128)S(1)}) custom-call(f32[3,125,125]{2,1,0:T(8,128)S(1)} %copy-done.2, f32[75]{0:T(128)S(1)} %reshape.23.mixing_ref), custom_call_target="tpu_custom_call" | custom-call | flops 1000000 | bytes 10000 | tf_op jit(solution)/shard_map/pallas_call | solution.py:507
  23.2 2.5 %shard_map.91 = (f32[256,256]{1,0:T(8,128)S(1)}, f32[640,256]{1,0:T(8,128)S(1)}, f32[256,256]{1,0:T(8,128)S(1)}, f32[640,256]{1,0:T(8,128)S(1)}) custom-call(s32[5]{0:T(128)S(1)} %stack.27.place_ref, f32[128,128]{1,0:T(8,128)S(1)} %get-tuple-element.35.sum_ref, f32[1280,256]{1,0:T(8,128)} %get-tuple-element.36.refs_0_, ...), custom_call_target="tpu_custom_call" | custom-call | flops 1000000 | bytes 10000 | tf_op jit(solution)/shard_map/pallas_call | solution.py:513
  25.7 0.0 copy-start.4
  25.7 3.6 %shard_map.89 = (f32[640,384]{1,0:T(8,128)S(1)}, f32[256,384]{1,0:T(8,128)S(1)}) custom-call(f32[5,125,384]{2,1,0:T(8,128)S(1)} %copy-done, f32[256,384]{1,0:T(8,128)S(1)} %get-tuple-element.31.f_ref, bf16[640,640]{1,0:T(8,128)(2,1)S(1)} %get-tuple-element.32.top_ref, bf16[640,640]{1,0:T(8,128)(2,1)S(1)} %get-tuple-element.33.rest_ref), custom_call_target="tpu_custom_call" | custom-call | flops 1000000 | bytes 10000 | tf_op jit(solution)/shard_map/pallas_call | solution.py:528
  29.3 0.0 collective-permute-done.5.refs_5_
  29.3 0.0 collective-permute-done.3.refs_3_
  29.3 0.0 collective-permute-done.4.refs_4_
  29.4 0.0 collective-permute-done.2.refs_1_
  29.4 5.3 %shard_map.92 = (f32[640,256]{1,0:T(8,128)S(1)}, f32[256,256]{1,0:T(8,128)S(1)}, f32[8,256]{1,0:T(8,128)S(1)}) custom-call(s32[5]{0:T(128)S(1)} %stack.27.place_ref, s32[1,256]{1,0:T(1,128)S(1)} %bitcast.14, bf16[640,640]{1,0:T(8,128)(2,1)S(1)} %get-tuple-element.32.top_ref, bf16[640,640]{1,0:T(8,128)(2,1)S(1)} %get-tuple-element.33.rest_ref, ...), custom_call_target="tpu_custom_call" | custom-call | flops 1000000 | bytes 10000 | tf_op jit(solution)/shard_map/pallas_call | solution.py:542
  34.7 3.2 %collective-permute-done.6.refs_1_ = f32[1280,256]{1,0:T(8,128)} collective-permute-done((f32[1280,256]{1,0:T(8,128)S(1)}, f32[1280,256]{1,0:T(8,128)}, u32[]{:S(2)}, u32[]{:S(2)}) %collective-permute-start.6) | collective-permute-done | bytes 1310752 | tf_op jit(solution)/shard_map/ppermute | solution.py:491
  37.9 4.1 %shard_map.93 = (f32[104,896]{1,0:T(8,128)S(1)}, f32[104,896]{1,0:T(8,128)S(1)}, f32[104,896]{1,0:T(8,128)S(1)}, f32[104,896]{1,0:T(8,128)S(1)}) custom-call(s32[5]{0:T(128)S(1)} %stack.27.place_ref, f32[640,256]{1,0:T(8,128)S(1)} %get-tuple-element.44.now_ref, f32[256,256]{1,0:T(8,128)S(1)} %get-tuple-element.45.faces_ref, ...), custom_call_target="tpu_custom_call" | custom-call | flops 1000000 | bytes 10000 | tf_op jit(solution)/shard_map/pallas_call | solution.py:553
  42.0 2.1 %collective-permute-start.10 = (f32[104,896]{1,0:T(8,128)S(1)}, f32[104,896]{1,0:T(8,128)S(1)}, u32[]{:S(2)}, u32[]{:S(2)}) collective-permute-start(f32[104,896]{1,0:T(8,128)S(1)} %get-tuple-element.52), channel_id=1, source_target_pairs={{0,6},{3,5},{4,2},{7,1},{8,14},{11,13},{12,10},{15,9},{16,22},{19,... | collective-permute-start | bytes 1118216 | tf_op jit(solution)/shard_map/ppermute | solution.py:448
  44.1 3.8 %collective-permute-start.9 = (f32[104,896]{1,0:T(8,128)S(1)}, f32[104,896]{1,0:T(8,128)S(1)}, u32[]{:S(2)}, u32[]{:S(2)}) collective-permute-start(f32[104,896]{1,0:T(8,128)S(1)} %get-tuple-element.51), channel_id=1, source_target_pairs={{0,4},{3,7},{4,0},{7,3},{8,12},{11,15},{12,8},{15,11},{16,20},{19,... | collective-permute-start | bytes 1118216 | tf_op jit(solution)/shard_map/ppermute | solution.py:448
  48.0 1.3 %collective-permute-start.7 = (f32[104,896]{1,0:T(8,128)S(1)}, f32[104,896]{1,0:T(8,128)S(1)}, u32[]{:S(2)}, u32[]{:S(2)}) collective-permute-start(f32[104,896]{1,0:T(8,128)S(1)} %get-tuple-element.50), channel_id=1, source_target_pairs={{0,2},{3,1},{4,6},{7,5},{8,10},{11,9},{12,14},{15,13},{16,18},{19,... | collective-permute-start | bytes 1118216 | tf_op jit(solution)/shard_map/ppermute | solution.py:448
  49.3 6.2 %collective-permute-done.9 = f32[104,896]{1,0:T(8,128)S(1)} collective-permute-done((f32[104,896]{1,0:T(8,128)S(1)}, f32[104,896]{1,0:T(8,128)S(1)}, u32[]{:S(2)}, u32[]{:S(2)}) %collective-permute-start.9) | collective-permute-done | bytes 372768 | tf_op jit(solution)/shard_map/ppermute | solution.py:448
  55.6 0.0 collective-permute-done.7
  55.7 0.1 collective-permute-start.12
  55.8 2.1 %collective-permute-start.8 = (f32[96,640]{1,0:T(8,128)S(1)}, f32[96,640]{1,0:T(8,128)S(1)}, u32[]{:S(2)}, u32[]{:S(2)}) collective-permute-start(f32[96,640]{1,0:T(8,128)S(1)} %slice.40.refs_0_), channel_id=1, source_target_pairs={{0,1},{1,0},{2,3},{3,2},{4,5},{5,4},{6,7},{7,6},{8,9},{9,8},{10,11... | collective-permute-start | bytes 737288 | tf_op jit(solution)/shard_map/ppermute | solution.py:471
  57.9 5.2 %collective-permute-done.12.refs_1_ = f32[208,256]{1,0:T(8,128)S(1)} collective-permute-done((f32[208,256]{1,0:T(8,128)S(1)}, f32[208,256]{1,0:T(8,128)S(1)}, u32[]{:S(2)}, u32[]{:S(2)}) %collective-permute-start.12) | collective-permute-done | bytes 213024 | tf_op jit(solution)/shard_map/ppermute | solution.py:471
  63.1 1.0 %shard_map.95 = (f32[160,128]{1,0:T(8,128)S(1)}, f32[128,128]{1,0:T(8,128)S(1)}) custom-call(s32[5]{0:T(128)S(1)} %stack.27.place_ref, f32[256,384]{1,0:T(8,128)S(1)} %get-tuple-element.42.base_ref, s32[2,128]{1,0:T(2,128)S(1)} %copy-done.3, f32[208,256]{1,0:T(8,128)S(1)} %pad_maximum_fusion.refs_0_, f32[208,256]{1,0:T(8,128)S(1)} %collective-permute-done.12.refs_1_), custom_call_target="tpu_custom_call" | custom-call | flops 1000000 | bytes 10000 | tf_op jit(solution)/shard_map/pallas_call | solution.py:572
  64.1 3.6 %collective-permute-start.13 = (f32[160,128]{1,0:T(8,128)S(1)}, f32[160,128]{1,0:T(8,128)S(1)}, u32[]{:S(2)}, u32[]{:S(2)}) collective-permute-start(f32[160,128]{1,0:T(8,128)S(1)} %get-tuple-element.54.one_ref), channel_id=1, source_target_pairs={{0,8},{16,24},{8,0},{24,16},{1,9},{17,25},{9,1},{25,17},{2,10},{18... | collective-permute-start | bytes 245768 | tf_op jit(solution)/shard_map/ppermute | solution.py:416
  67.7 0.0 collective-permute-done.8.refs_1_
  67.7 0.1 collective-permute-start.11
  67.8 2.3 %collective-permute-done.13.near_one_ref = f32[160,128]{1,0:T(8,128)S(1)} collective-permute-done((f32[160,128]{1,0:T(8,128)S(1)}, f32[160,128]{1,0:T(8,128)S(1)}, u32[]{:S(2)}, u32[]{:S(2)}) %collective-permute-start.13) | collective-permute-done | bytes 81952 | tf_op jit(solution)/shard_map/ppermute | solution.py:416
  70.1 3.2 %collective-permute-start.15 = (f32[32,128]{1,0:T(8,128)S(1)}, f32[32,128]{1,0:T(8,128)S(1)}, u32[]{:S(2)}, u32[]{:S(2)}) collective-permute-start(f32[32,128]{1,0:T(8,128)S(1)} %slice_add_fusion), channel_id=1, source_target_pairs={{0,16},{8,24},{16,0},{24,8},{1,17},{9,25},{17,1},{25,9},{2,18},{10... | collective-permute-start | bytes 49160 | tf_op jit(solution)/shard_map/ppermute | solution.py:427
  73.3 0.7 collective-permute-start.14
  73.9 1.2 %collective-permute-done.15 = f32[32,128]{1,0:T(8,128)S(1)} collective-permute-done((f32[32,128]{1,0:T(8,128)S(1)}, f32[32,128]{1,0:T(8,128)S(1)}, u32[]{:S(2)}, u32[]{:S(2)}) %collective-permute-start.15) | collective-permute-done | bytes 16416 | tf_op jit(solution)/shard_map/ppermute | solution.py:427
  75.1 0.6 add_bitcast_fusion
  75.7 1.0 %shard_map.94.now_ref = f32[640,384]{1,0:T(8,128)S(1)} custom-call(s32[5]{0:T(128)S(1)} %stack.27.place_ref, f32[640,384]{1,0:T(8,128)S(1)} %get-tuple-element.34.base_ref, f32[96,640]{1,0:T(8,128)S(1)} %slice.40.refs_0_, f32[96,640]{1,0:T(8,128)S(1)} %collective-permute-done.8.refs_1_, f32[96,640]{1,0:T(8,128)S(1)} %slice.41.refs_2_, ...), custom_call_target="tpu_custom_call" | custom-call | flops 1000000 | bytes 80000000 | tf_op jit(solution)/shard_map/pallas_call | solution.py:581
  76.7 0.0 collective-permute-done.14.near_two_ref
  76.7 1.8 %shard_map.96 = f32[5,125,384]{2,1,0:T(8,128)} custom-call(s32[5]{0:T(128)S(1)} %stack.27.place_ref, f32[640,384]{1,0:T(8,128)S(1)} %shard_map.94.now_ref, s32[2,128]{1,0:T(2,128)S(1)} %copy-done.3, f32[160,128]{1,0:T(8,128)S(1)} %get-tuple-element.54.one_ref, f32[128,128]{1,0:T(8,128)S(1)} %get-tuple-element.55.two_ref, ...), custom_call_target="tpu_custom_call" | custom-call | flops 1000000 | bytes 10000 | tf_op jit(solution)/shard_map/pallas_call | solution.py:588
  (24 shorter events, 0.2 us)
Async XLA Ops:
  0.6 1.7 %copy-start.1 = (f32[2,2,5,125,256]{4,1,3,2,0:T(2,128)S(1)}, f32[2,2,5,125,256]{4,1,3,2,0:T(2,128)}, u32[]{:S(2)}) copy-start(f32[2,2,5,125,256]{4,1,3,2,0:T(2,128)} %param.7) | copy-start | bytes 7680004
  2.4 4.1 %copy-start = (f32[5,125,384]{2,1,0:T(8,128)S(1)}, f32[5,125,384]{2,1,0:T(8,128)}, u32[]{:S(2)}) copy-start(f32[5,125,384]{2,1,0:T(8,128)} %a_in_ref.1) | copy-start | bytes 2880004
  2.4 4.1 %copy-start.3 = (s32[2,128]{1,0:T(2,128)S(1)}, s32[2,128]{1,0:T(2,128)}, u32[]{:S(2)}) copy-start(s32[2,128]{1,0:T(2,128)} %lists_ref.7) | copy-start | bytes 3076
  2.4 8.7 %copy-start.6 = (s32[384]{0:T(512)S(1)}, s32[384]{0:T(512)}, u32[]{:S(2)}) copy-start(s32[384]{0:T(512)} %param.13) | copy-start | bytes 4612
  3.6 17.3 %copy-start.5 = (f32[3,5,5]{2,0,1:T(4,128)S(1)}, f32[3,5,5]{2,0,1:T(4,128)}, u32[]{:S(2)}) copy-start(f32[3,5,5]{2,0,1:T(4,128)} %param.11) | copy-start | bytes 904
  3.6 25.7 %collective-permute-start.2 = (f32[1280,256]{1,0:T(8,128)}, f32[1280,256]{1,0:T(8,128)}, u32[]{:S(2)}, u32[]{:S(2)}) collective-permute-start(f32[1280,256]{1,0:T(8,128)} %get-tuple-element.36.refs_0_), channel_id=1, source_target_pairs={{1,0},{2,3},{5,4},{6,7},{9,8},{10,11},{13,12},{14,15},{17,16},{18,... | collective-permute-start | bytes 3932168 | tf_op jit(solution)/shard_map/ppermute | solution.py:491
  5.0 32.9 %collective-permute-start.6 = (f32[1280,256]{1,0:T(8,128)S(1)}, f32[1280,256]{1,0:T(8,128)}, u32[]{:S(2)}, u32[]{:S(2)}) collective-permute-start(f32[1280,256]{1,0:T(8,128)S(1)} %get-tuple-element.37.refs_1_.refs_0_), channel_id=1, source_target_pairs={{1,0},{2,3},{5,4},{6,7},{9,8},{10,11},{13,12},{14,15},{17,16},{18,... | collective-permute-start | bytes 3932168 | tf_op jit(solution)/shard_map/ppermute | solution.py:491
  7.3 5.3 %collective-permute-start = (f32[128,128]{1,0:T(8,128)S(1)}, f32[128,128]{1,0:T(8,128)S(1)}, u32[]{:S(2)}, u32[]{:S(2)}) collective-permute-start(f32[128,128]{1,0:T(8,128)S(1)} %get-tuple-element.29.one_ref), channel_id=1, source_target_pairs={{0,8},{16,24},{8,0},{24,16},{1,9},{17,25},{9,1},{25,17},{2,10},{18... | collective-permute-start | bytes 196616 | tf_op jit(solution)/shard_map/ppermute | solution.py:416
  10.4 2.2 %collective-permute-start.1 = (f32[128,128]{1,0:T(8,128)S(1)}, f32[128,128]{1,0:T(8,128)S(1)}, u32[]{:S(2)}, u32[]{:S(2)}) collective-permute-start(f32[128,128]{1,0:T(8,128)S(1)} %get-tuple-element.30.two_ref), channel_id=1, source_target_pairs={{8,16},{16,8},{9,17},{17,9},{10,18},{18,10},{11,19},{19,11},{12,20... | collective-permute-start | bytes 196616 | tf_op jit(solution)/shard_map/ppermute | solution.py:416
  14.5 14.9 %collective-permute-start.5 = (f32[96,896]{1,0:T(8,128)}, f32[96,896]{1,0:T(8,128)S(1)}, u32[]{:S(2)}, u32[]{:S(2)}) collective-permute-start(f32[96,896]{1,0:T(8,128)} %get-tuple-element.41), channel_id=1, source_target_pairs={{6,0},{5,3},{2,4},{1,7},{14,8},{13,11},{10,12},{9,15},{22,16},{21,... | collective-permute-start | bytes 1032200 | tf_op jit(solution)/shard_map/ppermute | solution.py:448
  15.7 13.6 %collective-permute-start.3 = (f32[96,896]{1,0:T(8,128)S(1)}, f32[96,896]{1,0:T(8,128)}, u32[]{:S(2)}, u32[]{:S(2)}) collective-permute-start(f32[96,896]{1,0:T(8,128)S(1)} %get-tuple-element.40.refs_2_), channel_id=1, source_target_pairs={{2,0},{1,3},{6,4},{5,7},{10,8},{9,11},{14,12},{13,15},{18,16},{17,... | collective-permute-start | bytes 1032200 | tf_op jit(solution)/shard_map/ppermute | solution.py:448
  17.0 12.3 %collective-permute-start.4 = (f32[96,896]{1,0:T(8,128)}, f32[96,896]{1,0:T(8,128)}, u32[]{:S(2)}, u32[]{:S(2)}) collective-permute-start(f32[96,896]{1,0:T(8,128)} %get-tuple-element.41), channel_id=1, source_target_pairs={{4,0},{7,3},{0,4},{3,7},{12,8},{15,11},{8,12},{11,15},{20,16},{23,... | collective-permute-start | bytes 1032200 | tf_op jit(solution)/shard_map/ppermute | solution.py:448
  21.0 0.9 %copy-start.2 = (f32[3,125,125]{2,1,0:T(8,128)S(1)}, f32[3,125,125]{2,1,0:T(8,128)}, u32[]{:S(2)}) copy-start(f32[3,125,125]{2,1,0:T(8,128)} %deriv_ref.1) | copy-start | bytes 562504
  25.7 3.7 %copy-start.4 = (s32[256,1]{0,1:T(1,128)S(1)}, s32[256,1]{0,1:T(1,128)}, u32[]{:S(2)}) copy-start(s32[256,1]{0,1:T(1,128)} %param.8) | copy-start | bytes 3076
  42.0 7.2 %collective-permute-start.10 = (f32[104,896]{1,0:T(8,128)S(1)}, f32[104,896]{1,0:T(8,128)S(1)}, u32[]{:S(2)}, u32[]{:S(2)}) collective-permute-start(f32[104,896]{1,0:T(8,128)S(1)} %get-tuple-element.52), channel_id=1, source_target_pairs={{0,6},{3,5},{4,2},{7,1},{8,14},{11,13},{12,10},{15,9},{16,22},{19,... | collective-permute-start | bytes 1118216 | tf_op jit(solution)/shard_map/ppermute | solution.py:448
  44.1 11.4 %collective-permute-start.9 = (f32[104,896]{1,0:T(8,128)S(1)}, f32[104,896]{1,0:T(8,128)S(1)}, u32[]{:S(2)}, u32[]{:S(2)}) collective-permute-start(f32[104,896]{1,0:T(8,128)S(1)} %get-tuple-element.51), channel_id=1, source_target_pairs={{0,4},{3,7},{4,0},{7,3},{8,12},{11,15},{12,8},{15,11},{16,20},{19,... | collective-permute-start | bytes 1118216 | tf_op jit(solution)/shard_map/ppermute | solution.py:448
  48.0 7.6 %collective-permute-start.7 = (f32[104,896]{1,0:T(8,128)S(1)}, f32[104,896]{1,0:T(8,128)S(1)}, u32[]{:S(2)}, u32[]{:S(2)}) collective-permute-start(f32[104,896]{1,0:T(8,128)S(1)} %get-tuple-element.50), channel_id=1, source_target_pairs={{0,2},{3,1},{4,6},{7,5},{8,10},{11,9},{12,14},{15,13},{16,18},{19,... | collective-permute-start | bytes 1118216 | tf_op jit(solution)/shard_map/ppermute | solution.py:448
  55.7 7.4 %collective-permute-start.12 = (f32[208,256]{1,0:T(8,128)S(1)}, f32[208,256]{1,0:T(8,128)S(1)}, u32[]{:S(2)}, u32[]{:S(2)}) collective-permute-start(f32[208,256]{1,0:T(8,128)S(1)} %pad_maximum_fusion.refs_0_), channel_id=1, source_target_pairs={{0,1},{1,0},{2,3},{3,2},{4,5},{5,4},{6,7},{7,6},{8,9},{9,8},{10,11... | collective-permute-start | bytes 638984 | tf_op jit(solution)/shard_map/ppermute | solution.py:471
  55.8 11.9 %collective-permute-start.8 = (f32[96,640]{1,0:T(8,128)S(1)}, f32[96,640]{1,0:T(8,128)S(1)}, u32[]{:S(2)}, u32[]{:S(2)}) collective-permute-start(f32[96,640]{1,0:T(8,128)S(1)} %slice.40.refs_0_), channel_id=1, source_target_pairs={{0,1},{1,0},{2,3},{3,2},{4,5},{5,4},{6,7},{7,6},{8,9},{9,8},{10,11... | collective-permute-start | bytes 737288 | tf_op jit(solution)/shard_map/ppermute | solution.py:471
  64.1 6.0 %collective-permute-start.13 = (f32[160,128]{1,0:T(8,128)S(1)}, f32[160,128]{1,0:T(8,128)S(1)}, u32[]{:S(2)}, u32[]{:S(2)}) collective-permute-start(f32[160,128]{1,0:T(8,128)S(1)} %get-tuple-element.54.one_ref), channel_id=1, source_target_pairs={{0,8},{16,24},{8,0},{24,16},{1,9},{17,25},{9,1},{25,17},{2,10},{18... | collective-permute-start | bytes 245768 | tf_op jit(solution)/shard_map/ppermute | solution.py:416
  67.7 8.0 %collective-permute-start.11 = (f32[96,640]{1,0:T(8,128)S(1)}, f32[96,640]{1,0:T(8,128)S(1)}, u32[]{:S(2)}, u32[]{:S(2)}) collective-permute-start(f32[96,640]{1,0:T(8,128)S(1)} %slice.41.refs_2_), channel_id=1, source_target_pairs={{0,1},{1,0},{2,3},{3,2},{4,5},{5,4},{6,7},{7,6},{8,9},{9,8},{10,11... | collective-permute-start | bytes 737288 | tf_op jit(solution)/shard_map/ppermute | solution.py:471
  70.1 5.0 %collective-permute-start.15 = (f32[32,128]{1,0:T(8,128)S(1)}, f32[32,128]{1,0:T(8,128)S(1)}, u32[]{:S(2)}, u32[]{:S(2)}) collective-permute-start(f32[32,128]{1,0:T(8,128)S(1)} %slice_add_fusion), channel_id=1, source_target_pairs={{0,16},{8,24},{16,0},{24,8},{1,17},{9,25},{17,1},{25,9},{2,18},{10... | collective-permute-start | bytes 49160 | tf_op jit(solution)/shard_map/ppermute | solution.py:427
  73.3 3.4 %collective-permute-start.14 = (f32[128,128]{1,0:T(8,128)S(1)}, f32[128,128]{1,0:T(8,128)S(1)}, u32[]{:S(2)}, u32[]{:S(2)}) collective-permute-start(f32[128,128]{1,0:T(8,128)S(1)} %get-tuple-element.55.two_ref), channel_id=1, source_target_pairs={{8,16},{16,8},{9,17},{17,9},{10,18},{18,10},{11,19},{19,11},{12,20... | collective-permute-start | bytes 196616 | tf_op jit(solution)/shard_map/ppermute | solution.py:416

commit v2 on v1

--- a/solution.py
+++ b/solution.py
@@ -117,14 +117,15 @@
 def put_traces(place_ref, low, high, one_ref, two_ref):
     even = place_ref[4] == 0
     one_ref[0:LANES, :] = jnp.where(even, high, low)
-    two_ref[...] = jnp.where(even, low, high)
+    two_ref[0:LANES, :] = jnp.where(even, low, high)
 
 
 def face_rows(place_ref, lists_ref, one_ref, two_ref, near_one_ref, near_two_ref, slots, to_ref):
     gain = step_size * face_gain
     even = place_ref[4] == 0
     one = gain * (near_one_ref[0:LANES, :] - one_ref[0:LANES, :])
-    two = gain * (near_two_ref[...] - two_ref[...])
+    near_two = jnp.where(place_ref[5] > 0, near_two_ref[0:LANES, :], 0.0)
+    two = gain * (near_two - two_ref[0:LANES, :])
     to_ref[0:LANES, :] = pick(
         jnp.where(even, two, one), chosen_slots(lists_ref[0:1, :], slots), NT
     )
@@ -291,7 +292,8 @@
 def first_kernel(cap, major, minor, local, nodes, place_ref, owner_ref, top_ref, rest_ref, sum_ref, r_ref, mean_ref, *refs):
     states, refs = refs[:minor], refs[minor:]
     blocks, refs = refs[: major * minor], refs[major * minor :]
-    now_ref, fx_ref, more_ref, got_ref, a_ref = refs[:5]
+    face_outs, refs = refs[:major], refs[major:]
+    now_ref, more_ref, got_ref, a_ref, fx_ref = refs[:5]
     elems = owner_ref.shape[1]
     slots = cap * major * minor
     wide = now_ref.shape[0]
@@ -312,6 +314,10 @@
     add_faces(now_ref, fx_ref, fields, nodes)
     take_faces(now_ref, fx_ref, fields, nodes)
     fx_ref[LANES - 3 : LANES - 2, :] = jnp.ones((1, elems), F32)
+    sent = pick_back(chosen, fx_ref[...])
+    width = cap * minor
+    for k in range(major):
+        face_outs[k][...] = sent[k * width : (k + 1) * width, :]
     more_ref[...] = jnp.concatenate(
         [density, param, slot.astype(F32), jnp.zeros((5, elems), F32)], axis=0
     )
@@ -322,7 +328,7 @@
     return dot(chosen, top, NT) + dot(chosen, rest, NT)
 
 
-def second_kernel(cap, major, minor, local, nodes, place_ref, now_ref, faces_ref, more_ref, top_ref, rest_ref, sum_ref, r_ref, mean_ref, *refs):
+def second_kernel(cap, major, minor, local, nodes, place_ref, now_ref, more_ref, top_ref, rest_ref, sum_ref, r_ref, mean_ref, *refs):
     states, refs = refs[:minor], refs[minor:]
     outs, refs = refs[: major * minor], refs[major * minor :]
     t_ref = refs[0]
@@ -338,7 +344,6 @@
     rows = lax.broadcasted_iota(jnp.int32, (slots, elems), 0)
     chosen = (rows == slot).astype(F32).astype(BF16)
     sent = pick_back(chosen, t_ref[...])
-    sent_faces = pick_back(chosen, faces_ref[...])
     density = (more_ref[0:1, :] + density) * (1.0 / (fields * nodes))
     density = jnp.where(slot >= 0, density, 0.0)
     param = more_ref[1:2, :].astype(jnp.int32)
@@ -350,8 +355,7 @@
     grad = pick(jnp.where(in_high, density, 0.0), in_low, NT)
     for n, out in enumerate(outs):
         out[0:cap, 0:wide] = sent[n * cap : (n + 1) * cap, :]
-        out[0:cap, wide:] = sent_faces[n * cap : (n + 1) * cap, :]
-        out[cap : cap + RIDE, :] = jnp.zeros((RIDE, wide + 2 * LANES), F32)
+        out[cap : cap + RIDE, :] = jnp.zeros((RIDE, wide), F32)
         for m in range(4):
             out[cap : cap + RIDE, m * LANES : (m + 1) * LANES] = grad[m * RIDE : (m + 1) * RIDE, :]
 
@@ -380,15 +384,16 @@
     for m in range(4):
         rows = slice(m // 2 * RIDE, (m // 2 + 1) * RIDE)
         at = LANES + m * RIDE
-        one_ref[at : at + RIDE, :] = grad[rows, m % 2 * LANES : (m % 2 + 1) * LANES]
+        part = grad[rows, m % 2 * LANES : (m % 2 + 1) * LANES]
+        one_ref[at : at + RIDE, :] = part
+        two_ref[at : at + RIDE, :] = part
 
 
 def assemble_kernel(nodes, cap, major, minor, place_ref, base_ref, *refs):
-    count = major * minor
-    out_ref, got_ref = refs[count:]
-    for j in range(major):
-        for k in range(minor):
-            place_block(place_ref, got_ref, refs[j * minor + k][0:cap, :], cap, major, minor, j, k)
+    out_ref, got_ref = refs[minor:]
+    for k in range(minor):
+        for j in range(major):
+            place_block(place_ref, got_ref, refs[k][j * cap : (j + 1) * cap, :], cap, major, minor, j, k)
     turned = got_ref[...].T
     mine = turned[nodes : nodes + 1, :] > 0.5
     out_ref[...] = jnp.where(mine, turned, base_ref[...])
@@ -408,25 +413,23 @@
     return lax.optimization_barrier((value, *earlier))[0]
 
 
-def across(one, two):
+def across(one, two, ends):
     size = lax.axis_size("region")
     near = []
     for value, first in ((one, 0), (two, 1)):
         pairs = [(i, i + 1) for i in range(first, size - 1, 2)]
+        if ends and first and size == 4:
+            pairs = pairs + [(0, 3)]
         near.append(lax.ppermute(value, "region", pairs + [(j, i) for i, j in pairs]))
     return near
 
 
-def summed_on(value, near, axis):
-    size = lax.axis_size(axis)
-    if size & (size - 1):
-        return lax.psum(value, axis)
-    value = value + near
-    k = 2
-    while k < size:
-        value = value + lax.ppermute(value, axis, [(i, i ^ k) for i in range(size)])
-        k = 2 * k
-    return value
+def over_regions(value, near_one, near_two):
+    size = lax.axis_size("region")
+    if size == 4:
+        far = lax.ppermute(value, "region", [(i, i ^ 2) for i in range(size)])
+        return (value + near_one) + (near_two + far)
+    return lax.psum(value, "region")
 
 
 def per_device(stored, new_owner, adjoint, deriv, mixing, face_lists, param_map):
@@ -473,8 +476,10 @@
     dom = lax.axis_index("dom")
     seg = lax.axis_index("segment")
     region = lax.axis_index("region")
+    size = lax.axis_size("region")
+    second = 1 - ((region == 0) | ((region == size - 1) & (size % 2 == 0))).astype(jnp.int32)
     ty, tc = dom // minor, dom % minor
-    place = jnp.stack([ty, tc, seg, (tc == seg).astype(jnp.int32), region % 2]).astype(jnp.int32)
+    place = jnp.stack([ty, tc, seg, (tc == seg).astype(jnp.int32), region % 2, second]).astype(jnp.int32)
     owner = new_owner.reshape(1, elems)
     mapped = param_map.reshape(1, slots)
 
@@ -503,7 +508,7 @@
         [SMEM] + [VMEM] * 2,
         [pltpu.VMEM((2, LANES, slots), F32)],
     )(place, adjoint, face_lists)
-    near_low, near_high = across(low, high)
+    near_low, near_high = across(low, high, False)
     top, rest, total = call(
         operator_kernel,
         (shape(wide, wide, dtype=BF16), shape(wide, wide, dtype=BF16), shape(LANES, LANES)),
@@ -539,49 +544,57 @@
         pltpu.VMEM((wide, elems), F32),
         pltpu.VMEM((wide, elems), F32),
     ]
-    now, faces_now, more = call(
+    *face_parts, now, more = call(
         functools.partial(first_kernel, cap, major, minor, local, nodes),
-        (shape(wide, elems), shape(2 * LANES, elems), shape(8, elems)),
+        (shape(cap * minor, 2 * LANES),) * major + (shape(wide, elems), shape(8, elems)),
         [SMEM] + [VMEM] * (6 + minor + dom_count),
         [
             pltpu.VMEM((slots, sent), F32),
             pltpu.VMEM((wide, elems), F32),
+            pltpu.VMEM((2 * LANES, elems), F32),
         ]
         + work,
     )(place, owner, top, rest, total, *ready[0:2], *states[0], *blocks)
 
+    moved = [face_parts[0]] + [
+        move(face_parts[j], [(at(y, x, x), at((y + j) % major, x, x)) for y in ys for x in xs])
+        for j in range(1, major)
+    ]
     parts = call(
         functools.partial(second_kernel, cap, major, minor, local, nodes),
-        (shape(cap + RIDE, sent),) * dom_count,
-        [SMEM] + [VMEM] * (8 + minor),
+        (shape(cap + RIDE, wide),) * dom_count,
+        [SMEM] + [VMEM] * (7 + minor),
         [pltpu.VMEM((wide, elems), F32)] + work,
-    )(place, now, faces_now, more, top, rest, total, *ready[2:4], *states[1])
+        moved=4e7,
+    )(place, now, more, top, rest, total, *ready[2:4], *states[1])
+    moved[-1] = after(moved[-1], *parts)
+    joined = [
+        jnp.concatenate([part[k * cap : (k + 1) * cap] for part in moved]) for k in range(minor)
+    ]
+    faces_mine = joined[0]
+    for k in range(1, minor):
+        pairs = [(at(y, x, x), at(y, x + k, x)) for y in ys for x in xs]
+        faces_mine = faces_mine + move(joined[k], pairs)
     got = from_workers(parts)
-    last_blocks = []
-    for value in got[:1]:
-        mine = value[0:cap, 0:wide]
-        last_blocks = last_blocks + [mine] + [to_segment(mine, k) for k in range(1, minor)]
     grad = sum(value[cap:, 0 : 4 * LANES] for value in got)
-    mine = jnp.concatenate(
-        [value[0:cap, wide:] for value in got] + [grad[:, 0 : 2 * LANES], grad[:, 2 * LANES :]]
-    )
+    mine = jnp.concatenate([faces_mine, grad[:, 0 : 2 * LANES], grad[:, 2 * LANES :]])
     face_blocks = [mine] + [to_segment(mine, k) for k in range(1, minor)]
-    for value in got[1:]:
-        mine = after(value[0:cap, 0:wide], last_blocks[-1])
-        last_blocks = last_blocks + [mine] + [to_segment(mine, k) for k in range(1, minor)]
+    mine = jnp.concatenate([value[0:cap] for value in got])
+    last_blocks = [mine] + [to_segment(mine, k) for k in range(1, minor)]
+    face_blocks[-1] = after(face_blocks[-1], mine)
     low1, high1 = call(
         functools.partial(faces_kernel, cap, major, minor),
-        (shape(LANES + 4 * RIDE, faces), trace),
+        (shape(LANES + 4 * RIDE, faces),) * 2,
         [SMEM] + [VMEM] * (2 + minor),
         [pltpu.VMEM((slots, 2 * LANES), F32)],
     )(place, base_face, face_lists, *face_blocks)
-    near_low1, near_high1 = across(low1, high1)
-    grad = summed_on(low1[LANES:], near_low1[LANES:], "region")
+    near_low1, near_high1 = across(low1, high1, True)
+    grad = over_regions(low1[LANES:], near_low1[LANES:], near_high1[LANES:])
 
     assembled = call(
         functools.partial(assemble_kernel, nodes, cap, major, minor),
         shape(wide, slots),
-        [SMEM] + [VMEM] * (1 + dom_count),
+        [SMEM] + [VMEM] * (1 + minor),
         [pltpu.VMEM((slots, wide), F32)],
         moved=8e7,
     )(place, base, *last_blocks)

time: 79 us -> 79 us (level)
  waiting for transfers between devices: 19.8 us -> 17 us
  starting transfers between devices: 29.7 us -> 32.4 us
    ppermute x6 -> x8, starting transfers between devices: 13.7 us -> 17.3 us  [move(): return lax.ppermute(value, axes, pairs)]
    ppermute x1, waiting for transfers between devices: 1.16 us -> 4.63 us  [over_regions(): far = lax.ppermute(value, 'region', [(i, i ^ 2) for i in range(size)])]
    ppermute x1, starting transfers between devices: 3.15 us -> 0.01 us  [over_regions(): far = lax.ppermute(value, 'region', [(i, i ^ 2) for i in range(size)])]
    ppermute x2, waiting for transfers between devices: 3.23 us -> 0.83 us  [per_device(): lax.ppermute(own[step], axes, [(at(y, x, x + k), at(y, x, x)) for y in ys...]
    ppermute x4, waiting for transfers between devices: 3.88 us -> 1.57 us  [across(): lax.ppermute(value, 'region', pairs + [(j, i) for i, j in pairs])]
    ppermute x6 -> x8, waiting for transfers between devices: 6.25 us -> 4.06 us  [move(): return lax.ppermute(value, axes, pairs)]
    ppermute x4, starting transfers between devices: 7.99 us -> 10.2 us  [across(): lax.ppermute(value, 'region', pairs + [(j, i) for i, j in pairs])]
    ppermute x3 -> x2, waiting for transfers between devices: 5.25 us -> 5.95 us  [to_segment(): return lax.ppermute(value, 'segment', [(x, (x + k) % minor) for x in xs])]
  transfers between devices with their start and end apart: 16 -> 17, of which waited for: 6 -> 7; matrix products, arithmetic and copies ran while one was open for 1% -> 1% of each run, Pallas kernels for 22% -> 26%
where the time goes in v2:
time: 79 us; the launch traced here: 78.5 us
  starting transfers between devices  32.4 us (41%)
  Pallas kernels  24.4 us (31%)
  waiting for transfers between devices  17 us (22%)
  local copies, waits for them, and re-layouts  2.91 us (4%)
  between operations  1 us (1%)
    ppermute x8, starting transfers between devices, move(): return lax.ppermute(value, axes, pairs)  17.3 us
    ppermute x4, starting transfers between devices, across(): lax.ppermute(value, 'region', pairs + [(j, i) for i, j in pairs])  10.2 us
    ppermute x2, waiting for transfers between devices, to_segment(): return lax.ppermute(value, 'segment', [(x, (x + k) % minor) for x in xs])  5.95 us
    pallas_call x1, Pallas kernels, per_device(): call(functools.partial(first_kernel, cap, major, minor, local, nodes), (s...  5.4 us
    ppermute x1, waiting for transfers between devices, over_regions(): far = lax.ppermute(value, 'region', [(i, i ^ 2) for i in range(size)])  4.63 us
    pallas_call x1, Pallas kernels, per_device(): call(functools.partial(second_kernel, cap, major, minor, local, nodes), (...  4.12 us
    ppermute x8, waiting for transfers between devices, move(): return lax.ppermute(value, axes, pairs)  4.06 us
    pallas_call x1, Pallas kernels, per_device(): call(linear_kernel, (shape(wide, slots), shape(2 * LANES, slots)), [VMEM]...  3.52 us
  transfers between devices with their start and end apart: 17, of which 7 were waited for; matrix products, arithmetic and copies ran while one was open for 1% of the time, Pallas kernels for 26%

profile of v2, /device:TPU:0, one launch (start us, length us, event | category | flops | bytes accessed | tf_op | source)
XLA Modules:
  0.0 78.5 jit_solution(15021602663205910025)
XLA Ops:
  0.6 1.7 %copy-done.1 = f32[2,2,5,125,256]{4,1,3,2,0:T(2,128)S(1)} copy-done((f32[2,2,5,125,256]{4,1,3,2,0:T(2,128)S(1)}, f32[2,2,5,125,256]{4,1,3,2,0:T(2,128)}, u32[]{:S(2)}) %copy-start.1) | copy-done | bytes 2560024
  2.4 1.3 %shard_map.90 = (f32[1280,256]{1,0:T(8,128)}, f32[1280,256]{1,0:T(8,128)S(1)}) custom-call(f32[5000,128]{1,0:T(8,128)S(1)} %bitcast.14), custom_call_target="tpu_custom_call" | custom-call | flops 1000000 | bytes 10000 | tf_op jit(solution)/shard_map/pallas_call | solution.py:488
  3.6 1.4 %collective-permute-start.2 = (f32[1280,256]{1,0:T(8,128)}, f32[1280,256]{1,0:T(8,128)}, u32[]{:S(2)}, u32[]{:S(2)}) collective-permute-start(f32[1280,256]{1,0:T(8,128)} %get-tuple-element.38.refs_0_), channel_id=1, source_target_pairs={{1,0},{2,3},{5,4},{6,7},{9,8},{10,11},{13,12},{14,15},{17,16},{18,... | collective-permute-start | bytes 3932168 | tf_op jit(solution)/shard_map/ppermute | solution.py:496
  5.1 1.3 %collective-permute-start.6 = (f32[1280,256]{1,0:T(8,128)S(1)}, f32[1280,256]{1,0:T(8,128)}, u32[]{:S(2)}, u32[]{:S(2)}) collective-permute-start(f32[1280,256]{1,0:T(8,128)S(1)} %get-tuple-element.39.refs_1_.refs_0_), channel_id=1, source_target_pairs={{1,0},{2,3},{5,4},{6,7},{9,8},{10,11},{13,12},{14,15},{17,16},{18,... | collective-permute-start | bytes 3932168 | tf_op jit(solution)/shard_map/ppermute | solution.py:496
  6.4 0.1 stack.31.place_ref
  6.5 0.8 %shard_map.86 = (f32[128,128]{1,0:T(8,128)S(1)}, f32[128,128]{1,0:T(8,128)S(1)}) custom-call(s32[6]{0:T(128)S(1)} %stack.31.place_ref, f32[5,125,384]{2,1,0:T(8,128)S(1)} %copy-done, s32[2,128]{1,0:T(2,128)S(1)} %copy-done.3), custom_call_target="tpu_custom_call" | custom-call | flops 1000000 | bytes 10000 | tf_op jit(solution)/shard_map/pallas_call | solution.py:505
  7.3 3.1 %collective-permute-start = (f32[128,128]{1,0:T(8,128)S(1)}, f32[128,128]{1,0:T(8,128)S(1)}, u32[]{:S(2)}, u32[]{:S(2)}) collective-permute-start(f32[128,128]{1,0:T(8,128)S(1)} %get-tuple-element.31.one_ref), channel_id=1, source_target_pairs={{0,8},{16,24},{8,0},{24,16},{1,9},{17,25},{9,1},{25,17},{2,10},{18... | collective-permute-start | bytes 196616 | tf_op jit(solution)/shard_map/ppermute | solution.py:423
  10.4 0.7 collective-permute-start.1
  11.1 1.6 %collective-permute-done.near_one_ref = f32[128,128]{1,0:T(8,128)S(1)} collective-permute-done((f32[128,128]{1,0:T(8,128)S(1)}, f32[128,128]{1,0:T(8,128)S(1)}, u32[]{:S(2)}, u32[]{:S(2)}) %collective-permute-start) | collective-permute-done | bytes 65568 | tf_op jit(solution)/shard_map/ppermute | solution.py:423
  12.7 0.0 collective-permute-done.1.near_two_ref
  12.7 1.8 %shard_map.87 = (f32[96,896]{1,0:T(8,128)S(1)}, f32[96,896]{1,0:T(8,128)}, f32[256,384]{1,0:T(8,128)S(1)}) custom-call(s32[6]{0:T(128)S(1)} %stack.31.place_ref, f32[5,125,384]{2,1,0:T(8,128)S(1)} %copy-done, s32[1,384]{1,0:T(1,128)S(1)} %reshape.22.map_ref, s32[2,128]{1,0:T(2,128)S(1)} %copy-done.3, f32[128,128]{1,0:T(8,128)S(1)} %get-tuple-element.31.one_ref, ...), custom_call_target="tpu_custom_call" | custom-call | flops 1000000 | bytes 10000 | tf_op jit(solution)/shard_map/pallas_call | solution.py:525
  14.5 1.3 %collective-permute-start.5 = (f32[96,896]{1,0:T(8,128)}, f32[96,896]{1,0:T(8,128)S(1)}, u32[]{:S(2)}, u32[]{:S(2)}) collective-permute-start(f32[96,896]{1,0:T(8,128)} %get-tuple-element.43), channel_id=1, source_target_pairs={{6,0},{5,3},{2,4},{1,7},{14,8},{13,11},{10,12},{9,15},{22,16},{21,... | collective-permute-start | bytes 1032200 | tf_op jit(solution)/shard_map/ppermute | solution.py:451
  15.8 1.3 %collective-permute-start.3 = (f32[96,896]{1,0:T(8,128)S(1)}, f32[96,896]{1,0:T(8,128)}, u32[]{:S(2)}, u32[]{:S(2)}) collective-permute-start(f32[96,896]{1,0:T(8,128)S(1)} %get-tuple-element.42.refs_2_), channel_id=1, source_target_pairs={{2,0},{1,3},{6,4},{5,7},{10,8},{9,11},{14,12},{13,15},{18,16},{17,... | collective-permute-start | bytes 1032200 | tf_op jit(solution)/shard_map/ppermute | solution.py:451
  17.1 3.9 %collective-permute-start.4 = (f32[96,896]{1,0:T(8,128)}, f32[96,896]{1,0:T(8,128)}, u32[]{:S(2)}, u32[]{:S(2)}) collective-permute-start(f32[96,896]{1,0:T(8,128)} %get-tuple-element.43), channel_id=1, source_target_pairs={{4,0},{7,3},{0,4},{3,7},{12,8},{15,11},{8,12},{11,15},{20,16},{23,... | collective-permute-start | bytes 1032200 | tf_op jit(solution)/shard_map/ppermute | solution.py:451
  21.0 0.1 reshape.23.mixing_ref
  21.0 0.0 copy-start.2
  21.1 0.9 %copy-done.2 = f32[3,125,125]{2,1,0:T(8,128)S(1)} copy-done((f32[3,125,125]{2,1,0:T(8,128)S(1)}, f32[3,125,125]{2,1,0:T(8,128)}, u32[]{:S(2)}) %copy-start.2) | copy-done | bytes 187524
  22.0 1.2 %shard_map.88 = (bf16[640,640]{1,0:T(8,128)(2,1)S(1)}, bf16[640,640]{1,0:T(8,128)(2,1)S(1)}, f32[128,128]{1,0:T(8,128)S(1)}) custom-call(f32[3,125,125]{2,1,0:T(8,128)S(1)} %copy-done.2, f32[75]{0:T(128)S(1)} %reshape.23.mixing_ref), custom_call_target="tpu_custom_call" | custom-call | flops 1000000 | bytes 10000 | tf_op jit(solution)/shard_map/pallas_call | solution.py:512
  23.2 2.4 %shard_map.91 = (f32[256,256]{1,0:T(8,128)S(1)}, f32[640,256]{1,0:T(8,128)S(1)}, f32[256,256]{1,0:T(8,128)S(1)}, f32[640,256]{1,0:T(8,128)S(1)}) custom-call(s32[6]{0:T(128)S(1)} %stack.31.place_ref, f32[128,128]{1,0:T(8,128)S(1)} %get-tuple-element.37.sum_ref, f32[1280,256]{1,0:T(8,128)} %get-tuple-element.38.refs_0_, ...), custom_call_target="tpu_custom_call" | custom-call | flops 1000000 | bytes 10000 | tf_op jit(solution)/shard_map/pallas_call | solution.py:518
  25.6 0.0 copy-start.4
  25.6 3.5 %shard_map.89 = (f32[640,384]{1,0:T(8,128)S(1)}, f32[256,384]{1,0:T(8,128)S(1)}) custom-call(f32[5,125,384]{2,1,0:T(8,128)S(1)} %copy-done, f32[256,384]{1,0:T(8,128)S(1)} %get-tuple-element.33.f_ref, bf16[640,640]{1,0:T(8,128)(2,1)S(1)} %get-tuple-element.34.top_ref, bf16[640,640]{1,0:T(8,128)(2,1)S(1)} %get-tuple-element.35.rest_ref), custom_call_target="tpu_custom_call" | custom-call | flops 1000000 | bytes 10000 | tf_op jit(solution)/shard_map/pallas_call | solution.py:533
  29.2 0.0 collective-permute-done.3.refs_3_
  29.2 0.1 collective-permute-done.4.refs_4_
  29.3 5.4 %shard_map.92 = (f32[192,256]{1,0:T(8,128)S(1)}, f32[192,256]{1,0:T(8,128)S(1)}, f32[640,256]{1,0:T(8,128)S(1)}, f32[8,256]{1,0:T(8,128)S(1)}) custom-call(s32[6]{0:T(128)S(1)} %stack.31.place_ref, s32[1,256]{1,0:T(1,128)S(1)} %bitcast.15, bf16[640,640]{1,0:T(8,128)(2,1)S(1)} %get-tuple-element.34.top_ref, bf16[640,640]{1,0:T(8,128)(2,1)S(1)} %get-tuple-element.35.rest_ref, ...), custom_call_target="tpu_custom_call" | custom-call | flops 1000000 | bytes 10000 | tf_op jit(solution)/shard_map/pallas_call | solution.py:547
  34.7 2.4 %collective-permute-start.11 = (f32[192,256]{1,0:T(8,128)S(1)}, f32[192,256]{1,0:T(8,128)S(1)}, u32[]{:S(2)}, u32[]{:S(2)}) collective-permute-start(f32[192,256]{1,0:T(8,128)S(1)} %get-tuple-element.55), channel_id=1, source_target_pairs={{0,4},{3,7},{4,0},{7,3},{8,12},{11,15},{12,8},{15,11},{16,20},{19,... | collective-permute-start | bytes 589832 | tf_op jit(solution)/shard_map/ppermute | solution.py:451
  37.1 0.8 %collective-permute-done.6.refs_1_ = f32[1280,256]{1,0:T(8,128)} collective-permute-done((f32[1280,256]{1,0:T(8,128)S(1)}, f32[1280,256]{1,0:T(8,128)}, u32[]{:S(2)}, u32[]{:S(2)}) %collective-permute-start.6) | collective-permute-done | bytes 1310752 | tf_op jit(solution)/shard_map/ppermute | solution.py:496
  37.9 4.1 %shard_map.93 = (f32[104,640]{1,0:T(8,128)S(1)}, f32[104,640]{1,0:T(8,128)S(1)}, f32[104,640]{1,0:T(8,128)S(1)}, f32[104,640]{1,0:T(8,128)S(1)}) custom-call(s32[6]{0:T(128)S(1)} %stack.31.place_ref, f32[640,256]{1,0:T(8,128)S(1)} %get-tuple-element.46.now_ref, f32[8,256]{1,0:T(8,128)S(1)} %get-tuple-element.47.more_ref, ...), custom_call_target="tpu_custom_call" | custom-call | flops 1000000 | bytes 40000000 | tf_op jit(solution)/shard_map/pallas_call | solution.py:563
  42.0 1.3 %collective-permute-start.7 = (f32[104,640]{1,0:T(8,128)S(1)}, f32[104,640]{1,0:T(8,128)S(1)}, u32[]{:S(2)}, u32[]{:S(2)}) collective-permute-start(f32[104,640]{1,0:T(8,128)S(1)} %get-tuple-element.51), channel_id=1, source_target_pairs={{0,2},{3,1},{4,6},{7,5},{8,10},{11,9},{12,14},{15,13},{16,18},{19,... | collective-permute-start | bytes 798728 | tf_op jit(solution)/shard_map/ppermute | solution.py:451
  43.4 4.6 %collective-permute-start.8 = (f32[104,640]{1,0:T(8,128)S(1)}, f32[104,640]{1,0:T(8,128)S(1)}, u32[]{:S(2)}, u32[]{:S(2)}) collective-permute-start(f32[104,640]{1,0:T(8,128)S(1)} %get-tuple-element.52), channel_id=1, source_target_pairs={{0,4},{3,7},{4,0},{7,3},{8,12},{11,15},{12,8},{15,11},{16,20},{19,... | collective-permute-start | bytes 798728 | tf_op jit(solution)/shard_map/ppermute | solution.py:451
  47.9 1.3 %collective-permute-start.9 = (f32[104,640]{1,0:T(8,128)S(1)}, f32[104,640]{1,0:T(8,128)S(1)}, u32[]{:S(2)}, u32[]{:S(2)}) collective-permute-start(f32[104,640]{1,0:T(8,128)S(1)} %get-tuple-element.53), channel_id=1, source_target_pairs={{0,6},{3,5},{4,2},{7,1},{8,14},{11,13},{12,10},{15,9},{16,22},{19,... | collective-permute-start | bytes 798728 | tf_op jit(solution)/shard_map/ppermute | solution.py:451
  49.3 0.0 collective-permute-done.11
  49.3 1.3 %collective-permute-start.12 = (f32[192,256]{1,0:T(8,128)S(1)}, f32[192,256]{1,0:T(8,128)S(1)}, u32[]{:S(2)}, u32[]{:S(2)}) collective-permute-start(f32[192,256]{1,0:T(8,128)S(1)} %pad_maximum_fusion.2), channel_id=1, source_target_pairs={{0,2},{3,1},{4,6},{7,5},{8,10},{11,9},{12,14},{15,13},{16,18},{19,... | collective-permute-start | bytes 589832 | tf_op jit(solution)/shard_map/ppermute | solution.py:451
  50.6 0.0 collective-permute-done.7
  50.7 1.6 %collective-permute-done.8 = f32[104,640]{1,0:T(8,128)S(1)} collective-permute-done((f32[104,640]{1,0:T(8,128)S(1)}, f32[104,640]{1,0:T(8,128)S(1)}, u32[]{:S(2)}, u32[]{:S(2)}) %collective-permute-start.8) | collective-permute-done | bytes 266272 | tf_op jit(solution)/shard_map/ppermute | solution.py:451
  52.3 2.4 %collective-permute-done.9 = f32[104,640]{1,0:T(8,128)S(1)} collective-permute-done((f32[104,640]{1,0:T(8,128)S(1)}, f32[104,640]{1,0:T(8,128)S(1)}, u32[]{:S(2)}, u32[]{:S(2)}) %collective-permute-start.9) | collective-permute-done | bytes 266272 | tf_op jit(solution)/shard_map/ppermute | solution.py:451
  54.8 0.0 collective-permute-done.12
  54.9 0.7 collective-permute-start.13
  55.6 1.4 %collective-permute-start.10 = (f32[192,640]{1,0:T(8,128)S(1)}, f32[192,640]{1,0:T(8,128)S(1)}, u32[]{:S(2)}, u32[]{:S(2)}) collective-permute-start(f32[192,640]{1,0:T(8,128)S(1)} %pad_maximum_fusion.refs_0_), channel_id=1, source_target_pairs={{0,1},{1,0},{2,3},{3,2},{4,5},{5,4},{6,7},{7,6},{8,9},{9,8},{10,11... | collective-permute-start | bytes 1474568 | tf_op jit(solution)/shard_map/ppermute | solution.py:474
  57.0 5.9 %collective-permute-done.13.refs_1_ = f32[208,256]{1,0:T(8,128)S(1)} collective-permute-done((f32[208,256]{1,0:T(8,128)S(1)}, f32[208,256]{1,0:T(8,128)S(1)}, u32[]{:S(2)}, u32[]{:S(2)}) %collective-permute-start.13) | collective-permute-done | bytes 213024 | tf_op jit(solution)/shard_map/ppermute | solution.py:474
  63.0 1.0 %shard_map.95 = (f32[160,128]{1,0:T(8,128)S(1)}, f32[160,128]{1,0:T(8,128)S(1)}) custom-call(s32[6]{0:T(128)S(1)} %stack.31.place_ref, f32[256,384]{1,0:T(8,128)S(1)} %get-tuple-element.44.base_ref, s32[2,128]{1,0:T(2,128)S(1)} %copy-done.3, f32[208,256]{1,0:T(8,128)S(1)} %pad_maximum_fusion.1.refs_0_, f32[208,256]{1,0:T(8,128)S(1)} %collective-permute-done.13.refs_1_), custom_call_target="tpu_custom_call" | custom-call | flops 1000000 | bytes 10000 | tf_op jit(solution)/shard_map/pallas_call | solution.py:585
  64.0 3.5 %collective-permute-start.14 = (f32[160,128]{1,0:T(8,128)S(1)}, f32[160,128]{1,0:T(8,128)S(1)}, u32[]{:S(2)}, u32[]{:S(2)}) collective-permute-start(f32[160,128]{1,0:T(8,128)S(1)} %get-tuple-element.58.one_ref), channel_id=1, source_target_pairs={{0,8},{16,24},{8,0},{24,16},{1,9},{17,25},{9,1},{25,17},{2,10},{18... | collective-permute-start | bytes 245768 | tf_op jit(solution)/shard_map/ppermute | solution.py:423
  67.4 3.0 %collective-permute-start.15 = (f32[160,128]{1,0:T(8,128)S(1)}, f32[160,128]{1,0:T(8,128)S(1)}, u32[]{:S(2)}, u32[]{:S(2)}) collective-permute-start(f32[160,128]{1,0:T(8,128)S(1)} %get-tuple-element.59.two_ref), channel_id=1, source_target_pairs={{8,16},{0,24},{16,8},{24,0},{9,17},{1,25},{17,9},{25,1},{10,18},{2... | collective-permute-start | bytes 245768 | tf_op jit(solution)/shard_map/ppermute | solution.py:423
  70.4 0.0 collective-permute-start.16
  70.4 4.6 %collective-permute-done.16 = f32[32,128]{1,0:T(8,128)S(1)} collective-permute-done((f32[32,128]{1,0:T(8,128)S(1)}, f32[32,128]{1,0:T(8,128)S(1)}, u32[]{:S(2)}, u32[]{:S(2)}) %collective-permute-start.16) | collective-permute-done | bytes 16416 | tf_op jit(solution)/shard_map/ppermute | solution.py:430
  75.0 0.0 collective-permute-done.14.near_one_ref
  75.0 0.6 fusion.1
  75.6 1.0 %shard_map.94.now_ref = f32[640,384]{1,0:T(8,128)S(1)} custom-call(s32[6]{0:T(128)S(1)} %stack.31.place_ref, f32[640,384]{1,0:T(8,128)S(1)} %get-tuple-element.36.base_ref, f32[192,640]{1,0:T(8,128)S(1)} %pad_maximum_fusion.refs_0_, f32[192,640]{1,0:T(8,128)S(1)} %collective-permute-done.10.refs_1_), custom_call_target="tpu_custom_call" | custom-call | flops 1000000 | bytes 80000000 | tf_op jit(solution)/shard_map/pallas_call | solution.py:594
  76.6 1.8 %shard_map.96 = f32[5,125,384]{2,1,0:T(8,128)} custom-call(s32[6]{0:T(128)S(1)} %stack.31.place_ref, f32[640,384]{1,0:T(8,128)S(1)} %shard_map.94.now_ref, s32[2,128]{1,0:T(2,128)S(1)} %copy-done.3, f32[160,128]{1,0:T(8,128)S(1)} %get-tuple-element.58.one_ref, f32[160,128]{1,0:T(8,128)S(1)} %get-tuple-element.59.two_ref, ...), custom_call_target="tpu_custom_call" | custom-call | flops 1000000 | bytes 10000 | tf_op jit(solution)/shard_map/pallas_call | solution.py:601
  (29 shorter events, 0.3 us)
Async XLA Ops:
  0.6 1.7 %copy-start.1 = (f32[2,2,5,125,256]{4,1,3,2,0:T(2,128)S(1)}, f32[2,2,5,125,256]{4,1,3,2,0:T(2,128)}, u32[]{:S(2)}) copy-start(f32[2,2,5,125,256]{4,1,3,2,0:T(2,128)} %param.7) | copy-start | bytes 7680004
  2.4 4.1 %copy-start = (f32[5,125,384]{2,1,0:T(8,128)S(1)}, f32[5,125,384]{2,1,0:T(8,128)}, u32[]{:S(2)}) copy-start(f32[5,125,384]{2,1,0:T(8,128)} %a_in_ref.1) | copy-start | bytes 2880004
  2.4 4.1 %copy-start.3 = (s32[2,128]{1,0:T(2,128)S(1)}, s32[2,128]{1,0:T(2,128)}, u32[]{:S(2)}) copy-start(s32[2,128]{1,0:T(2,128)} %lists_ref.7) | copy-start | bytes 3076
  2.4 8.7 %copy-start.6 = (s32[384]{0:T(512)S(1)}, s32[384]{0:T(512)}, u32[]{:S(2)}) copy-start(s32[384]{0:T(512)} %param.13) | copy-start | bytes 4612
  3.6 17.3 %copy-start.5 = (f32[3,5,5]{2,0,1:T(4,128)S(1)}, f32[3,5,5]{2,0,1:T(4,128)}, u32[]{:S(2)}) copy-start(f32[3,5,5]{2,0,1:T(4,128)} %param.11) | copy-start | bytes 904
  3.6 25.6 %collective-permute-start.2 = (f32[1280,256]{1,0:T(8,128)}, f32[1280,256]{1,0:T(8,128)}, u32[]{:S(2)}, u32[]{:S(2)}) collective-permute-start(f32[1280,256]{1,0:T(8,128)} %get-tuple-element.38.refs_0_), channel_id=1, source_target_pairs={{1,0},{2,3},{5,4},{6,7},{9,8},{10,11},{13,12},{14,15},{17,16},{18,... | collective-permute-start | bytes 3932168 | tf_op jit(solution)/shard_map/ppermute | solution.py:496
  5.1 32.9 %collective-permute-start.6 = (f32[1280,256]{1,0:T(8,128)S(1)}, f32[1280,256]{1,0:T(8,128)}, u32[]{:S(2)}, u32[]{:S(2)}) collective-permute-start(f32[1280,256]{1,0:T(8,128)S(1)} %get-tuple-element.39.refs_1_.refs_0_), channel_id=1, source_target_pairs={{1,0},{2,3},{5,4},{6,7},{9,8},{10,11},{13,12},{14,15},{17,16},{18,... | collective-permute-start | bytes 3932168 | tf_op jit(solution)/shard_map/ppermute | solution.py:496
  7.3 5.3 %collective-permute-start = (f32[128,128]{1,0:T(8,128)S(1)}, f32[128,128]{1,0:T(8,128)S(1)}, u32[]{:S(2)}, u32[]{:S(2)}) collective-permute-start(f32[128,128]{1,0:T(8,128)S(1)} %get-tuple-element.31.one_ref), channel_id=1, source_target_pairs={{0,8},{16,24},{8,0},{24,16},{1,9},{17,25},{9,1},{25,17},{2,10},{18... | collective-permute-start | bytes 196616 | tf_op jit(solution)/shard_map/ppermute | solution.py:423
  10.4 2.2 %collective-permute-start.1 = (f32[128,128]{1,0:T(8,128)S(1)}, f32[128,128]{1,0:T(8,128)S(1)}, u32[]{:S(2)}, u32[]{:S(2)}) collective-permute-start(f32[128,128]{1,0:T(8,128)S(1)} %get-tuple-element.32.two_ref), channel_id=1, source_target_pairs={{8,16},{16,8},{9,17},{17,9},{10,18},{18,10},{11,19},{19,11},{12,20... | collective-permute-start | bytes 196616 | tf_op jit(solution)/shard_map/ppermute | solution.py:423
  14.5 14.7 %collective-permute-start.5 = (f32[96,896]{1,0:T(8,128)}, f32[96,896]{1,0:T(8,128)S(1)}, u32[]{:S(2)}, u32[]{:S(2)}) collective-permute-start(f32[96,896]{1,0:T(8,128)} %get-tuple-element.43), channel_id=1, source_target_pairs={{6,0},{5,3},{2,4},{1,7},{14,8},{13,11},{10,12},{9,15},{22,16},{21,... | collective-permute-start | bytes 1032200 | tf_op jit(solution)/shard_map/ppermute | solution.py:451
  15.8 13.4 %collective-permute-start.3 = (f32[96,896]{1,0:T(8,128)S(1)}, f32[96,896]{1,0:T(8,128)}, u32[]{:S(2)}, u32[]{:S(2)}) collective-permute-start(f32[96,896]{1,0:T(8,128)S(1)} %get-tuple-element.42.refs_2_), channel_id=1, source_target_pairs={{2,0},{1,3},{6,4},{5,7},{10,8},{9,11},{14,12},{13,15},{18,16},{17,... | collective-permute-start | bytes 1032200 | tf_op jit(solution)/shard_map/ppermute | solution.py:451
  17.1 12.2 %collective-permute-start.4 = (f32[96,896]{1,0:T(8,128)}, f32[96,896]{1,0:T(8,128)}, u32[]{:S(2)}, u32[]{:S(2)}) collective-permute-start(f32[96,896]{1,0:T(8,128)} %get-tuple-element.43), channel_id=1, source_target_pairs={{4,0},{7,3},{0,4},{3,7},{12,8},{15,11},{8,12},{11,15},{20,16},{23,... | collective-permute-start | bytes 1032200 | tf_op jit(solution)/shard_map/ppermute | solution.py:451
  21.0 0.9 %copy-start.2 = (f32[3,125,125]{2,1,0:T(8,128)S(1)}, f32[3,125,125]{2,1,0:T(8,128)}, u32[]{:S(2)}) copy-start(f32[3,125,125]{2,1,0:T(8,128)} %deriv_ref.1) | copy-start | bytes 562504
  25.6 3.6 %copy-start.4 = (s32[256,1]{0,1:T(1,128)S(1)}, s32[256,1]{0,1:T(1,128)}, u32[]{:S(2)}) copy-start(s32[256,1]{0,1:T(1,128)} %param.8) | copy-start | bytes 3076
  34.7 14.6 %collective-permute-start.11 = (f32[192,256]{1,0:T(8,128)S(1)}, f32[192,256]{1,0:T(8,128)S(1)}, u32[]{:S(2)}, u32[]{:S(2)}) collective-permute-start(f32[192,256]{1,0:T(8,128)S(1)} %get-tuple-element.55), channel_id=1, source_target_pairs={{0,4},{3,7},{4,0},{7,3},{8,12},{11,15},{12,8},{15,11},{16,20},{19,... | collective-permute-start | bytes 589832 | tf_op jit(solution)/shard_map/ppermute | solution.py:451
  42.0 8.6 %collective-permute-start.7 = (f32[104,640]{1,0:T(8,128)S(1)}, f32[104,640]{1,0:T(8,128)S(1)}, u32[]{:S(2)}, u32[]{:S(2)}) collective-permute-start(f32[104,640]{1,0:T(8,128)S(1)} %get-tuple-element.51), channel_id=1, source_target_pairs={{0,2},{3,1},{4,6},{7,5},{8,10},{11,9},{12,14},{15,13},{16,18},{19,... | collective-permute-start | bytes 798728 | tf_op jit(solution)/shard_map/ppermute | solution.py:451
  43.4 9.0 %collective-permute-start.8 = (f32[104,640]{1,0:T(8,128)S(1)}, f32[104,640]{1,0:T(8,128)S(1)}, u32[]{:S(2)}, u32[]{:S(2)}) collective-permute-start(f32[104,640]{1,0:T(8,128)S(1)} %get-tuple-element.52), channel_id=1, source_target_pairs={{0,4},{3,7},{4,0},{7,3},{8,12},{11,15},{12,8},{15,11},{16,20},{19,... | collective-permute-start | bytes 798728 | tf_op jit(solution)/shard_map/ppermute | solution.py:451
  47.9 6.8 %collective-permute-start.9 = (f32[104,640]{1,0:T(8,128)S(1)}, f32[104,640]{1,0:T(8,128)S(1)}, u32[]{:S(2)}, u32[]{:S(2)}) collective-permute-start(f32[104,640]{1,0:T(8,128)S(1)} %get-tuple-element.53), channel_id=1, source_target_pairs={{0,6},{3,5},{4,2},{7,1},{8,14},{11,13},{12,10},{15,9},{16,22},{19,... | collective-permute-start | bytes 798728 | tf_op jit(solution)/shard_map/ppermute | solution.py:451
  49.3 5.5 %collective-permute-start.12 = (f32[192,256]{1,0:T(8,128)S(1)}, f32[192,256]{1,0:T(8,128)S(1)}, u32[]{:S(2)}, u32[]{:S(2)}) collective-permute-start(f32[192,256]{1,0:T(8,128)S(1)} %pad_maximum_fusion.2), channel_id=1, source_target_pairs={{0,2},{3,1},{4,6},{7,5},{8,10},{11,9},{12,14},{15,13},{16,18},{19,... | collective-permute-start | bytes 589832 | tf_op jit(solution)/shard_map/ppermute | solution.py:451
  54.9 8.1 %collective-permute-start.13 = (f32[208,256]{1,0:T(8,128)S(1)}, f32[208,256]{1,0:T(8,128)S(1)}, u32[]{:S(2)}, u32[]{:S(2)}) collective-permute-start(f32[208,256]{1,0:T(8,128)S(1)} %pad_maximum_fusion.1.refs_0_), channel_id=1, source_target_pairs={{0,1},{1,0},{2,3},{3,2},{4,5},{5,4},{6,7},{7,6},{8,9},{9,8},{10,11... | collective-permute-start | bytes 638984 | tf_op jit(solution)/shard_map/ppermute | solution.py:474
  55.6 20.0 %collective-permute-start.10 = (f32[192,640]{1,0:T(8,128)S(1)}, f32[192,640]{1,0:T(8,128)S(1)}, u32[]{:S(2)}, u32[]{:S(2)}) collective-permute-start(f32[192,640]{1,0:T(8,128)S(1)} %pad_maximum_fusion.refs_0_), channel_id=1, source_target_pairs={{0,1},{1,0},{2,3},{3,2},{4,5},{5,4},{6,7},{7,6},{8,9},{9,8},{10,11... | collective-permute-start | bytes 1474568 | tf_op jit(solution)/shard_map/ppermute | solution.py:474
  64.0 11.1 %collective-permute-start.14 = (f32[160,128]{1,0:T(8,128)S(1)}, f32[160,128]{1,0:T(8,128)S(1)}, u32[]{:S(2)}, u32[]{:S(2)}) collective-permute-start(f32[160,128]{1,0:T(8,128)S(1)} %get-tuple-element.58.one_ref), channel_id=1, source_target_pairs={{0,8},{16,24},{8,0},{24,16},{1,9},{17,25},{9,1},{25,17},{2,10},{18... | collective-permute-start | bytes 245768 | tf_op jit(solution)/shard_map/ppermute | solution.py:423
  67.4 7.6 %collective-permute-start.15 = (f32[160,128]{1,0:T(8,128)S(1)}, f32[160,128]{1,0:T(8,128)S(1)}, u32[]{:S(2)}, u32[]{:S(2)}) collective-permute-start(f32[160,128]{1,0:T(8,128)S(1)} %get-tuple-element.59.two_ref), channel_id=1, source_target_pairs={{8,16},{0,24},{16,8},{24,0},{9,17},{1,25},{17,9},{25,1},{10,18},{2... | collective-permute-start | bytes 245768 | tf_op jit(solution)/shard_map/ppermute | solution.py:423
  70.4 4.6 %collective-permute-start.16 = (f32[32,128]{1,0:T(8,128)S(1)}, f32[32,128]{1,0:T(8,128)S(1)}, u32[]{:S(2)}, u32[]{:S(2)}) collective-permute-start(f32[32,128]{1,0:T(8,128)S(1)} %slice.49), channel_id=1, source_target_pairs={{0,16},{8,24},{16,0},{24,8},{1,17},{9,25},{17,1},{25,9},{2,18},{10... | collective-permute-start | bytes 49160 | tf_op jit(solution)/shard_map/ppermute | solution.py:430

commit v3 on v2

--- a/solution.py
+++ b/solution.py
@@ -171,7 +171,7 @@
             rest_ref[f * LANES : (f + 1) * LANES, g * LANES : (g + 1) * LANES] = rest
 
 
-def linear_kernel(a_in_ref, f_ref, top_ref, rest_ref, base_ref, face_ref, now_ref, x_ref):
+def linear_kernel(a_in_ref, f_ref, top_ref, rest_ref, now_ref, face_ref, x_ref):
     fields, nodes, _ = a_in_ref.shape
     x_ref[...] = jnp.zeros_like(x_ref)
     for f in range(fields):
@@ -181,8 +181,11 @@
     now_ref[...] = x + step_size * product(op, x)
     add_faces(now_ref, f_ref, fields, nodes)
     take_faces(now_ref, face_ref, fields, nodes)
+
+
+def again_kernel(now_ref, top_ref, rest_ref, base_ref):
     now = now_ref[...]
-    base_ref[...] = now + step_size * product(op, now)
+    base_ref[...] = now + step_size * product((top_ref[...], rest_ref[...]), now)
 
 
 def add_faces(to_ref, face_ref, fields, nodes):
@@ -530,13 +533,13 @@
     )(place, adjoint, mapped, face_lists, low, high, near_low, near_high)
     blocks = to_workers(a_out)
 
-    base, base_face = call(
+    base_once, base_face = call(
         linear_kernel,
         (shape(wide, slots), shape(2 * LANES, slots)),
         [VMEM] * 4,
-        [pltpu.VMEM((wide, slots), F32), pltpu.VMEM((wide, slots), F32)],
+        [pltpu.VMEM((wide, slots), F32)],
     )(adjoint, f0, top, rest)
-    blocks[-1] = after(blocks[-1], base, base_face)
+    blocks[-1] = after(blocks[-1], base_once, base_face)
 
     work = [
         pltpu.VMEM((local * LANES, elems), F32),
@@ -581,7 +584,8 @@
     face_blocks = [mine] + [to_segment(mine, k) for k in range(1, minor)]
     mine = jnp.concatenate([value[0:cap] for value in got])
     last_blocks = [mine] + [to_segment(mine, k) for k in range(1, minor)]
-    face_blocks[-1] = after(face_blocks[-1], mine)
+    base = call(again_kernel, shape(wide, slots), [VMEM] * 3)(after(base_once, mine), top, rest)
+    face_blocks[-1] = after(face_blocks[-1], mine, base)
     low1, high1 = call(
         functools.partial(faces_kernel, cap, major, minor),
         (shape(LANES + 4 * RIDE, faces),) * 2,

time: 79 us -> 77.9 us (0.986)
  starting transfers between devices: 32.4 us -> 31.5 us
    pallas_call x1, Pallas kernels: 3.52 us -> 1.67 us  [per_device(): call(linear_kernel, (shape(wide, slots), shape(2 * LANES, slots)), [VMEM]...]
    ppermute x8, waiting for transfers between devices: 4.06 us -> 5.74 us  [move(): return lax.ppermute(value, axes, pairs)]
    ppermute x2, waiting for transfers between devices: 5.95 us -> 4.38 us  [to_segment(): return lax.ppermute(value, 'segment', [(x, (x + k) % minor) for x in xs])]
    pallas_call x0 -> x1, Pallas kernels: none -> 1.56 us  [per_device(): call(again_kernel, shape(wide, slots), [VMEM] * 3)]
    ppermute x4, starting transfers between devices: 10.2 us -> 9.11 us  [across(): lax.ppermute(value, 'region', pairs + [(j, i) for i, j in pairs])]
  transfers between devices with their start and end apart: 17 -> 17, of which waited for: 7 -> 8; matrix products, arithmetic and copies ran while one was open for 1% -> 1% of each run, Pallas kernels for 26% -> 26%
where the time goes in v3:
time: 77.9 us; the launch traced here: 77.4 us
  starting transfers between devices  31.5 us (40%)
  Pallas kernels  24.1 us (31%)
  waiting for transfers between devices  17.2 us (22%)
  local copies, waits for them, and re-layouts  2.91 us (4%)
  between operations  0.99 us (1%)
  other arithmetic  0.79 us (1%)
    ppermute x8, starting transfers between devices, move(): return lax.ppermute(value, axes, pairs)  17.5 us
    ppermute x4, starting transfers between devices, across(): lax.ppermute(value, 'region', pairs + [(j, i) for i, j in pairs])  9.11 us
    ppermute x8, waiting for transfers between devices, move(): return lax.ppermute(value, axes, pairs)  5.74 us
    pallas_call x1, Pallas kernels, per_device(): call(functools.partial(first_kernel, cap, major, minor, local, nodes), (s...  5.4 us
    ppermute x1, waiting for transfers between devices, over_regions(): far = lax.ppermute(value, 'region', [(i, i ^ 2) for i in range(size)])  4.63 us
    ppermute x2, waiting for transfers between devices, to_segment(): return lax.ppermute(value, 'segment', [(x, (x + k) % minor) for x in xs])  4.38 us
    pallas_call x1, Pallas kernels, per_device(): call(functools.partial(second_kernel, cap, major, minor, local, nodes), (...  4.11 us
    ppermute x2, starting transfers between devices, per_device(): lax.ppermute(own[step], axes, [(at(y, x, x + k), at(y, x, x)) for y in ys...  2.7 us
  transfers between devices with their start and end apart: 17, of which 8 were waited for; matrix products, arithmetic and copies ran while one was open for 1% of the time, Pallas kernels for 26%

profile of v3, /device:TPU:0, one launch (start us, length us, event | category | flops | bytes accessed | tf_op | source)
XLA Modules:
  0.0 77.4 jit_solution(12837459568039580341)
XLA Ops:
  0.6 1.7 %copy-done.1 = f32[2,2,5,125,256]{4,1,3,2,0:T(2,128)S(1)} copy-done((f32[2,2,5,125,256]{4,1,3,2,0:T(2,128)S(1)}, f32[2,2,5,125,256]{4,1,3,2,0:T(2,128)}, u32[]{:S(2)}) %copy-start.1) | copy-done | bytes 2560024
  2.4 1.3 %shard_map.90 = (f32[1280,256]{1,0:T(8,128)}, f32[1280,256]{1,0:T(8,128)S(1)}) custom-call(f32[5000,128]{1,0:T(8,128)S(1)} %bitcast.14), custom_call_target="tpu_custom_call" | custom-call | flops 1000000 | bytes 10000 | tf_op jit(solution)/shard_map/pallas_call | solution.py:491
  3.6 1.4 %collective-permute-start.2 = (f32[1280,256]{1,0:T(8,128)}, f32[1280,256]{1,0:T(8,128)}, u32[]{:S(2)}, u32[]{:S(2)}) collective-permute-start(f32[1280,256]{1,0:T(8,128)} %get-tuple-element.39.refs_0_), channel_id=1, source_target_pairs={{1,0},{2,3},{5,4},{6,7},{9,8},{10,11},{13,12},{14,15},{17,16},{18,... | collective-permute-start | bytes 3932168 | tf_op jit(solution)/shard_map/ppermute | solution.py:499
  5.1 1.3 %collective-permute-start.6 = (f32[1280,256]{1,0:T(8,128)S(1)}, f32[1280,256]{1,0:T(8,128)}, u32[]{:S(2)}, u32[]{:S(2)}) collective-permute-start(f32[1280,256]{1,0:T(8,128)S(1)} %get-tuple-element.40.refs_1_.refs_0_), channel_id=1, source_target_pairs={{1,0},{2,3},{5,4},{6,7},{9,8},{10,11},{13,12},{14,15},{17,16},{18,... | collective-permute-start | bytes 3932168 | tf_op jit(solution)/shard_map/ppermute | solution.py:499
  6.4 0.1 stack.31.place_ref
  6.5 0.8 %shard_map.86 = (f32[128,128]{1,0:T(8,128)S(1)}, f32[128,128]{1,0:T(8,128)S(1)}) custom-call(s32[6]{0:T(128)S(1)} %stack.31.place_ref, f32[5,125,384]{2,1,0:T(8,128)S(1)} %copy-done, s32[2,128]{1,0:T(2,128)S(1)} %copy-done.3), custom_call_target="tpu_custom_call" | custom-call | flops 1000000 | bytes 10000 | tf_op jit(solution)/shard_map/pallas_call | solution.py:508
  7.3 3.1 %collective-permute-start = (f32[128,128]{1,0:T(8,128)S(1)}, f32[128,128]{1,0:T(8,128)S(1)}, u32[]{:S(2)}, u32[]{:S(2)}) collective-permute-start(f32[128,128]{1,0:T(8,128)S(1)} %get-tuple-element.32.one_ref), channel_id=1, source_target_pairs={{0,8},{16,24},{8,0},{24,16},{1,9},{17,25},{9,1},{25,17},{2,10},{18... | collective-permute-start | bytes 196616 | tf_op jit(solution)/shard_map/ppermute | solution.py:426
  10.4 0.7 collective-permute-start.1
  11.1 1.6 %collective-permute-done.near_one_ref = f32[128,128]{1,0:T(8,128)S(1)} collective-permute-done((f32[128,128]{1,0:T(8,128)S(1)}, f32[128,128]{1,0:T(8,128)S(1)}, u32[]{:S(2)}, u32[]{:S(2)}) %collective-permute-start) | collective-permute-done | bytes 65568 | tf_op jit(solution)/shard_map/ppermute | solution.py:426
  12.7 0.0 collective-permute-done.1.near_two_ref
  12.7 1.8 %shard_map.87 = (f32[96,896]{1,0:T(8,128)S(1)}, f32[96,896]{1,0:T(8,128)}, f32[256,384]{1,0:T(8,128)S(1)}) custom-call(s32[6]{0:T(128)S(1)} %stack.31.place_ref, f32[5,125,384]{2,1,0:T(8,128)S(1)} %copy-done, s32[1,384]{1,0:T(1,128)S(1)} %reshape.22.map_ref, s32[2,128]{1,0:T(2,128)S(1)} %copy-done.3, f32[128,128]{1,0:T(8,128)S(1)} %get-tuple-element.32.one_ref, ...), custom_call_target="tpu_custom_call" | custom-call | flops 1000000 | bytes 10000 | tf_op jit(solution)/shard_map/pallas_call | solution.py:528
  14.5 1.3 %collective-permute-start.5 = (f32[96,896]{1,0:T(8,128)}, f32[96,896]{1,0:T(8,128)S(1)}, u32[]{:S(2)}, u32[]{:S(2)}) collective-permute-start(f32[96,896]{1,0:T(8,128)} %get-tuple-element.44), channel_id=1, source_target_pairs={{6,0},{5,3},{2,4},{1,7},{14,8},{13,11},{10,12},{9,15},{22,16},{21,... | collective-permute-start | bytes 1032200 | tf_op jit(solution)/shard_map/ppermute | solution.py:454
  15.8 1.3 %collective-permute-start.3 = (f32[96,896]{1,0:T(8,128)S(1)}, f32[96,896]{1,0:T(8,128)}, u32[]{:S(2)}, u32[]{:S(2)}) collective-permute-start(f32[96,896]{1,0:T(8,128)S(1)} %get-tuple-element.43.refs_2_), channel_id=1, source_target_pairs={{2,0},{1,3},{6,4},{5,7},{10,8},{9,11},{14,12},{13,15},{18,16},{17,... | collective-permute-start | bytes 1032200 | tf_op jit(solution)/shard_map/ppermute | solution.py:454
  17.1 3.9 %collective-permute-start.4 = (f32[96,896]{1,0:T(8,128)}, f32[96,896]{1,0:T(8,128)}, u32[]{:S(2)}, u32[]{:S(2)}) collective-permute-start(f32[96,896]{1,0:T(8,128)} %get-tuple-element.44), channel_id=1, source_target_pairs={{4,0},{7,3},{0,4},{3,7},{12,8},{15,11},{8,12},{11,15},{20,16},{23,... | collective-permute-start | bytes 1032200 | tf_op jit(solution)/shard_map/ppermute | solution.py:454
  21.0 0.1 reshape.23.mixing_ref
  21.0 0.0 copy-start.2
  21.1 0.9 %copy-done.2 = f32[3,125,125]{2,1,0:T(8,128)S(1)} copy-done((f32[3,125,125]{2,1,0:T(8,128)S(1)}, f32[3,125,125]{2,1,0:T(8,128)}, u32[]{:S(2)}) %copy-start.2) | copy-done | bytes 187524
  22.0 1.2 %shard_map.88 = (bf16[640,640]{1,0:T(8,128)(2,1)S(1)}, bf16[640,640]{1,0:T(8,128)(2,1)S(1)}, f32[128,128]{1,0:T(8,128)S(1)}) custom-call(f32[3,125,125]{2,1,0:T(8,128)S(1)} %copy-done.2, f32[75]{0:T(128)S(1)} %reshape.23.mixing_ref), custom_call_target="tpu_custom_call" | custom-call | flops 1000000 | bytes 10000 | tf_op jit(solution)/shard_map/pallas_call | solution.py:515
  23.2 2.4 %shard_map.91 = (f32[256,256]{1,0:T(8,128)S(1)}, f32[640,256]{1,0:T(8,128)S(1)}, f32[256,256]{1,0:T(8,128)S(1)}, f32[640,256]{1,0:T(8,128)S(1)}) custom-call(s32[6]{0:T(128)S(1)} %stack.31.place_ref, f32[128,128]{1,0:T(8,128)S(1)} %get-tuple-element.38.sum_ref, f32[1280,256]{1,0:T(8,128)} %get-tuple-element.39.refs_0_, ...), custom_call_target="tpu_custom_call" | custom-call | flops 1000000 | bytes 10000 | tf_op jit(solution)/shard_map/pallas_call | solution.py:521
  25.6 0.0 copy-start.4
  25.6 1.7 %shard_map.89 = (f32[640,384]{1,0:T(8,128)S(1)}, f32[256,384]{1,0:T(8,128)S(1)}) custom-call(f32[5,125,384]{2,1,0:T(8,128)S(1)} %copy-done, f32[256,384]{1,0:T(8,128)S(1)} %get-tuple-element.34.f_ref, bf16[640,640]{1,0:T(8,128)(2,1)S(1)} %get-tuple-element.35.top_ref, bf16[640,640]{1,0:T(8,128)(2,1)S(1)} %get-tuple-element.36.rest_ref), custom_call_target="tpu_custom_call" | custom-call | flops 1000000 | bytes 10000 | tf_op jit(solution)/shard_map/pallas_call | solution.py:536
  27.3 0.9 %collective-permute-done.5.refs_5_ = f32[96,896]{1,0:T(8,128)S(1)} collective-permute-done((f32[96,896]{1,0:T(8,128)}, f32[96,896]{1,0:T(8,128)S(1)}, u32[]{:S(2)}, u32[]{:S(2)}) %collective-permute-start.5) | collective-permute-done | bytes 344096 | tf_op jit(solution)/shard_map/ppermute | solution.py:454
  28.2 0.0 collective-permute-done.3.refs_3_
  28.2 1.1 %collective-permute-done.4.refs_4_ = f32[96,896]{1,0:T(8,128)} collective-permute-done((f32[96,896]{1,0:T(8,128)}, f32[96,896]{1,0:T(8,128)}, u32[]{:S(2)}, u32[]{:S(2)}) %collective-permute-start.4) | collective-permute-done | bytes 344096 | tf_op jit(solution)/shard_map/ppermute | solution.py:454
  29.2 0.0 collective-permute-done.2.refs_1_
  29.3 5.4 %shard_map.92 = (f32[192,256]{1,0:T(8,128)S(1)}, f32[192,256]{1,0:T(8,128)S(1)}, f32[640,256]{1,0:T(8,128)S(1)}, f32[8,256]{1,0:T(8,128)S(1)}) custom-call(s32[6]{0:T(128)S(1)} %stack.31.place_ref, s32[1,256]{1,0:T(1,128)S(1)} %bitcast.15, bf16[640,640]{1,0:T(8,128)(2,1)S(1)} %get-tuple-element.35.top_ref, bf16[640,640]{1,0:T(8,128)(2,1)S(1)} %get-tuple-element.36.rest_ref, ...), custom_call_target="tpu_custom_call" | custom-call | flops 1000000 | bytes 10000 | tf_op jit(solution)/shard_map/pallas_call | solution.py:550
  34.7 2.4 %collective-permute-start.11 = (f32[192,256]{1,0:T(8,128)S(1)}, f32[192,256]{1,0:T(8,128)S(1)}, u32[]{:S(2)}, u32[]{:S(2)}) collective-permute-start(f32[192,256]{1,0:T(8,128)S(1)} %get-tuple-element.57), channel_id=1, source_target_pairs={{0,4},{3,7},{4,0},{7,3},{8,12},{11,15},{12,8},{15,11},{16,20},{19,... | collective-permute-start | bytes 589832 | tf_op jit(solution)/shard_map/ppermute | solution.py:454
  37.1 0.8 %collective-permute-done.6.refs_1_ = f32[1280,256]{1,0:T(8,128)} collective-permute-done((f32[1280,256]{1,0:T(8,128)S(1)}, f32[1280,256]{1,0:T(8,128)}, u32[]{:S(2)}, u32[]{:S(2)}) %collective-permute-start.6) | collective-permute-done | bytes 1310752 | tf_op jit(solution)/shard_map/ppermute | solution.py:499
  37.9 4.1 %shard_map.93 = (f32[104,640]{1,0:T(8,128)S(1)}, f32[104,640]{1,0:T(8,128)S(1)}, f32[104,640]{1,0:T(8,128)S(1)}, f32[104,640]{1,0:T(8,128)S(1)}) custom-call(s32[6]{0:T(128)S(1)} %stack.31.place_ref, f32[640,256]{1,0:T(8,128)S(1)} %get-tuple-element.47.now_ref, f32[8,256]{1,0:T(8,128)S(1)} %get-tuple-element.48.more_ref, ...), custom_call_target="tpu_custom_call" | custom-call | flops 1000000 | bytes 40000000 | tf_op jit(solution)/shard_map/pallas_call | solution.py:566
  42.0 1.3 %collective-permute-start.7 = (f32[104,640]{1,0:T(8,128)S(1)}, f32[104,640]{1,0:T(8,128)S(1)}, u32[]{:S(2)}, u32[]{:S(2)}) collective-permute-start(f32[104,640]{1,0:T(8,128)S(1)} %get-tuple-element.52), channel_id=1, source_target_pairs={{0,2},{3,1},{4,6},{7,5},{8,10},{11,9},{12,14},{15,13},{16,18},{19,... | collective-permute-start | bytes 798728 | tf_op jit(solution)/shard_map/ppermute | solution.py:454
  43.3 4.6 %collective-permute-start.8 = (f32[104,640]{1,0:T(8,128)S(1)}, f32[104,640]{1,0:T(8,128)S(1)}, u32[]{:S(2)}, u32[]{:S(2)}) collective-permute-start(f32[104,640]{1,0:T(8,128)S(1)} %get-tuple-element.53), channel_id=1, source_target_pairs={{0,4},{3,7},{4,0},{7,3},{8,12},{11,15},{12,8},{15,11},{16,20},{19,... | collective-permute-start | bytes 798728 | tf_op jit(solution)/shard_map/ppermute | solution.py:454
  47.9 1.3 %collective-permute-start.9 = (f32[104,640]{1,0:T(8,128)S(1)}, f32[104,640]{1,0:T(8,128)S(1)}, u32[]{:S(2)}, u32[]{:S(2)}) collective-permute-start(f32[104,640]{1,0:T(8,128)S(1)} %get-tuple-element.54), channel_id=1, source_target_pairs={{0,6},{3,5},{4,2},{7,1},{8,14},{11,13},{12,10},{15,9},{16,22},{19,... | collective-permute-start | bytes 798728 | tf_op jit(solution)/shard_map/ppermute | solution.py:454
  49.3 1.5 %collective-permute-start.12 = (f32[192,256]{1,0:T(8,128)S(1)}, f32[192,256]{1,0:T(8,128)S(1)}, u32[]{:S(2)}, u32[]{:S(2)}) collective-permute-start(f32[192,256]{1,0:T(8,128)S(1)} %pad_maximum_fusion.2), channel_id=1, source_target_pairs={{0,2},{3,1},{4,6},{7,5},{8,10},{11,9},{12,14},{15,13},{16,18},{19,... | collective-permute-start | bytes 589832 | tf_op jit(solution)/shard_map/ppermute | solution.py:454
  50.9 1.4 %collective-permute-done.8 = f32[104,640]{1,0:T(8,128)S(1)} collective-permute-done((f32[104,640]{1,0:T(8,128)S(1)}, f32[104,640]{1,0:T(8,128)S(1)}, u32[]{:S(2)}, u32[]{:S(2)}) %collective-permute-start.8) | collective-permute-done | bytes 266272 | tf_op jit(solution)/shard_map/ppermute | solution.py:454
  52.3 2.4 %collective-permute-done.9 = f32[104,640]{1,0:T(8,128)S(1)} collective-permute-done((f32[104,640]{1,0:T(8,128)S(1)}, f32[104,640]{1,0:T(8,128)S(1)}, u32[]{:S(2)}, u32[]{:S(2)}) %collective-permute-start.9) | collective-permute-done | bytes 266272 | tf_op jit(solution)/shard_map/ppermute | solution.py:454
  54.8 0.0 collective-permute-done.12
  54.9 0.4 collective-permute-start.13
  55.3 1.8 %collective-permute-start.10 = (f32[192,640]{1,0:T(8,128)S(1)}, f32[192,640]{1,0:T(8,128)S(1)}, u32[]{:S(2)}, u32[]{:S(2)}) collective-permute-start(f32[192,640]{1,0:T(8,128)S(1)} %pad_maximum_fusion.refs_0_), channel_id=1, source_target_pairs={{0,1},{1,0},{2,3},{3,2},{4,5},{5,4},{6,7},{7,6},{8,9},{9,8},{10,11... | collective-permute-start | bytes 1474568 | tf_op jit(solution)/shard_map/ppermute | solution.py:477
  57.1 1.6 %shard_map.94.base_ref = f32[640,384]{1,0:T(8,128)S(1)} custom-call(f32[640,384]{1,0:T(8,128)S(1)} %get-tuple-element.55.now_ref, bf16[640,640]{1,0:T(8,128)(2,1)S(1)} %get-tuple-element.35.top_ref, bf16[640,640]{1,0:T(8,128)(2,1)S(1)} %get-tuple-element.36.rest_ref), custom_call_target="tpu_custom_call" | custom-call | flops 1000000 | bytes 10000 | tf_op jit(solution)/shard_map/pallas_call | solution.py:587
  58.6 4.4 %collective-permute-done.13.refs_1_ = f32[208,256]{1,0:T(8,128)S(1)} collective-permute-done((f32[208,256]{1,0:T(8,128)S(1)}, f32[208,256]{1,0:T(8,128)S(1)}, u32[]{:S(2)}, u32[]{:S(2)}) %collective-permute-start.13) | collective-permute-done | bytes 213024 | tf_op jit(solution)/shard_map/ppermute | solution.py:477
  63.0 1.0 %shard_map.96 = (f32[160,128]{1,0:T(8,128)S(1)}, f32[160,128]{1,0:T(8,128)S(1)}) custom-call(s32[6]{0:T(128)S(1)} %stack.31.place_ref, f32[256,384]{1,0:T(8,128)S(1)} %get-tuple-element.45.base_ref, s32[2,128]{1,0:T(2,128)S(1)} %copy-done.3, f32[208,256]{1,0:T(8,128)S(1)} %pad_maximum_fusion.1.refs_0_, f32[208,256]{1,0:T(8,128)S(1)} %collective-permute-done.13.refs_1_), custom_call_target="tpu_custom_call" | custom-call | flops 1000000 | bytes 10000 | tf_op jit(solution)/shard_map/pallas_call | solution.py:589
  64.0 2.7 %collective-permute-start.14 = (f32[160,128]{1,0:T(8,128)S(1)}, f32[160,128]{1,0:T(8,128)S(1)}, u32[]{:S(2)}, u32[]{:S(2)}) collective-permute-start(f32[160,128]{1,0:T(8,128)S(1)} %get-tuple-element.60.one_ref), channel_id=1, source_target_pairs={{0,8},{16,24},{8,0},{24,16},{1,9},{17,25},{9,1},{25,17},{2,10},{18... | collective-permute-start | bytes 245768 | tf_op jit(solution)/shard_map/ppermute | solution.py:426
  66.7 2.6 %collective-permute-start.15 = (f32[160,128]{1,0:T(8,128)S(1)}, f32[160,128]{1,0:T(8,128)S(1)}, u32[]{:S(2)}, u32[]{:S(2)}) collective-permute-start(f32[160,128]{1,0:T(8,128)S(1)} %get-tuple-element.61.two_ref), channel_id=1, source_target_pairs={{8,16},{0,24},{16,8},{24,0},{9,17},{1,25},{17,9},{25,1},{10,18},{2... | collective-permute-start | bytes 245768 | tf_op jit(solution)/shard_map/ppermute | solution.py:426
  69.3 0.0 collective-permute-start.16
  69.3 4.6 %collective-permute-done.16 = f32[32,128]{1,0:T(8,128)S(1)} collective-permute-done((f32[32,128]{1,0:T(8,128)S(1)}, f32[32,128]{1,0:T(8,128)S(1)}, u32[]{:S(2)}, u32[]{:S(2)}) %collective-permute-start.16) | collective-permute-done | bytes 16416 | tf_op jit(solution)/shard_map/ppermute | solution.py:433
  74.0 0.6 fusion.1
  74.6 1.0 %shard_map.95.now_ref = f32[640,384]{1,0:T(8,128)S(1)} custom-call(s32[6]{0:T(128)S(1)} %stack.31.place_ref, f32[640,384]{1,0:T(8,128)S(1)} %shard_map.94.base_ref, f32[192,640]{1,0:T(8,128)S(1)} %pad_maximum_fusion.refs_0_, f32[192,640]{1,0:T(8,128)S(1)} %collective-permute-done.10.refs_1_), custom_call_target="tpu_custom_call" | custom-call | flops 1000000 | bytes 80000000 | tf_op jit(solution)/shard_map/pallas_call | solution.py:598
  75.6 1.8 %shard_map.97 = f32[5,125,384]{2,1,0:T(8,128)} custom-call(s32[6]{0:T(128)S(1)} %stack.31.place_ref, f32[640,384]{1,0:T(8,128)S(1)} %shard_map.95.now_ref, s32[2,128]{1,0:T(2,128)S(1)} %copy-done.3, f32[160,128]{1,0:T(8,128)S(1)} %get-tuple-element.60.one_ref, f32[160,128]{1,0:T(8,128)S(1)} %get-tuple-element.61.two_ref, ...), custom_call_target="tpu_custom_call" | custom-call | flops 1000000 | bytes 10000 | tf_op jit(solution)/shard_map/pallas_call | solution.py:605
  (30 shorter events, 0.3 us)
Async XLA Ops:
  0.6 1.7 %copy-start.1 = (f32[2,2,5,125,256]{4,1,3,2,0:T(2,128)S(1)}, f32[2,2,5,125,256]{4,1,3,2,0:T(2,128)}, u32[]{:S(2)}) copy-start(f32[2,2,5,125,256]{4,1,3,2,0:T(2,128)} %param.7) | copy-start | bytes 7680004
  2.4 4.1 %copy-start = (f32[5,125,384]{2,1,0:T(8,128)S(1)}, f32[5,125,384]{2,1,0:T(8,128)}, u32[]{:S(2)}) copy-start(f32[5,125,384]{2,1,0:T(8,128)} %a_in_ref.1) | copy-start | bytes 2880004
  2.4 4.1 %copy-start.3 = (s32[2,128]{1,0:T(2,128)S(1)}, s32[2,128]{1,0:T(2,128)}, u32[]{:S(2)}) copy-start(s32[2,128]{1,0:T(2,128)} %lists_ref.7) | copy-start | bytes 3076
  2.4 8.7 %copy-start.6 = (s32[384]{0:T(512)S(1)}, s32[384]{0:T(512)}, u32[]{:S(2)}) copy-start(s32[384]{0:T(512)} %param.13) | copy-start | bytes 4612
  3.6 17.3 %copy-start.5 = (f32[3,5,5]{2,0,1:T(4,128)S(1)}, f32[3,5,5]{2,0,1:T(4,128)}, u32[]{:S(2)}) copy-start(f32[3,5,5]{2,0,1:T(4,128)} %param.11) | copy-start | bytes 904
  3.6 25.6 %collective-permute-start.2 = (f32[1280,256]{1,0:T(8,128)}, f32[1280,256]{1,0:T(8,128)}, u32[]{:S(2)}, u32[]{:S(2)}) collective-permute-start(f32[1280,256]{1,0:T(8,128)} %get-tuple-element.39.refs_0_), channel_id=1, source_target_pairs={{1,0},{2,3},{5,4},{6,7},{9,8},{10,11},{13,12},{14,15},{17,16},{18,... | collective-permute-start | bytes 3932168 | tf_op jit(solution)/shard_map/ppermute | solution.py:499
  5.1 32.9 %collective-permute-start.6 = (f32[1280,256]{1,0:T(8,128)S(1)}, f32[1280,256]{1,0:T(8,128)}, u32[]{:S(2)}, u32[]{:S(2)}) collective-permute-start(f32[1280,256]{1,0:T(8,128)S(1)} %get-tuple-element.40.refs_1_.refs_0_), channel_id=1, source_target_pairs={{1,0},{2,3},{5,4},{6,7},{9,8},{10,11},{13,12},{14,15},{17,16},{18,... | collective-permute-start | bytes 3932168 | tf_op jit(solution)/shard_map/ppermute | solution.py:499
  7.3 5.3 %collective-permute-start = (f32[128,128]{1,0:T(8,128)S(1)}, f32[128,128]{1,0:T(8,128)S(1)}, u32[]{:S(2)}, u32[]{:S(2)}) collective-permute-start(f32[128,128]{1,0:T(8,128)S(1)} %get-tuple-element.32.one_ref), channel_id=1, source_target_pairs={{0,8},{16,24},{8,0},{24,16},{1,9},{17,25},{9,1},{25,17},{2,10},{18... | collective-permute-start | bytes 196616 | tf_op jit(solution)/shard_map/ppermute | solution.py:426
  10.4 2.2 %collective-permute-start.1 = (f32[128,128]{1,0:T(8,128)S(1)}, f32[128,128]{1,0:T(8,128)S(1)}, u32[]{:S(2)}, u32[]{:S(2)}) collective-permute-start(f32[128,128]{1,0:T(8,128)S(1)} %get-tuple-element.33.two_ref), channel_id=1, source_target_pairs={{8,16},{16,8},{9,17},{17,9},{10,18},{18,10},{11,19},{19,11},{12,20... | collective-permute-start | bytes 196616 | tf_op jit(solution)/shard_map/ppermute | solution.py:426
  14.5 13.7 %collective-permute-start.5 = (f32[96,896]{1,0:T(8,128)}, f32[96,896]{1,0:T(8,128)S(1)}, u32[]{:S(2)}, u32[]{:S(2)}) collective-permute-start(f32[96,896]{1,0:T(8,128)} %get-tuple-element.44), channel_id=1, source_target_pairs={{6,0},{5,3},{2,4},{1,7},{14,8},{13,11},{10,12},{9,15},{22,16},{21,... | collective-permute-start | bytes 1032200 | tf_op jit(solution)/shard_map/ppermute | solution.py:454
  15.8 12.4 %collective-permute-start.3 = (f32[96,896]{1,0:T(8,128)S(1)}, f32[96,896]{1,0:T(8,128)}, u32[]{:S(2)}, u32[]{:S(2)}) collective-permute-start(f32[96,896]{1,0:T(8,128)S(1)} %get-tuple-element.43.refs_2_), channel_id=1, source_target_pairs={{2,0},{1,3},{6,4},{5,7},{10,8},{9,11},{14,12},{13,15},{18,16},{17,... | collective-permute-start | bytes 1032200 | tf_op jit(solution)/shard_map/ppermute | solution.py:454
  17.1 12.2 %collective-permute-start.4 = (f32[96,896]{1,0:T(8,128)}, f32[96,896]{1,0:T(8,128)}, u32[]{:S(2)}, u32[]{:S(2)}) collective-permute-start(f32[96,896]{1,0:T(8,128)} %get-tuple-element.44), channel_id=1, source_target_pairs={{4,0},{7,3},{0,4},{3,7},{12,8},{15,11},{8,12},{11,15},{20,16},{23,... | collective-permute-start | bytes 1032200 | tf_op jit(solution)/shard_map/ppermute | solution.py:454
  21.0 0.9 %copy-start.2 = (f32[3,125,125]{2,1,0:T(8,128)S(1)}, f32[3,125,125]{2,1,0:T(8,128)}, u32[]{:S(2)}) copy-start(f32[3,125,125]{2,1,0:T(8,128)} %deriv_ref.1) | copy-start | bytes 562504
  25.6 3.6 %copy-start.4 = (s32[256,1]{0,1:T(1,128)S(1)}, s32[256,1]{0,1:T(1,128)}, u32[]{:S(2)}) copy-start(s32[256,1]{0,1:T(1,128)} %param.8) | copy-start | bytes 3076
  34.7 14.6 %collective-permute-start.11 = (f32[192,256]{1,0:T(8,128)S(1)}, f32[192,256]{1,0:T(8,128)S(1)}, u32[]{:S(2)}, u32[]{:S(2)}) collective-permute-start(f32[192,256]{1,0:T(8,128)S(1)} %get-tuple-element.57), channel_id=1, source_target_pairs={{0,4},{3,7},{4,0},{7,3},{8,12},{11,15},{12,8},{15,11},{16,20},{19,... | collective-permute-start | bytes 589832 | tf_op jit(solution)/shard_map/ppermute | solution.py:454
  42.0 8.8 %collective-permute-start.7 = (f32[104,640]{1,0:T(8,128)S(1)}, f32[104,640]{1,0:T(8,128)S(1)}, u32[]{:S(2)}, u32[]{:S(2)}) collective-permute-start(f32[104,640]{1,0:T(8,128)S(1)} %get-tuple-element.52), channel_id=1, source_target_pairs={{0,2},{3,1},{4,6},{7,5},{8,10},{11,9},{12,14},{15,13},{16,18},{19,... | collective-permute-start | bytes 798728 | tf_op jit(solution)/shard_map/ppermute | solution.py:454
  43.3 9.0 %collective-permute-start.8 = (f32[104,640]{1,0:T(8,128)S(1)}, f32[104,640]{1,0:T(8,128)S(1)}, u32[]{:S(2)}, u32[]{:S(2)}) collective-permute-start(f32[104,640]{1,0:T(8,128)S(1)} %get-tuple-element.53), channel_id=1, source_target_pairs={{0,4},{3,7},{4,0},{7,3},{8,12},{11,15},{12,8},{15,11},{16,20},{19,... | collective-permute-start | bytes 798728 | tf_op jit(solution)/shard_map/ppermute | solution.py:454
  47.9 6.8 %collective-permute-start.9 = (f32[104,640]{1,0:T(8,128)S(1)}, f32[104,640]{1,0:T(8,128)S(1)}, u32[]{:S(2)}, u32[]{:S(2)}) collective-permute-start(f32[104,640]{1,0:T(8,128)S(1)} %get-tuple-element.54), channel_id=1, source_target_pairs={{0,6},{3,5},{4,2},{7,1},{8,14},{11,13},{12,10},{15,9},{16,22},{19,... | collective-permute-start | bytes 798728 | tf_op jit(solution)/shard_map/ppermute | solution.py:454
  49.3 5.5 %collective-permute-start.12 = (f32[192,256]{1,0:T(8,128)S(1)}, f32[192,256]{1,0:T(8,128)S(1)}, u32[]{:S(2)}, u32[]{:S(2)}) collective-permute-start(f32[192,256]{1,0:T(8,128)S(1)} %pad_maximum_fusion.2), channel_id=1, source_target_pairs={{0,2},{3,1},{4,6},{7,5},{8,10},{11,9},{12,14},{15,13},{16,18},{19,... | collective-permute-start | bytes 589832 | tf_op jit(solution)/shard_map/ppermute | solution.py:454
  54.9 8.1 %collective-permute-start.13 = (f32[208,256]{1,0:T(8,128)S(1)}, f32[208,256]{1,0:T(8,128)S(1)}, u32[]{:S(2)}, u32[]{:S(2)}) collective-permute-start(f32[208,256]{1,0:T(8,128)S(1)} %pad_maximum_fusion.1.refs_0_), channel_id=1, source_target_pairs={{0,1},{1,0},{2,3},{3,2},{4,5},{5,4},{6,7},{7,6},{8,9},{9,8},{10,11... | collective-permute-start | bytes 638984 | tf_op jit(solution)/shard_map/ppermute | solution.py:477
  55.3 19.3 %collective-permute-start.10 = (f32[192,640]{1,0:T(8,128)S(1)}, f32[192,640]{1,0:T(8,128)S(1)}, u32[]{:S(2)}, u32[]{:S(2)}) collective-permute-start(f32[192,640]{1,0:T(8,128)S(1)} %pad_maximum_fusion.refs_0_), channel_id=1, source_target_pairs={{0,1},{1,0},{2,3},{3,2},{4,5},{5,4},{6,7},{7,6},{8,9},{9,8},{10,11... | collective-permute-start | bytes 1474568 | tf_op jit(solution)/shard_map/ppermute | solution.py:477
  64.0 10.0 %collective-permute-start.14 = (f32[160,128]{1,0:T(8,128)S(1)}, f32[160,128]{1,0:T(8,128)S(1)}, u32[]{:S(2)}, u32[]{:S(2)}) collective-permute-start(f32[160,128]{1,0:T(8,128)S(1)} %get-tuple-element.60.one_ref), channel_id=1, source_target_pairs={{0,8},{16,24},{8,0},{24,16},{1,9},{17,25},{9,1},{25,17},{2,10},{18... | collective-permute-start | bytes 245768 | tf_op jit(solution)/shard_map/ppermute | solution.py:426
  66.7 7.3 %collective-permute-start.15 = (f32[160,128]{1,0:T(8,128)S(1)}, f32[160,128]{1,0:T(8,128)S(1)}, u32[]{:S(2)}, u32[]{:S(2)}) collective-permute-start(f32[160,128]{1,0:T(8,128)S(1)} %get-tuple-element.61.two_ref), channel_id=1, source_target_pairs={{8,16},{0,24},{16,8},{24,0},{9,17},{1,25},{17,9},{25,1},{10,18},{2... | collective-permute-start | bytes 245768 | tf_op jit(solution)/shard_map/ppermute | solution.py:426
  69.3 4.6 %collective-permute-start.16 = (f32[32,128]{1,0:T(8,128)S(1)}, f32[32,128]{1,0:T(8,128)S(1)}, u32[]{:S(2)}, u32[]{:S(2)}) collective-permute-start(f32[32,128]{1,0:T(8,128)S(1)} %slice.49), channel_id=1, source_target_pairs={{0,16},{8,24},{16,0},{24,8},{1,17},{9,25},{17,1},{25,9},{2,18},{10... | collective-permute-start | bytes 49160 | tf_op jit(solution)/shard_map/ppermute | solution.py:433
